TPU v7x, 256 devices: a whole 4x4x8 slice. The times are simulated.
256 devices in a mesh: replica: 8 (over z_lo, core), fsdp: 32 (over z_hi, x, y).
Axes of the slice: x: 4, y: 4, z: 8 (z_hi: 2, z_lo: 4; z = z_hi * 4 + z_lo), core: 2. Of those that a mesh axis runs over, the one named last changes fastest.
Arguments:
- anchor: float32 [8192, 1024], P('fsdp'), may hold values from -6 to 6
- first_moment: float32 [8, 8192, 1024], P('replica', 'fsdp'), may hold values from -4 to 4
- second_moment: float32 [8, 8192, 1024], P('replica', 'fsdp'), may hold values from 0.3 to 3
- outer_momentum: float32 [8192, 1024], P('fsdp'), may hold values from -6 to 6
- activations: bfloat16 [8, 2, 4096, 8192], P('replica', None, 'fsdp'), may hold values from -6 to 6
- cotangents: bfloat16 [8, 2, 4096, 1024], P('replica', None, 'fsdp'), may hold values from -0.21875 to 0.21875
- token_ids: int32 [8, 2, 4096], P('replica', None, 'fsdp'), may hold values from 0 to 128255, as said below
- exponents: int32 [8, 8192, 8], P('replica', 'fsdp'), may hold values from -13 to -9
Outputs:
- new_weights: float32 [8192, 1024], P('fsdp')
- new_momentum: float32 [8192, 1024], P('fsdp')
- new_first: float32 [8, 8192, 1024], P('replica', 'fsdp')
- new_second: float32 [8, 8192, 1024], P('replica', 'fsdp')
Inputs may be any that keep to these rules, and one draw needn't show every extreme that they name: `token_ids`: 0 is the padding id; in each aligned block of 128 tokens of one replica and step the padding is a tail, and the first quarter of the block or more is not padding.
All inputs are finite; a program needn't handle non-finite values.
Results may differ from a plain program's by a relative error of at most 0.0055.
Values may be sent and summed in bfloat16 or wider, within the bound.
No kernel may reach another device: no remote copies, remote signals or barrier semaphores. Data moves between devices by JAX's collectives and lax.ppermute only.
A program may use at most 192 MiB of HBM per device.

v0:
```python
import jax
import jax.numpy as jnp
from jax import lax
from jax.sharding import PartitionSpec as P

BETA_ONE = 0.9
BETA_TWO = 0.95
EPSILON = 1e-08
INNER_RATE = 0.1
DECAY = 0.1
OUTER_RATE = 0.7
MOMENTUM = 0.9
CODE_LIMIT = 448.0


def adam_update(weights, first, second, gradient):
    first = BETA_ONE * first + (1.0 - BETA_ONE) * gradient
    second = BETA_TWO * second + (1.0 - BETA_TWO) * gradient * gradient
    weights = weights - INNER_RATE * (first / (jnp.sqrt(second) + EPSILON) + DECAY * weights)
    return (weights, first, second)


def block_factor(exponents):
    return jnp.left_shift(jnp.ones_like(exponents), -exponents).astype(jnp.float32)


def decode_blocks(delta, exponents):
    blocks = delta.reshape(delta.shape[0], -1, 128)
    factor = block_factor(exponents)[..., None]
    coded = jnp.clip(blocks * factor, -CODE_LIMIT, CODE_LIMIT).astype(jnp.bfloat16)
    coded = lax.optimization_barrier(coded)
    return (coded.astype(jnp.float32) / factor).reshape(delta.shape)


def contract_tokens(left, right):
    return lax.dot_general(
        left, right, (((0,), (0,)), ((), ())), preferred_element_type=jnp.float32
    )


def on_device(
    anchor,
    first_moment,
    second_moment,
    outer_momentum,
    activations,
    cotangents,
    token_ids,
    exponents,
):
    shard_rows = anchor.shape[0]
    width = anchor.shape[1]
    steps = cotangents.shape[1]
    masked = jnp.where((token_ids[0] != 0)[..., None], cotangents[0], jnp.zeros_like(cotangents[0]))
    gradients = []
    columns = lax.all_to_all(activations[0], "fsdp", split_axis=2, concat_axis=1, tiled=True)
    empty = jnp.zeros((shard_rows, width), jnp.float32)
    for step in range(steps):

        def add_tokens(total, piece, start, owned=columns[step]):
            return contract_tokens(owned, piece)

        gradients.append(
            add_tokens(
                empty, lax.all_gather(masked[step], "fsdp", axis=0, tiled=True), jnp.int32(0)
            )
        )
    weights = anchor
    first = first_moment[0]
    second = second_moment[0]
    for step in range(steps):
        weights, first, second = adam_update(weights, first, second, gradients[step])
    decoded = decode_blocks(anchor - weights, exponents[0])
    replicas = lax.axis_size("replica")
    average = lax.psum(decoded.astype(jnp.bfloat16), "replica").astype(jnp.float32) / replicas
    new_momentum = MOMENTUM * outer_momentum + average
    new_weights = anchor - OUTER_RATE * (average + MOMENTUM * new_momentum)
    return (new_weights, new_momentum, first[None], second[None])


def solution(mesh):
    in_specs = (
        P("fsdp", None),
        P("replica", "fsdp", None),
        P("replica", "fsdp", None),
        P("fsdp", None),
        P("replica", None, "fsdp", None),
        P("replica", None, "fsdp", None),
        P("replica", None, "fsdp"),
        P("replica", "fsdp", None),
    )
    out_specs = (
        P("fsdp", None),
        P("fsdp", None),
        P("replica", "fsdp", None),
        P("replica", "fsdp", None),
    )
    return jax.shard_map(
        on_device, mesh=mesh, in_specs=in_specs, out_specs=out_specs, check_vma=False
    )
```

profile of v0, /device:TPU:1, one launch (start us, length us, event | category | flops | bytes accessed | tf_op | source)
XLA Modules:
  0.0 473.1 jit_solution(15377144489898343093)
XLA Ops:
  7.2 0.0 all-gather.5.cloned.1.call-start
  7.2 0.7 compare_bitcast_fusion
  7.9 1.1 bitcast_select_fusion
  9.0 0.8 fusion.15
  9.9 0.0 all-gather.5.cloned.1.call-update
  9.9 0.0 all-gather.7.cloned.1.call-start
  9.9 0.7 all-gather.7.cloned.1.call-update
  10.6 11.2 %copy.49 = bf16[1,2,128,8192]{2,1,3,0:T(2,128)(2,1)} copy(bf16[1,2,128,8192]{3,2,1,0:T(8,128)(2,1)} %param.12) | data formatting | bytes 8388608 | tf_op args[4]
  21.8 0.0 copy-start
  21.8 0.0 copy-start.1
  21.8 14.8 %all-to-all-start = ((bf16[2,128,8192]{1,0,2:T(2,128)(2,1)}), bf16[2,128,8192]{1,0,2:T(2,128)(2,1)}, u32[]{:S(2)}, u32[]{:S(2)}) async-start(bf16[2,128,8192]{1,0,2:T(2,128)(2,1)} %bitcast.50), calls=%async_computation | async-start | bytes 8388608 | tf_op jit(solution)/shard_map/all_to_all | solution.py:56
  36.6 0.0 copy-start.3
  36.6 0.0 all-reduce.2.cloned.1.call-start
  36.7 0.0 copy-done
  36.7 0.3 copy.58
  37.0 0.0 copy-done.1
  37.0 1.3 copy.48
  38.3 2.5 copy.52
  40.9 0.0 copy-done.3
  40.9 105.9 %all-to-all-done = bf16[2,128,8192]{1,0,2:T(2,128)(2,1)} async-done(((bf16[2,128,8192]{1,0,2:T(2,128)(2,1)}), bf16[2,128,8192]{1,0,2:T(2,128)(2,1)}, u32[]{:S(2)}, u32[]{:S(2)}) %all-to-all-start) | async-done | bytes 4194336 | tf_op jit(solution)/shard_map/all_to_all | solution.py:56
  146.8 2.7 copy.50
  149.5 2.2 fusion.14
  151.7 3.5 copy.51
  155.2 4.1 copy.55
  159.3 69.1 %all-gather.5.cloned.1.call-done = bf16[1,4096,1024]{2,1,0:T(8,128)(2,1)} async-done(((bf16[1,128,1024]{2,1,0:T(8,128)(2,1)}), bf16[1,4096,1024]{2,1,0:T(8,128)(2,1)}) %all-gather.5.cloned.1.call-update) | async-done | bytes 8388624 | tf_op jit(solution)/shard_map/all_gather | solution.py:65
  228.4 6.7 %fusion.4 = f32[256,1024]{0,1:T(8,128)} fusion(bf16[4096,256]{1,0:T(8,128)(2,1)S(1)} %bitcast.52, bf16[1,4096,1024]{2,1,0:T(8,128)(2,1)} %all-gather.5.cloned.1.call-done), kind=kOutput, calls=%fused_computation.6 | convolution fusion | flops 2147483648 | bytes 11534336 | tf_op jit(solution)/shard_map/dot_general | solution.py:36
  235.1 146.5 %all-gather.7.cloned.1.call-done = bf16[1,4096,1024]{2,1,0:T(8,128)(2,1)} async-done(((bf16[1,128,1024]{2,1,0:T(8,128)(2,1)}), bf16[1,4096,1024]{2,1,0:T(8,128)(2,1)}) %all-gather.7.cloned.1.call-update) | async-done | bytes 8388624 | tf_op jit(solution)/shard_map/all_gather | solution.py:65
  381.7 0.0 copy-start.2
  381.7 9.8 %fusion.12 = (f32[1,256,1024]{1,2,0:T(8,128)}, f32[256,1024]{0,1:T(8,128)S(1)}, f32[1,256,1024]{1,2,0:T(8,128)}) fusion(f32[256,1024]{0,1:T(8,128)} %fusion.4, f32[1,256,1024]{1,2,0:T(8,128)} %copy.52, f32[256,1024]{0,1:T(8,128)S(1)} %copy.58, f32[1,256,1024]{1,2,0:T(8,128)} %copy.48, bf16[4096,256]{1,0:T(8,128)(2,1)} %bitcast.53, ...), kind=kOutput, calls=%fused_computation.19 | convolution fusion | flops 2154561536 | bytes 17825792 | tf_op jit(solution)/shard_map/dot_general | solution.py:36
  391.4 0.1 clamp_convert_fusion
  391.6 0.9 divide_convert_fusion
  392.4 0.0 all-reduce.2.cloned.1.call-update
  392.5 0.0 copy-done.2
  392.5 0.3 copy.57
  392.8 2.5 copy.61
  395.3 2.5 copy.62
  397.9 62.6 %all-reduce.2.cloned.1.call-done = bf16[256,1024]{0,1:T(8,128)(2,1)} async-done(((bf16[256,1024]{0,1:T(8,128)(2,1)}), bf16[256,1024]{0,1:T(8,128)(2,1)}) %all-reduce.2.cloned.1.call-update) | async-done | bytes 524304 | tf_op jit(solution)/shard_map/psum | solution.py:75
  460.4 2.3 multiply_add_fusion
  462.7 2.5 copy.59
  465.3 1.3 copy.60
  (1 shorter events, 0.0 us)
Async XLA Ops:
  7.2 221.2 %all-gather.5.cloned.1.call-start = ((), (), s32[]{:S(2)}) async-start(), calls=%async_computation.2 | async-start | bytes 8650752 | tf_op jit(solution)/shard_map/all_gather | solution.py:65
  9.9 371.8 %all-gather.7.cloned.1.call-start = ((), (), s32[]{:S(2)}) async-start(), calls=%async_computation.3 | async-start | bytes 8650752 | tf_op jit(solution)/shard_map/all_gather | solution.py:65
  21.8 14.8 %copy-start = (f32[256,1024]{1,0:T(8,128)S(1)}, f32[256,1024]{1,0:T(8,128)}, u32[]{:S(2)}) copy-start(f32[256,1024]{1,0:T(8,128)} %param.8) | copy-start | bytes 3145732
  21.8 15.2 %copy-start.1 = (f32[1,256,1024]{2,1,0:T(8,128)S(1)}, f32[1,256,1024]{2,1,0:T(8,128)}, u32[]{:S(2)}) copy-start(f32[1,256,1024]{2,1,0:T(8,128)} %param.9) | copy-start | bytes 3145732
  21.8 124.9 %all-to-all-start = ((bf16[2,128,8192]{1,0,2:T(2,128)(2,1)}), bf16[2,128,8192]{1,0,2:T(2,128)(2,1)}, u32[]{:S(2)}, u32[]{:S(2)}) async-start(bf16[2,128,8192]{1,0,2:T(2,128)(2,1)} %bitcast.50), calls=%async_computation | async-start | bytes 8388608 | tf_op jit(solution)/shard_map/all_to_all | solution.py:56
  36.6 4.3 copy-start.3
  36.6 423.8 %all-reduce.2.cloned.1.call-start = ((), (), s32[]{:S(2)}) async-start(), calls=%async_computation.1 | async-start | bytes 1048576 | tf_op jit(solution)/shard_map/psum | solution.py:75
  381.7 10.8 %copy-start.2 = (f32[256,1024]{1,0:T(8,128)S(1)}, f32[256,1024]{1,0:T(8,128)}, u32[]{:S(2)}) copy-start(f32[256,1024]{1,0:T(8,128)} %param.11) | copy-start | bytes 3145732
Sparse Core Ops, SparseCore 0:
  12.1 216.2 all-gather.4
  232.5 149.1 all-gather.6
  392.6 67.8 all-reduce.1
where the time goes:
time: 476 us; the launch traced here: 473 us
  waiting for transfers between devices  385 us (81%)
  local copies, waits for them, and re-layouts  38 us (8%)
  matrix products  16.5 us (3%)
  starting transfers between devices  14.9 us (3%)
  between operations  13.8 us (3%)
  other arithmetic  5.12 us (1%)
    all_gather x2, waiting for transfers between devices, on_device(): lax.all_gather(masked[step], 'fsdp', axis=0, tiled=True)  216 us
    all_to_all x1, waiting for transfers between devices, on_device(): lax.all_to_all(activations[0], 'fsdp', split_axis=2, concat_axis=1, tiled...  106 us
    psum x1, waiting for transfers between devices, on_device(): lax.psum(decoded.astype(jnp.bfloat16), 'replica').astype(jnp.float32)  62.6 us
    unnamed x17, local copies, waits for them, and re-layouts  24.6 us
    dot_general x2, matrix products, contract_tokens(): lax.dot_general(left, right, (((0,), (0,)), ((), ())), preferred_element_...  16.5 us
    all_to_all x1, starting transfers between devices, on_device(): lax.all_to_all(activations[0], 'fsdp', split_axis=2, concat_axis=1, tiled...  14.8 us
    slice x3, local copies, waits for them, and re-layouts, add_tokens(): columns[step]  9.81 us
  transfers between devices with their start and end apart: 4, of which 4 were waited for; matrix products, arithmetic and copies ran while one was open for 8% of the time, Pallas kernels for 0%

commit v1 on v0

v1 whole, which is shorter than its diff:
```python
import functools

import jax
import jax.numpy as jnp
from jax import lax
from jax.experimental import pallas as pl
from jax.experimental.pallas import tpu as pltpu
from jax.sharding import PartitionSpec as P

BETA_ONE = 0.9
BETA_TWO = 0.95
EPSILON = 1e-08
INNER_RATE = 0.1
DECAY = 0.1
OUTER_RATE = 0.7
MOMENTUM = 0.9
CODE_LIMIT = 448.0

NZ, NX, NY = 2, 4, 4
PLANE = NX * NY
LINE, CORES = 4, 2
VMEM = 56 * 1024 * 1024


def fsdp_shift(dz, dx, dy):
    def at(z, x, y):
        return ((z % NZ) * NX + x % NX) * NY + y % NY

    return [
        (at(z, x, y), at(z + dz, x + dx, y + dy))
        for z in range(NZ)
        for x in range(NX)
        for y in range(NY)
    ]


def replica_shift(dz, dc):
    return [
        (z * CORES + c, ((z + dz) % LINE) * CORES + (c + dc) % CORES)
        for z in range(LINE)
        for c in range(CORES)
    ]


PLANES = [list(range(z * PLANE, (z + 1) * PLANE)) for z in range(NZ)]
X_RING = (fsdp_shift(0, 1, 0), fsdp_shift(0, -1, 0))
Y_RING = (fsdp_shift(0, 0, 1), fsdp_shift(0, 0, -1))
Z_SWAP = fsdp_shift(1, 0, 0)


def split_kernel(spot, features, out):
    for q in range(out.shape[0]):
        out[q] = features[0, 0, :, q * 256 : (q + 1) * 256]


def split_rows(spot, features, step):
    tokens, rows = features.shape[2:]
    shard = rows // (NZ * PLANE)
    return pl.pallas_call(
        split_kernel,
        grid_spec=pltpu.PrefetchScalarGridSpec(
            num_scalar_prefetch=1,
            grid=(4,),
            in_specs=[
                pl.BlockSpec((1, 1, tokens, 4 * shard), lambda i, spot: (0, step, 0, spot[0] * 4 + i))
            ],
            out_specs=pl.BlockSpec((4, tokens, shard), lambda i, spot: (i, 0, 0)),
        ),
        out_shape=jax.ShapeDtypeStruct((PLANE, tokens, shard), features.dtype),
    )(spot, features)


def ring_gather(block, ring):
    ahead, back = ring
    left = lax.ppermute(block, "fsdp", ahead)
    right = lax.ppermute(block, "fsdp", back)
    far_zero = lax.ppermute(left[0], "fsdp", ahead)
    far_one = lax.ppermute(right[1], "fsdp", back)
    return block, left, right, (far_zero, far_one)


def stack_pieces(pieces, at):
    own, left, right, (far_zero, far_one) = pieces
    far = jnp.stack([far_zero, far_one])
    whole = jnp.stack([own, left, far, right], axis=1)
    order = lax.rem(at - jnp.arange(4, dtype=jnp.int32) + 4, 4)
    return jnp.take(whole, order, axis=1)


def dot_kernel(step, spot, a, *refs):
    first_set, second_set = refs[0:4], refs[4:8]
    out, tokens, sems = refs[8:]
    x, y = spot[0], spot[1]
    copies = []
    for turn, piece in enumerate(first_set):
        source = piece.at[step] if len(piece.shape) == 4 else piece
        copies.append(
            pltpu.make_async_copy(source, tokens.at[:, lax.rem(y - turn + 4, 4), 0], sems.at[turn])
        )
    for turn, piece in enumerate(second_set):
        source = piece.at[step] if len(piece.shape) == 4 else piece
        copies.append(
            pltpu.make_async_copy(source, tokens.at[lax.rem(x - turn + 4, 4), :, 1], sems.at[4 + turn])
        )
    for copy in copies:
        copy.start()
    left = a[...].reshape(-1, a.shape[-1])
    for copy in copies:
        copy.wait()
    depth = left.shape[0]

    width = 256
    for n in range(0, out.shape[1], width):
        right = tokens[:, :, :, :, n : n + width].reshape(depth, width)
        out[:, n : n + width] = lax.dot_general(
            left, right, (((0,), (0,)), ((), ())), preferred_element_type=jnp.float32
        ).astype(out.dtype)


def contract(spot, a, sets, step, dtype):
    width = sets[0][0].shape[-1]
    pieces = []
    for own, left, right, far in sets:
        pieces += [own, left, far[step], right]
    return pl.pallas_call(
        functools.partial(dot_kernel, step),
        in_specs=[pl.BlockSpec(memory_space=pltpu.SMEM), pl.BlockSpec(memory_space=pltpu.VMEM)]
        + [pl.BlockSpec(memory_space=pl.ANY)] * 8,
        out_specs=pl.BlockSpec(memory_space=pltpu.VMEM),
        out_shape=jax.ShapeDtypeStruct((a.shape[2], width), dtype),
        scratch_shapes=[
            pltpu.VMEM((NX, NY, 2, a.shape[1] // 2, width), a.dtype),
            pltpu.SemaphoreType.DMA((8,)),
        ],
        compiler_params=pltpu.CompilerParams(vmem_limit_bytes=VMEM),
    )(spot, a, *pieces)


def adam_update(weights, first, second, gradient):
    first = BETA_ONE * first + (1.0 - BETA_ONE) * gradient
    second = BETA_TWO * second + (1.0 - BETA_TWO) * gradient * gradient
    weights = weights - INNER_RATE * (first / (jnp.sqrt(second) + EPSILON) + DECAY * weights)
    return weights, first, second


def adam_kernel(
    spot, anchor, first, second, own_a, got_a, own_b, got_b, scale, decoded, new_first, new_second
):
    start = anchor[...]
    weights, one, two = start, first[0], second[0]
    for own, got in ((own_a, got_a), (own_b, got_b)):
        gradient = own[...] + got[...].astype(jnp.float32)
        weights, one, two = adam_update(weights, one, two, gradient)
    new_first[0] = one
    new_second[0] = two
    delta = start - weights
    factors = jnp.left_shift(jnp.ones_like(scale[0]), -scale[0]).astype(jnp.float32)
    for block in range(delta.shape[1] // 128):
        columns = slice(block * 128, (block + 1) * 128)
        factor = factors[:, block : block + 1]
        coded = jnp.clip(delta[:, columns] * factor, -CODE_LIMIT, CODE_LIMIT).astype(jnp.bfloat16)
        decoded[:, columns] = (coded.astype(jnp.float32) / factor).astype(jnp.bfloat16)


def adam(spot, anchor, first, second, own_a, got_a, own_b, got_b, exponents):
    rows, width = anchor.shape
    tile = 32
    steps = rows // tile
    flat = pl.BlockSpec((tile, width), lambda i, spot: (i, 0))
    deep = pl.BlockSpec((1, tile, width), lambda i, spot: (0, i, 0))
    return pl.pallas_call(
        adam_kernel,
        grid_spec=pltpu.PrefetchScalarGridSpec(
            num_scalar_prefetch=1,
            grid=(steps,),
            in_specs=[flat, deep, deep, flat, flat, flat, flat]
            + [pl.BlockSpec((1, tile, exponents.shape[2]), lambda i, spot: (0, i, 0))],
            out_specs=[flat, deep, deep],
        ),
        out_shape=[
            jax.ShapeDtypeStruct((rows, width), jnp.bfloat16),
            jax.ShapeDtypeStruct(first.shape, jnp.float32),
            jax.ShapeDtypeStruct(second.shape, jnp.float32),
        ],
    )(spot, anchor, first, second, own_a, got_a, own_b, got_b, exponents)


def replica_sum(decoded):
    rows, width = decoded.shape
    place = lax.axis_index("replica")
    line, core = place // CORES, place % CORES
    halves = decoded.reshape(CORES, rows // CORES, width)
    keep = lax.dynamic_index_in_dim(halves, core, 0, keepdims=False)
    send = lax.dynamic_index_in_dim(halves, 1 - core, 0, keepdims=False)
    got = lax.ppermute(send, "replica", replica_shift(0, 1))
    half = (keep.astype(jnp.float32) + got.astype(jnp.float32)).astype(jnp.bfloat16)
    parts = half.reshape(LINE, -1, width)
    total = lax.dynamic_index_in_dim(parts, line, 0, keepdims=False).astype(jnp.float32)
    for turn in (1, 2, 3):
        part = lax.dynamic_index_in_dim(parts, lax.rem(line + turn, LINE), 0, keepdims=False)
        got = lax.ppermute(part, "replica", replica_shift(turn, 0))
        total = total + got.astype(jnp.float32)
    total = total.astype(jnp.bfloat16)
    whole = [total]
    for turn in (1, 2, 3):
        whole.append(lax.ppermute(total, "replica", replica_shift(turn, 0)))
    order = lax.rem(line - jnp.arange(LINE, dtype=jnp.int32) + LINE, LINE)
    half = jnp.take(jnp.stack(whole), order, axis=0).reshape(-1, width)
    other = lax.ppermute(half, "replica", replica_shift(0, 1))
    even = core == 0
    return jnp.concatenate([jnp.where(even, half, other), jnp.where(even, other, half)])


def on_device(
    anchor, first_moment, second_moment, outer_momentum, activations, cotangents, token_ids, exponents
):
    place = lax.axis_index("fsdp").astype(jnp.int32)
    z, x, y = place // PLANE, (place // NY) % NX, place % NY
    masked = jnp.where((token_ids[0] != 0)[..., None], cotangents[0], jnp.zeros_like(cotangents[0]))
    half = masked.shape[1] // 2

    sent = {}
    for step in range(2):
        for mine in (0, 1):
            side = jnp.where(mine == 1, z, 1 - z)
            sent[step, mine] = split_rows(side.reshape(1), activations, step)

    early = ring_gather(masked[:, :half], X_RING)
    late = ring_gather(masked[:, half:], Y_RING)
    early = ring_gather(stack_pieces(early, x), Y_RING)
    late = ring_gather(stack_pieces(late, y), X_RING)
    sets = (early, late)

    spot = jnp.stack([x, y])
    got, own = {}, {}
    columns = {}
    for mine, step in ((0, 0), (0, 1), (1, 0), (1, 1)):
        columns[step, mine] = lax.all_to_all(
            sent[step, mine], "fsdp", 0, 0, axis_index_groups=PLANES, tiled=True
        )
    for step in range(2):
        part = contract(spot, columns[step, 0], sets, step, jnp.bfloat16)
        got[step] = lax.ppermute(part, "fsdp", Z_SWAP)
    for step in range(2):
        own[step] = contract(spot, columns[step, 1], sets, step, jnp.float32)

    decoded, new_first, new_second = adam(
        spot, anchor, first_moment, second_moment, own[0], got[0], own[1], got[1], exponents
    )
    replicas = lax.axis_size("replica")
    average = replica_sum(decoded).astype(jnp.float32) / replicas
    new_momentum = MOMENTUM * outer_momentum + average
    new_weights = anchor - OUTER_RATE * (average + MOMENTUM * new_momentum)
    return new_weights, new_momentum, new_first, new_second


def solution(mesh):
    in_specs = (
        P("fsdp", None),
        P("replica", "fsdp", None),
        P("replica", "fsdp", None),
        P("fsdp", None),
        P("replica", None, "fsdp", None),
        P("replica", None, "fsdp", None),
        P("replica", None, "fsdp"),
        P("replica", "fsdp", None),
    )
    out_specs = (
        P("fsdp", None),
        P("fsdp", None),
        P("replica", "fsdp", None),
        P("replica", "fsdp", None),
    )
    return jax.shard_map(
        on_device, mesh=mesh, in_specs=in_specs, out_specs=out_specs, check_vma=False
    )
```

time: 476 us -> 204 us (0.43)
  waiting for transfers between devices: 385 us -> 37.7 us
  starting transfers between devices: 14.9 us -> 91 us
  Pallas kernels: 0 us -> 43.9 us
  local copies, waits for them, and re-layouts: 38 us -> 17.8 us
  matrix products: 16.5 us -> 0 us
  between operations: 13.8 us -> 1.06 us
  other arithmetic: 5.12 us -> 11.3 us
    all_gather x2 -> x0, waiting for transfers between devices: 216 us -> none  [on_device(): lax.all_gather(masked[step], 'fsdp', axis=0, tiled=True)]
    all_to_all x1 -> x4, waiting for transfers between devices: 106 us -> 13.1 us  [on_device(): lax.all_to_all(sent[step, mine], 'fsdp', 0, 0, axis_index_groups=PLANES,...]
    ppermute x0 -> x26, starting transfers between devices: none -> 70.2 us  [the longest x1 22.3 us: replica_sum(): got = lax.ppermute(send, 'replica', replica_shift(0, 1))]
    psum x1 -> x0, waiting for transfers between devices: 62.6 us -> none  [on_device(): lax.psum(decoded.astype(jnp.bfloat16), 'replica').astype(jnp.float32)]
    pallas_call x0 -> x9, Pallas kernels: none -> 43.9 us  [the longest x4 22.6 us: contract(): pl.pallas_call(functools.partial(dot_kernel, step), in_specs=[pl.BlockSpe...]
    ppermute x0 -> x26, waiting for transfers between devices: none -> 24.7 us  [the longest x4 8.54 us: ring_gather(): far_zero = lax.ppermute(left[0], 'fsdp', ahead)]
    unnamed x17 -> x31, local copies, waits for them, and re-layouts: 24.6 us -> 5.19 us
    dot_general x2 -> x0, matrix products: 16.5 us -> none  [contract_tokens(): lax.dot_general(left, right, (((0,), (0,)), ((), ())), preferred_element_...]
  transfers between devices with their start and end apart: 4 -> 30, of which waited for: 4 -> 9; matrix products, arithmetic and copies ran while one was open for 8% -> 9% of each run, Pallas kernels for 0% -> 18%
where the time goes in v1:
time: 204 us; the launch traced here: 203 us
  starting transfers between devices  91 us (45%)
  Pallas kernels  43.9 us (22%)
  waiting for transfers between devices  37.7 us (18%)
  local copies, waits for them, and re-layouts  17.8 us (9%)
  other arithmetic  11.3 us (6%)
    pallas_call x4, Pallas kernels, contract(): pl.pallas_call(functools.partial(dot_kernel, step), in_specs=[pl.BlockSpe...  22.6 us
    ppermute x1, starting transfers between devices, replica_sum(): got = lax.ppermute(send, 'replica', replica_shift(0, 1))  22.3 us
    all_to_all x4, starting transfers between devices, on_device(): lax.all_to_all(sent[step, mine], 'fsdp', 0, 0, axis_index_groups=PLANES,...  20.8 us
    pallas_call x4, Pallas kernels, split_rows(): pl.pallas_call(split_kernel, grid_spec=pltpu.PrefetchScalarGridSpec(num_s...  13.4 us
    all_to_all x4, waiting for transfers between devices, on_device(): lax.all_to_all(sent[step, mine], 'fsdp', 0, 0, axis_index_groups=PLANES,...  13.1 us
    ppermute x4, starting transfers between devices, ring_gather(): far_zero = lax.ppermute(left[0], 'fsdp', ahead)  9.74 us
    ppermute x4, starting transfers between devices, ring_gather(): far_one = lax.ppermute(right[1], 'fsdp', back)  8.9 us
    ppermute x4, waiting for transfers between devices, ring_gather(): far_zero = lax.ppermute(left[0], 'fsdp', ahead)  8.54 us
  transfers between devices with their start and end apart: 30, of which 9 were waited for; matrix products, arithmetic and copies ran while one was open for 9% of the time, Pallas kernels for 18%

profile of v1, /device:TPU:1, one launch (start us, length us, event | category | flops | bytes accessed | tf_op | source)
XLA Modules:
  0.0 202.8 jit_solution(4458466810142064097)
XLA Ops:
  2.6 2.2 %collective-permute-start.7 = (bf16[2,64,1024]{2,1,0:T(8,128)(2,1)S(1)}, bf16[2,64,1024]{2,1,0:T(8,128)(2,1)S(1)}, u32[]{:S(2)}, u32[]{:S(2)}) collective-permute-start(bf16[2,64,1024]{2,1,0:T(8,128)(2,1)S(1)} %get-tuple-element.17), channel_id=1, source_target_pairs={{0,1},{1,2},{2,3},{3,0},{4,5},{5,6},{6,7},{7,4},{8,9},{9,10},{10,1... | collective-permute-start | bytes 786440 | tf_op jit(solution)/shard_map/ppermute | solution.py:75
  4.8 1.5 collective-permute-start.9
  6.3 1.2 collective-permute-start
  7.5 1.5 collective-permute-start.2
  9.0 3.4 %shard_map.117 = bf16[16,128,256]{2,1,0:T(8,128)(2,1)} custom-call(s32[1]{0:T(128)} %bitcast.28.spot, bf16[1,2,128,8192]{3,2,1,0:T(8,128)(2,1)} %features.7), custom_call_target="tpu_custom_call" | custom-call | tf_op jit(solution)/shard_map/pallas_call | solution.py:59
  12.4 4.2 %all-to-all-start.3 = ((bf16[16,128,256]{2,1,0:T(8,128)(2,1)}), bf16[16,128,256]{2,1,0:T(8,128)(2,1)S(1)}, u32[]{:S(2)}, u32[]{:S(2)}) async-start(bf16[16,128,256]{2,1,0:T(8,128)(2,1)} %shard_map.117), calls=%async_computation.3 | async-start | bytes 2097152 | tf_op jit(solution)/shard_map/all_to_all | solution.py:238
  16.7 3.4 %shard_map.115 = bf16[16,128,256]{2,1,0:T(8,128)(2,1)} custom-call(s32[1]{0:T(128)} %bitcast.2.spot, bf16[1,2,128,8192]{3,2,1,0:T(8,128)(2,1)} %features.7), custom_call_target="tpu_custom_call" | custom-call | tf_op jit(solution)/shard_map/pallas_call | solution.py:59
  20.1 1.4 collective-permute-start.8
  21.5 1.4 collective-permute-start.10
  23.0 1.4 collective-permute-start.1
  25.1 1.3 collective-permute-start.3
  26.4 8.5 %collective-permute-done.8 = bf16[64,1024]{1,0:T(8,128)(2,1)S(1)} collective-permute-done((bf16[64,1024]{1,0:T(8,128)(2,1)S(1)}, bf16[64,1024]{1,0:T(8,128)(2,1)S(1)}, u32[]{:S(2)}, u32[]{:S(2)}) %collective-permute-start.8) | collective-permute-done | bytes 131104 | tf_op jit(solution)/shard_map/ppermute | solution.py:77
  37.0 1.7 collective-permute-start.13
  39.7 2.1 %pad_maximum_fusion = bf16[2,4,64,1024]{3,2,1,0:T(8,128)(2,1)} fusion(bf16[2,1,64,1024]{3,2,1,0:T(8,128)(2,1)} %bitcast.79, bf16[2,1,64,1024]{3,2,1,0:T(8,128)(2,1)S(1)} %maximum_bitcast_fusion, bf16[2,1,64,1024]{3,2,1,0:T(8,128)(2,1)} %bitcast.78, bf16[2,1,64,1024]{3,2,1,0:T(8,128)(2,1)S(1)} %get-tuple-element.16), kind=kLoop, calls=%fused_computation.3 | loop fusion | flops 1572864 | bytes 2097152 | tf_op jit(solution)/shard_map/stack | solution.py:85
  41.8 2.8 %gather_fusion.1 = bf16[4,2,64,1024]{3,2,1,0:T(8,128)(2,1)} fusion(bf16[2,4,64,1024]{3,2,1,0:T(8,128)(2,1)} %pad_maximum_fusion, s32[1024]{0:T(1024)S(1)} %pad_clamp_fusion.2), kind=kCustom, calls=%fused_computation.clone | custom fusion | bytes 2097168 | tf_op jit(solution)/shard_map/jit(_take)/gather | solution.py:87
  45.6 4.3 %all-to-all-start.2 = ((bf16[16,128,256]{2,1,0:T(8,128)(2,1)}), bf16[16,128,256]{2,1,0:T(8,128)(2,1)}, u32[]{:S(2)}, u32[]{:S(2)}) async-start(bf16[16,128,256]{2,1,0:T(8,128)(2,1)} %shard_map.115), calls=%async_computation.2 | async-start | bytes 2097152 | tf_op jit(solution)/shard_map/all_to_all | solution.py:238
  50.0 1.4 fusion.1.refs_0_
  51.4 2.5 %collective-permute-start.6 = (bf16[2,4,64,1024]{3,2,1,0:T(8,128)(2,1)S(1)}, bf16[2,4,64,1024]{3,2,1,0:T(8,128)(2,1)}, u32[]{:S(2)}, u32[]{:S(2)}) collective-permute-start(bf16[2,4,64,1024]{3,2,1,0:T(8,128)(2,1)S(1)} %fusion.1.refs_0_), channel_id=1, source_target_pairs={{0,3},{1,0},{2,1},{3,2},{4,7},{5,4},{6,5},{7,6},{8,11},{9,8},{10,9... | collective-permute-start | bytes 3145736 | tf_op jit(solution)/shard_map/ppermute | solution.py:76
  53.9 1.2 collective-permute-start.11
  55.1 3.4 %shard_map.113 = bf16[16,128,256]{2,1,0:T(8,128)(2,1)} custom-call(s32[1]{0:T(128)} %bitcast.28.spot, bf16[1,2,128,8192]{3,2,1,0:T(8,128)(2,1)} %features.7), custom_call_target="tpu_custom_call" | custom-call | tf_op jit(solution)/shard_map/pallas_call | solution.py:59
  58.5 13.1 %all-to-all-done.2.a = bf16[16,128,256]{2,1,0:T(8,128)(2,1)} async-done(((bf16[16,128,256]{2,1,0:T(8,128)(2,1)}), bf16[16,128,256]{2,1,0:T(8,128)(2,1)}, u32[]{:S(2)}, u32[]{:S(2)}) %all-to-all-start.2) | async-done | bytes 1048608 | tf_op jit(solution)/shard_map/all_to_all | solution.py:238
  71.5 7.5 %all-to-all-start.1 = ((bf16[16,128,256]{2,1,0:T(8,128)(2,1)}), bf16[16,128,256]{2,1,0:T(8,128)(2,1)}, u32[]{:S(2)}, u32[]{:S(2)}) async-start(bf16[16,128,256]{2,1,0:T(8,128)(2,1)} %shard_map.113), calls=%async_computation.1 | async-start | bytes 2097152 | tf_op jit(solution)/shard_map/all_to_all | solution.py:238
  80.0 2.5 %collective-permute-start.16 = (bf16[4,64,1024]{2,1,0:T(8,128)(2,1)}, bf16[4,64,1024]{2,1,0:T(8,128)(2,1)}, u32[]{:S(2)}, u32[]{:S(2)}) collective-permute-start(bf16[4,64,1024]{2,1,0:T(8,128)(2,1)} %slice_bitcast_fusion), channel_id=1, source_target_pairs={{0,12},{1,13},{2,14},{3,15},{4,0},{5,1},{6,2},{7,3},{8,4},{9,5},{1... | collective-permute-start | bytes 1572872 | tf_op jit(solution)/shard_map/ppermute | solution.py:78
  82.5 3.1 %collective-permute-done.6.refs_3_ = bf16[2,4,64,1024]{3,2,1,0:T(8,128)(2,1)} collective-permute-done((bf16[2,4,64,1024]{3,2,1,0:T(8,128)(2,1)S(1)}, bf16[2,4,64,1024]{3,2,1,0:T(8,128)(2,1)}, u32[]{:S(2)}, u32[]{:S(2)}) %collective-permute-start.6) | collective-permute-done | bytes 1048608 | tf_op jit(solution)/shard_map/ppermute | solution.py:76
  85.6 1.9 slice_bitcast_fusion.1
  87.5 3.6 %collective-permute-start.15 = (bf16[4,64,1024]{2,1,0:T(8,128)(2,1)}, bf16[4,64,1024]{2,1,0:T(8,128)(2,1)}, u32[]{:S(2)}, u32[]{:S(2)}) collective-permute-start(bf16[4,64,1024]{2,1,0:T(8,128)(2,1)} %slice_bitcast_fusion.1), channel_id=1, source_target_pairs={{0,3},{1,0},{2,1},{3,2},{4,7},{5,4},{6,5},{7,6},{8,11},{9,8},{10,9... | collective-permute-start | bytes 1572872 | tf_op jit(solution)/shard_map/ppermute | solution.py:78
  91.1 1.9 slice_bitcast_fusion.2
  93.0 3.3 %collective-permute-start.12 = (bf16[4,64,1024]{2,1,0:T(8,128)(2,1)}, bf16[4,64,1024]{2,1,0:T(8,128)(2,1)S(1)}, u32[]{:S(2)}, u32[]{:S(2)}) collective-permute-start(bf16[4,64,1024]{2,1,0:T(8,128)(2,1)} %slice_bitcast_fusion.2), channel_id=1, source_target_pairs={{0,4},{1,5},{2,6},{3,7},{4,8},{5,9},{6,10},{7,11},{8,12},{9,13},{1... | collective-permute-start | bytes 1572872 | tf_op jit(solution)/shard_map/ppermute | solution.py:77
  96.3 1.9 slice_bitcast_fusion.3
  98.2 3.6 %collective-permute-start.5 = (bf16[4,64,1024]{2,1,0:T(8,128)(2,1)}, bf16[4,64,1024]{2,1,0:T(8,128)(2,1)S(1)}, u32[]{:S(2)}, u32[]{:S(2)}) collective-permute-start(bf16[4,64,1024]{2,1,0:T(8,128)(2,1)} %slice_bitcast_fusion.3), channel_id=1, source_target_pairs={{0,1},{1,2},{2,3},{3,0},{4,5},{5,6},{6,7},{7,4},{8,9},{9,10},{10,1... | collective-permute-start | bytes 1572872 | tf_op jit(solution)/shard_map/ppermute | solution.py:77
  101.8 3.4 %shard_map.111 = bf16[16,128,256]{2,1,0:T(8,128)(2,1)} custom-call(s32[1]{0:T(128)} %bitcast.2.spot, bf16[1,2,128,8192]{3,2,1,0:T(8,128)(2,1)} %features.7), custom_call_target="tpu_custom_call" | custom-call | tf_op jit(solution)/shard_map/pallas_call | solution.py:59
  105.2 4.7 %all-to-all-start = ((bf16[16,128,256]{2,1,0:T(8,128)(2,1)}), bf16[16,128,256]{2,1,0:T(8,128)(2,1)S(1)}, u32[]{:S(2)}, u32[]{:S(2)}) async-start(bf16[16,128,256]{2,1,0:T(8,128)(2,1)} %shard_map.111), calls=%async_computation | async-start | bytes 2097152 | tf_op jit(solution)/shard_map/all_to_all | solution.py:238
  110.6 5.6 %shard_map.118 = bf16[256,1024]{1,0:T(8,128)(2,1)} custom-call(s32[2]{0:T(128)} %pad_add_fusion.spot, bf16[16,128,256]{2,1,0:T(8,128)(2,1)} %copy-done.3, bf16[2,4,64,1024]{3,2,1,0:T(8,128)(2,1)} %copy-done.1, bf16[2,4,64,1024]{3,2,1,0:T(8,128)(2,1)} %collective-permute-done.4.refs_1_, bf16[4,64,1024]{2,1,0:T(8,128)(2,1)} %collective-permute-done.15.refs_2_, ...), custom_call_target="tpu_custom_call" | custom-call | tf_op jit(solution)/shard_map/pallas_call | solution.py:125
  116.1 7.0 %collective-permute-start.17 = (bf16[256,1024]{1,0:T(8,128)(2,1)}, bf16[256,1024]{1,0:T(8,128)(2,1)S(1)}, u32[]{:S(2)}, u32[]{:S(2)}) collective-permute-start(bf16[256,1024]{1,0:T(8,128)(2,1)} %shard_map.118), channel_id=1, source_target_pairs={{0,16},{1,17},{2,18},{3,19},{4,20},{5,21},{6,22},{7,23},{8,24},{9,... | collective-permute-start | bytes 1572872 | tf_op jit(solution)/shard_map/ppermute | solution.py:243
  124.7 5.6 %shard_map.114 = bf16[256,1024]{1,0:T(8,128)(2,1)} custom-call(s32[2]{0:T(128)} %pad_add_fusion.spot, bf16[16,128,256]{2,1,0:T(8,128)(2,1)} %all-to-all-done.1.a, bf16[2,4,64,1024]{3,2,1,0:T(8,128)(2,1)} %copy-done.1, bf16[2,4,64,1024]{3,2,1,0:T(8,128)(2,1)} %collective-permute-done.4.refs_1_, bf16[4,64,1024]{2,1,0:T(8,128)(2,1)} %copy-done.7, ...), custom_call_target="tpu_custom_call" | custom-call | tf_op jit(solution)/shard_map/pallas_call | solution.py:125
  131.2 5.7 %shard_map.116.own_b = f32[256,1024]{1,0:T(8,128)} custom-call(s32[2]{0:T(128)} %pad_add_fusion.spot, bf16[16,128,256]{2,1,0:T(8,128)(2,1)} %all-to-all-done.2.a, bf16[2,4,64,1024]{3,2,1,0:T(8,128)(2,1)} %copy-done.1, bf16[2,4,64,1024]{3,2,1,0:T(8,128)(2,1)} %collective-permute-done.4.refs_1_, bf16[4,64,1024]{2,1,0:T(8,128)(2,1)} %collective-permute-done.15.refs_2_, ...), custom_call_target="tpu_custom_call" | custom-call | tf_op jit(solution)/shard_map/pallas_call | solution.py:125
  137.9 5.7 %shard_map.112.own_a = f32[256,1024]{1,0:T(8,128)} custom-call(s32[2]{0:T(128)} %pad_add_fusion.spot, bf16[16,128,256]{2,1,0:T(8,128)(2,1)} %copy-done.4, bf16[2,4,64,1024]{3,2,1,0:T(8,128)(2,1)} %copy-done.1, bf16[2,4,64,1024]{3,2,1,0:T(8,128)(2,1)} %collective-permute-done.4.refs_1_, bf16[4,64,1024]{2,1,0:T(8,128)(2,1)} %copy-done.7, ...), custom_call_target="tpu_custom_call" | custom-call | tf_op jit(solution)/shard_map/pallas_call | solution.py:125
  143.7 2.9 %collective-permute-done.14.got_a = bf16[256,1024]{1,0:T(8,128)(2,1)S(1)} collective-permute-done((bf16[256,1024]{1,0:T(8,128)(2,1)}, bf16[256,1024]{1,0:T(8,128)(2,1)S(1)}, u32[]{:S(2)}, u32[]{:S(2)}) %collective-permute-start.14) | collective-permute-done | bytes 524320 | tf_op jit(solution)/shard_map/ppermute | solution.py:243
  147.4 7.9 %shard_map.119 = (bf16[256,1024]{1,0:T(8,128)(2,1)}, f32[1,256,1024]{2,1,0:T(8,128)}, f32[1,256,1024]{2,1,0:T(8,128)}) custom-call(s32[2]{0:T(128)} %pad_add_fusion.spot, f32[256,1024]{1,0:T(8,128)} %anchor.1, f32[1,256,1024]{2,1,0:T(8,128)} %first.1, f32[1,256,1024]{2,1,0:T(8,128)} %second.1, f32[256,1024]{1,0:T(8,128)} %shard_map.112.own_a, ...), custom_call_target="tpu_custom_call" | custom-call | tf_op jit(solution)/shard_map/pallas_call | solution.py:171
  156.3 22.3 %collective-permute-start.18 = (bf16[128,1024]{1,0:T(8,128)(2,1)S(1)}, bf16[128,1024]{1,0:T(8,128)(2,1)S(1)}, u32[]{:S(2)}, u32[]{:S(2)}) collective-permute-start(bf16[128,1024]{1,0:T(8,128)(2,1)S(1)} %dynamic-slice_bitcast_fusion), channel_id=1, source_target_pairs={{0,32},{32,0},{64,96},{96,64},{128,160},{160,128},{192,224},{224,1... | collective-permute-start | bytes 786440 | tf_op jit(solution)/shard_map/ppermute | solution.py:195
  180.8 2.2 %collective-permute-start.19 = (bf16[32,1024]{1,0:T(8,128)(2,1)S(1)}, bf16[32,1024]{1,0:T(8,128)(2,1)S(1)}, u32[]{:S(2)}, u32[]{:S(2)}) collective-permute-start(bf16[32,1024]{1,0:T(8,128)(2,1)S(1)} %get-tuple-element.19), channel_id=1, source_target_pairs={{0,64},{32,96},{64,128},{96,160},{128,192},{160,224},{192,0},{224,... | collective-permute-start | bytes 196616 | tf_op jit(solution)/shard_map/ppermute | solution.py:201
  183.7 2.3 %collective-permute-start.21 = (bf16[32,1024]{1,0:T(8,128)(2,1)S(1)}, bf16[32,1024]{1,0:T(8,128)(2,1)S(1)}, u32[]{:S(2)}, u32[]{:S(2)}) collective-permute-start(bf16[32,1024]{1,0:T(8,128)(2,1)S(1)} %get-tuple-element.20), channel_id=1, source_target_pairs={{0,192},{32,224},{64,0},{96,32},{128,64},{160,96},{192,128},{224,1... | collective-permute-start | bytes 196616 | tf_op jit(solution)/shard_map/ppermute | solution.py:201
  186.0 3.4 %collective-permute-done.20 = bf16[32,1024]{1,0:T(8,128)(2,1)S(1)} collective-permute-done((bf16[32,1024]{1,0:T(8,128)(2,1)S(1)}, bf16[32,1024]{1,0:T(8,128)(2,1)S(1)}, u32[]{:S(2)}, u32[]{:S(2)}) %collective-permute-start.20) | collective-permute-done | bytes 65568 | tf_op jit(solution)/shard_map/ppermute | solution.py:201
  189.4 1.8 collective-permute-start.22
  191.5 1.9 collective-permute-start.24
  194.5 3.5 %collective-permute-done.23 = bf16[32,1024]{1,0:T(8,128)(2,1)S(1)} collective-permute-done((bf16[32,1024]{1,0:T(8,128)(2,1)S(1)}, bf16[32,1024]{1,0:T(8,128)(2,1)S(1)}, u32[]{:S(2)}, u32[]{:S(2)}) %collective-permute-start.23) | collective-permute-done | bytes 65568 | tf_op jit(solution)/shard_map/ppermute | solution.py:206
  198.7 1.2 collective-permute-start.25
  201.2 1.7 multiply_subtract_fusion
  (93 shorter events, 19.9 us)
Async XLA Ops:
  2.6 17.5 %collective-permute-start.7 = (bf16[2,64,1024]{2,1,0:T(8,128)(2,1)S(1)}, bf16[2,64,1024]{2,1,0:T(8,128)(2,1)S(1)}, u32[]{:S(2)}, u32[]{:S(2)}) collective-permute-start(bf16[2,64,1024]{2,1,0:T(8,128)(2,1)S(1)} %get-tuple-element.17), channel_id=1, source_target_pairs={{0,1},{1,2},{2,3},{3,0},{4,5},{5,6},{6,7},{7,4},{8,9},{9,10},{10,1... | collective-permute-start | bytes 786440 | tf_op jit(solution)/shard_map/ppermute | solution.py:75
  4.8 16.7 %collective-permute-start.9 = (bf16[2,64,1024]{2,1,0:T(8,128)(2,1)S(1)}, bf16[2,64,1024]{2,1,0:T(8,128)(2,1)S(1)}, u32[]{:S(2)}, u32[]{:S(2)}) collective-permute-start(bf16[2,64,1024]{2,1,0:T(8,128)(2,1)S(1)} %get-tuple-element.17), channel_id=1, source_target_pairs={{0,3},{1,0},{2,1},{3,2},{4,7},{5,4},{6,5},{7,6},{8,11},{9,8},{10,9... | collective-permute-start | bytes 786440 | tf_op jit(solution)/shard_map/ppermute | solution.py:76
  6.3 16.6 %collective-permute-start = (bf16[2,64,1024]{2,1,0:T(8,128)(2,1)S(1)}, bf16[2,64,1024]{2,1,0:T(8,128)(2,1)S(1)}, u32[]{:S(2)}, u32[]{:S(2)}) collective-permute-start(bf16[2,64,1024]{2,1,0:T(8,128)(2,1)S(1)} %get-tuple-element.18), channel_id=1, source_target_pairs={{0,4},{1,5},{2,6},{3,7},{4,8},{5,9},{6,10},{7,11},{8,12},{9,13},{1... | collective-permute-start | bytes 786440 | tf_op jit(solution)/shard_map/ppermute | solution.py:75
  7.5 16.8 %collective-permute-start.2 = (bf16[2,64,1024]{2,1,0:T(8,128)(2,1)S(1)}, bf16[2,64,1024]{2,1,0:T(8,128)(2,1)S(1)}, u32[]{:S(2)}, u32[]{:S(2)}) collective-permute-start(bf16[2,64,1024]{2,1,0:T(8,128)(2,1)S(1)} %get-tuple-element.18), channel_id=1, source_target_pairs={{0,12},{1,13},{2,14},{3,15},{4,0},{5,1},{6,2},{7,3},{8,4},{9,5},{1... | collective-permute-start | bytes 786440 | tf_op jit(solution)/shard_map/ppermute | solution.py:76
  12.4 32.3 %all-to-all-start.3 = ((bf16[16,128,256]{2,1,0:T(8,128)(2,1)}), bf16[16,128,256]{2,1,0:T(8,128)(2,1)S(1)}, u32[]{:S(2)}, u32[]{:S(2)}) async-start(bf16[16,128,256]{2,1,0:T(8,128)(2,1)} %shard_map.117), calls=%async_computation.3 | async-start | bytes 2097152 | tf_op jit(solution)/shard_map/all_to_all | solution.py:238
  20.1 14.9 %collective-permute-start.8 = (bf16[64,1024]{1,0:T(8,128)(2,1)S(1)}, bf16[64,1024]{1,0:T(8,128)(2,1)S(1)}, u32[]{:S(2)}, u32[]{:S(2)}) collective-permute-start(bf16[64,1024]{1,0:T(8,128)(2,1)S(1)} %slice_bitcast_fusion.5), channel_id=1, source_target_pairs={{0,1},{1,2},{2,3},{3,0},{4,5},{5,6},{6,7},{7,4},{8,9},{9,10},{10,1... | collective-permute-start | bytes 393224 | tf_op jit(solution)/shard_map/ppermute | solution.py:77
  21.5 13.5 %copy-start.11 = (bf16[2,64,1024]{2,1,0:T(8,128)(2,1)}, bf16[2,64,1024]{2,1,0:T(8,128)(2,1)S(1)}, u32[]{:S(2)}) copy-start(bf16[2,64,1024]{2,1,0:T(8,128)(2,1)S(1)} %collective-permute-done.9) | copy-start | bytes 786436
  21.5 13.4 %collective-permute-start.10 = (bf16[64,1024]{1,0:T(8,128)(2,1)S(1)}, bf16[64,1024]{1,0:T(8,128)(2,1)S(1)}, u32[]{:S(2)}, u32[]{:S(2)}) collective-permute-start(bf16[64,1024]{1,0:T(8,128)(2,1)S(1)} %slice_bitcast_fusion.4), channel_id=1, source_target_pairs={{0,3},{1,0},{2,1},{3,2},{4,7},{5,4},{6,5},{7,6},{8,11},{9,8},{10,9... | collective-permute-start | bytes 393224 | tf_op jit(solution)/shard_map/ppermute | solution.py:78
  22.9 12.1 %copy-start.9 = (bf16[2,64,1024]{2,1,0:T(8,128)(2,1)}, bf16[2,64,1024]{2,1,0:T(8,128)(2,1)S(1)}, u32[]{:S(2)}) copy-start(bf16[2,64,1024]{2,1,0:T(8,128)(2,1)S(1)} %collective-permute-done) | copy-start | bytes 786436
  23.0 15.7 %collective-permute-start.1 = (bf16[64,1024]{1,0:T(8,128)(2,1)S(1)}, bf16[64,1024]{1,0:T(8,128)(2,1)}, u32[]{:S(2)}, u32[]{:S(2)}) collective-permute-start(bf16[64,1024]{1,0:T(8,128)(2,1)S(1)} %slice_bitcast_fusion.7), channel_id=1, source_target_pairs={{0,4},{1,5},{2,6},{3,7},{4,8},{5,9},{6,10},{7,11},{8,12},{9,13},{1... | collective-permute-start | bytes 393224 | tf_op jit(solution)/shard_map/ppermute | solution.py:77
  24.4 10.6 %copy-start.10 = (bf16[2,64,1024]{2,1,0:T(8,128)(2,1)}, bf16[2,64,1024]{2,1,0:T(8,128)(2,1)S(1)}, u32[]{:S(2)}) copy-start(bf16[2,64,1024]{2,1,0:T(8,128)(2,1)S(1)} %collective-permute-done.2) | copy-start | bytes 786436
  25.1 13.6 %collective-permute-start.3 = (bf16[64,1024]{1,0:T(8,128)(2,1)}, bf16[64,1024]{1,0:T(8,128)(2,1)}, u32[]{:S(2)}, u32[]{:S(2)}) collective-permute-start(bf16[64,1024]{1,0:T(8,128)(2,1)} %slice_bitcast_fusion.6), channel_id=1, source_target_pairs={{0,12},{1,13},{2,14},{3,15},{4,0},{5,1},{6,2},{7,3},{8,4},{9,5},{1... | collective-permute-start | bytes 393224 | tf_op jit(solution)/shard_map/ppermute | solution.py:78
  37.0 16.9 %copy-start = (bf16[2,4,64,1024]{3,2,1,0:T(8,128)(2,1)}, bf16[2,4,64,1024]{3,2,1,0:T(8,128)(2,1)S(1)}, u32[]{:S(2)}) copy-start(bf16[2,4,64,1024]{3,2,1,0:T(8,128)(2,1)S(1)} %fusion.refs_4_) | copy-start | bytes 3145732
  37.0 42.0 %collective-permute-start.13 = (bf16[2,4,64,1024]{3,2,1,0:T(8,128)(2,1)S(1)}, bf16[2,4,64,1024]{3,2,1,0:T(8,128)(2,1)S(1)}, u32[]{:S(2)}, u32[]{:S(2)}) collective-permute-start(bf16[2,4,64,1024]{3,2,1,0:T(8,128)(2,1)S(1)} %fusion.refs_4_), channel_id=1, source_target_pairs={{0,12},{1,13},{2,14},{3,15},{4,0},{5,1},{6,2},{7,3},{8,4},{9,5},{1... | collective-permute-start | bytes 3145736 | tf_op jit(solution)/shard_map/ppermute | solution.py:76
  44.6 1.0 copy-start.3
  45.6 25.9 %all-to-all-start.2 = ((bf16[16,128,256]{2,1,0:T(8,128)(2,1)}), bf16[16,128,256]{2,1,0:T(8,128)(2,1)}, u32[]{:S(2)}, u32[]{:S(2)}) async-start(bf16[16,128,256]{2,1,0:T(8,128)(2,1)} %shard_map.115), calls=%async_computation.2 | async-start | bytes 2097152 | tf_op jit(solution)/shard_map/all_to_all | solution.py:238
  51.4 28.6 %copy-start.1 = (bf16[2,4,64,1024]{3,2,1,0:T(8,128)(2,1)}, bf16[2,4,64,1024]{3,2,1,0:T(8,128)(2,1)S(1)}, u32[]{:S(2)}) copy-start(bf16[2,4,64,1024]{3,2,1,0:T(8,128)(2,1)S(1)} %fusion.1.refs_0_) | copy-start | bytes 3145732
  51.4 34.2 %collective-permute-start.6 = (bf16[2,4,64,1024]{3,2,1,0:T(8,128)(2,1)S(1)}, bf16[2,4,64,1024]{3,2,1,0:T(8,128)(2,1)}, u32[]{:S(2)}, u32[]{:S(2)}) collective-permute-start(bf16[2,4,64,1024]{3,2,1,0:T(8,128)(2,1)S(1)} %fusion.1.refs_0_), channel_id=1, source_target_pairs={{0,3},{1,0},{2,1},{3,2},{4,7},{5,4},{6,5},{7,6},{8,11},{9,8},{10,9... | collective-permute-start | bytes 3145736 | tf_op jit(solution)/shard_map/ppermute | solution.py:76
  53.9 37.3 %collective-permute-start.11 = (bf16[2,4,64,1024]{3,2,1,0:T(8,128)(2,1)S(1)}, bf16[2,4,64,1024]{3,2,1,0:T(8,128)(2,1)}, u32[]{:S(2)}, u32[]{:S(2)}) collective-permute-start(bf16[2,4,64,1024]{3,2,1,0:T(8,128)(2,1)S(1)} %fusion.refs_4_), channel_id=1, source_target_pairs={{0,4},{1,5},{2,6},{3,7},{4,8},{5,9},{6,10},{7,11},{8,12},{9,13},{1... | collective-permute-start | bytes 3145736 | tf_op jit(solution)/shard_map/ppermute | solution.py:75
  55.1 41.2 %collective-permute-start.4 = (bf16[2,4,64,1024]{3,2,1,0:T(8,128)(2,1)S(1)}, bf16[2,4,64,1024]{3,2,1,0:T(8,128)(2,1)}, u32[]{:S(2)}, u32[]{:S(2)}) collective-permute-start(bf16[2,4,64,1024]{3,2,1,0:T(8,128)(2,1)S(1)} %fusion.1.refs_0_), channel_id=1, source_target_pairs={{0,1},{1,2},{2,3},{3,0},{4,5},{5,6},{6,7},{7,4},{8,9},{9,10},{10,1... | collective-permute-start | bytes 3145736 | tf_op jit(solution)/shard_map/ppermute | solution.py:75
  71.5 33.6 %all-to-all-start.1 = ((bf16[16,128,256]{2,1,0:T(8,128)(2,1)}), bf16[16,128,256]{2,1,0:T(8,128)(2,1)}, u32[]{:S(2)}, u32[]{:S(2)}) async-start(bf16[16,128,256]{2,1,0:T(8,128)(2,1)} %shard_map.113), calls=%async_computation.1 | async-start | bytes 2097152 | tf_op jit(solution)/shard_map/all_to_all | solution.py:238
  79.0 26.1 %copy-start.2 = (bf16[2,4,64,1024]{3,2,1,0:T(8,128)(2,1)}, bf16[2,4,64,1024]{3,2,1,0:T(8,128)(2,1)S(1)}, u32[]{:S(2)}) copy-start(bf16[2,4,64,1024]{3,2,1,0:T(8,128)(2,1)S(1)} %collective-permute-done.13.refs_7_) | copy-start | bytes 3145732
  80.0 30.6 %collective-permute-start.16 = (bf16[4,64,1024]{2,1,0:T(8,128)(2,1)}, bf16[4,64,1024]{2,1,0:T(8,128)(2,1)}, u32[]{:S(2)}, u32[]{:S(2)}) collective-permute-start(bf16[4,64,1024]{2,1,0:T(8,128)(2,1)} %slice_bitcast_fusion), channel_id=1, source_target_pairs={{0,12},{1,13},{2,14},{3,15},{4,0},{5,1},{6,2},{7,3},{8,4},{9,5},{1... | collective-permute-start | bytes 1572872 | tf_op jit(solution)/shard_map/ppermute | solution.py:78
  87.5 23.1 %collective-permute-start.15 = (bf16[4,64,1024]{2,1,0:T(8,128)(2,1)}, bf16[4,64,1024]{2,1,0:T(8,128)(2,1)}, u32[]{:S(2)}, u32[]{:S(2)}) collective-permute-start(bf16[4,64,1024]{2,1,0:T(8,128)(2,1)} %slice_bitcast_fusion.1), channel_id=1, source_target_pairs={{0,3},{1,0},{2,1},{3,2},{4,7},{5,4},{6,5},{7,6},{8,11},{9,8},{10,9... | collective-permute-start | bytes 1572872 | tf_op jit(solution)/shard_map/ppermute | solution.py:78
  93.0 30.1 %collective-permute-start.12 = (bf16[4,64,1024]{2,1,0:T(8,128)(2,1)}, bf16[4,64,1024]{2,1,0:T(8,128)(2,1)S(1)}, u32[]{:S(2)}, u32[]{:S(2)}) collective-permute-start(bf16[4,64,1024]{2,1,0:T(8,128)(2,1)} %slice_bitcast_fusion.2), channel_id=1, source_target_pairs={{0,4},{1,5},{2,6},{3,7},{4,8},{5,9},{6,10},{7,11},{8,12},{9,13},{1... | collective-permute-start | bytes 1572872 | tf_op jit(solution)/shard_map/ppermute | solution.py:77
  98.2 24.9 %collective-permute-start.5 = (bf16[4,64,1024]{2,1,0:T(8,128)(2,1)}, bf16[4,64,1024]{2,1,0:T(8,128)(2,1)S(1)}, u32[]{:S(2)}, u32[]{:S(2)}) collective-permute-start(bf16[4,64,1024]{2,1,0:T(8,128)(2,1)} %slice_bitcast_fusion.3), channel_id=1, source_target_pairs={{0,1},{1,2},{2,3},{3,0},{4,5},{5,6},{6,7},{7,4},{8,9},{9,10},{10,1... | collective-permute-start | bytes 1572872 | tf_op jit(solution)/shard_map/ppermute | solution.py:77
  105.2 31.8 %all-to-all-start = ((bf16[16,128,256]{2,1,0:T(8,128)(2,1)}), bf16[16,128,256]{2,1,0:T(8,128)(2,1)S(1)}, u32[]{:S(2)}, u32[]{:S(2)}) async-start(bf16[16,128,256]{2,1,0:T(8,128)(2,1)} %shard_map.111), calls=%async_computation | async-start | bytes 2097152 | tf_op jit(solution)/shard_map/all_to_all | solution.py:238
  116.1 14.3 %copy-start.14 = (s32[1,256,8]{1,2,0:T(8,128)S(1)}, s32[1,256,8]{1,2,0:T(8,128)}, u32[]{:S(2)}) copy-start(s32[1,256,8]{1,2,0:T(8,128)} %param.17) | copy-start | bytes 24580
  116.1 27.6 %collective-permute-start.17 = (bf16[256,1024]{1,0:T(8,128)(2,1)}, bf16[256,1024]{1,0:T(8,128)(2,1)S(1)}, u32[]{:S(2)}, u32[]{:S(2)}) collective-permute-start(bf16[256,1024]{1,0:T(8,128)(2,1)} %shard_map.118), channel_id=1, source_target_pairs={{0,16},{1,17},{2,18},{3,19},{4,20},{5,21},{6,22},{7,23},{8,24},{9,... | collective-permute-start | bytes 1572872 | tf_op jit(solution)/shard_map/ppermute | solution.py:243
  123.1 0.8 copy-start.6
  123.9 0.8 copy-start.7
  130.3 16.3 %collective-permute-start.14 = (bf16[256,1024]{1,0:T(8,128)(2,1)}, bf16[256,1024]{1,0:T(8,128)(2,1)S(1)}, u32[]{:S(2)}, u32[]{:S(2)}) collective-permute-start(bf16[256,1024]{1,0:T(8,128)(2,1)} %shard_map.114), channel_id=1, source_target_pairs={{0,16},{1,17},{2,18},{3,19},{4,20},{5,21},{6,22},{7,23},{8,24},{9,... | collective-permute-start | bytes 1572872 | tf_op jit(solution)/shard_map/ppermute | solution.py:243
  137.0 1.0 copy-start.4
  143.7 57.5 %copy-start.5 = (f32[256,1024]{1,0:T(8,128)S(1)}, f32[256,1024]{1,0:T(8,128)}, u32[]{:S(2)}) copy-start(f32[256,1024]{1,0:T(8,128)} %anchor.1) | copy-start | bytes 3145732
  143.7 57.5 %copy-start.8 = (f32[256,1024]{1,0:T(8,128)S(1)}, f32[256,1024]{1,0:T(8,128)}, u32[]{:S(2)}) copy-start(f32[256,1024]{1,0:T(8,128)} %param.13) | copy-start | bytes 3145732
  143.7 2.9 %copy-start.12 = (bf16[256,1024]{1,0:T(8,128)(2,1)}, bf16[256,1024]{1,0:T(8,128)(2,1)S(1)}, u32[]{:S(2)}) copy-start(bf16[256,1024]{1,0:T(8,128)(2,1)S(1)} %collective-permute-done.17.got_b) | copy-start | bytes 1572868
  146.6 0.8 copy-start.13
  156.3 23.4 %collective-permute-start.18 = (bf16[128,1024]{1,0:T(8,128)(2,1)S(1)}, bf16[128,1024]{1,0:T(8,128)(2,1)S(1)}, u32[]{:S(2)}, u32[]{:S(2)}) collective-permute-start(bf16[128,1024]{1,0:T(8,128)(2,1)S(1)} %dynamic-slice_bitcast_fusion), channel_id=1, source_target_pairs={{0,32},{32,0},{64,96},{96,64},{128,160},{160,128},{192,224},{224,1... | collective-permute-start | bytes 786440 | tf_op jit(solution)/shard_map/ppermute | solution.py:195
  180.8 5.2 %collective-permute-start.19 = (bf16[32,1024]{1,0:T(8,128)(2,1)S(1)}, bf16[32,1024]{1,0:T(8,128)(2,1)S(1)}, u32[]{:S(2)}, u32[]{:S(2)}) collective-permute-start(bf16[32,1024]{1,0:T(8,128)(2,1)S(1)} %get-tuple-element.19), channel_id=1, source_target_pairs={{0,64},{32,96},{64,128},{96,160},{128,192},{160,224},{192,0},{224,... | collective-permute-start | bytes 196616 | tf_op jit(solution)/shard_map/ppermute | solution.py:201
  183.0 6.4 %collective-permute-start.20 = (bf16[32,1024]{1,0:T(8,128)(2,1)S(1)}, bf16[32,1024]{1,0:T(8,128)(2,1)S(1)}, u32[]{:S(2)}, u32[]{:S(2)}) collective-permute-start(bf16[32,1024]{1,0:T(8,128)(2,1)S(1)} %get-tuple-element.21), channel_id=1, source_target_pairs={{0,128},{32,160},{64,192},{96,224},{128,0},{160,32},{192,64},{224,... | collective-permute-start | bytes 196616 | tf_op jit(solution)/shard_map/ppermute | solution.py:201
  183.7 5.7 %collective-permute-start.21 = (bf16[32,1024]{1,0:T(8,128)(2,1)S(1)}, bf16[32,1024]{1,0:T(8,128)(2,1)S(1)}, u32[]{:S(2)}, u32[]{:S(2)}) collective-permute-start(bf16[32,1024]{1,0:T(8,128)(2,1)S(1)} %get-tuple-element.20), channel_id=1, source_target_pairs={{0,192},{32,224},{64,0},{96,32},{128,64},{160,96},{192,128},{224,1... | collective-permute-start | bytes 196616 | tf_op jit(solution)/shard_map/ppermute | solution.py:201
  189.4 5.0 %collective-permute-start.22 = (bf16[32,1024]{1,0:T(8,128)(2,1)S(1)}, bf16[32,1024]{1,0:T(8,128)(2,1)S(1)}, u32[]{:S(2)}, u32[]{:S(2)}) collective-permute-start(bf16[32,1024]{1,0:T(8,128)(2,1)S(1)} %fusion.5), channel_id=1, source_target_pairs={{0,64},{32,96},{64,128},{96,160},{128,192},{160,224},{192,0},{224,... | collective-permute-start | bytes 196616 | tf_op jit(solution)/shard_map/ppermute | solution.py:206
  191.2 6.7 %collective-permute-start.23 = (bf16[32,1024]{1,0:T(8,128)(2,1)S(1)}, bf16[32,1024]{1,0:T(8,128)(2,1)S(1)}, u32[]{:S(2)}, u32[]{:S(2)}) collective-permute-start(bf16[32,1024]{1,0:T(8,128)(2,1)S(1)} %fusion.5), channel_id=1, source_target_pairs={{0,128},{32,160},{64,192},{96,224},{128,0},{160,32},{192,64},{224,... | collective-permute-start | bytes 196616 | tf_op jit(solution)/shard_map/ppermute | solution.py:206
  191.5 6.5 %collective-permute-start.24 = (bf16[32,1024]{1,0:T(8,128)(2,1)S(1)}, bf16[32,1024]{1,0:T(8,128)(2,1)S(1)}, u32[]{:S(2)}, u32[]{:S(2)}) collective-permute-start(bf16[32,1024]{1,0:T(8,128)(2,1)S(1)} %fusion.5), channel_id=1, source_target_pairs={{0,192},{32,224},{64,0},{96,32},{128,64},{160,96},{192,128},{224,1... | collective-permute-start | bytes 196616 | tf_op jit(solution)/shard_map/ppermute | solution.py:206
  198.7 2.4 %collective-permute-start.25 = (bf16[128,1024]{1,0:T(8,128)(2,1)S(1)}, bf16[128,1024]{1,0:T(8,128)(2,1)S(1)}, u32[]{:S(2)}, u32[]{:S(2)}) collective-permute-start(bf16[128,1024]{1,0:T(8,128)(2,1)S(1)} %bitcast_select_fusion.1), channel_id=1, source_target_pairs={{0,32},{32,0},{64,96},{96,64},{128,160},{160,128},{192,224},{224,1... | collective-permute-start | bytes 786440 | tf_op jit(solution)/shard_map/ppermute | solution.py:209

commit v2 on v0

v2 whole, which is shorter than its diff:
```python
import functools

import jax
import jax.numpy as jnp
from jax import lax
from jax.experimental import pallas as pl
from jax.experimental.pallas import tpu as pltpu
from jax.sharding import PartitionSpec as P

BETA_ONE = 0.9
BETA_TWO = 0.95
EPSILON = 1e-08
INNER_RATE = 0.1
DECAY = 0.1
OUTER_RATE = 0.7
MOMENTUM = 0.9
CODE_LIMIT = 448.0
LOWEST = 13

NZ, NX, NY = 2, 4, 4
PLANE = NX * NY
LINE, CORES = 4, 2
LIMIT = 12 * 1024 * 1024

HBM = pl.BlockSpec(memory_space=pltpu.HBM)
VMEM = pl.BlockSpec(memory_space=pltpu.VMEM)
SMEM = pl.BlockSpec(memory_space=pltpu.SMEM)
PARAMS = pltpu.CompilerParams(vmem_limit_bytes=LIMIT)
SHORT = pl.CostEstimate(flops=1, bytes_accessed=1, transcendentals=0)


def fsdp_shift(dz, dx, dy):
    def at(z, x, y):
        return ((z % NZ) * NX + x % NX) * NY + y % NY

    return [
        (at(z, x, y), at(z + dz, x + dx, y + dy))
        for z in range(NZ)
        for x in range(NX)
        for y in range(NY)
    ]


def replica_shift(dz, dc):
    return [
        (z * CORES + c, ((z + dz) % LINE) * CORES + (c + dc) % CORES)
        for z in range(LINE)
        for c in range(CORES)
    ]


def along(dim, block, turn):
    shift = (0, turn, 0) if dim == "x" else (0, 0, turn)
    return lax.ppermute(block, "fsdp", fsdp_shift(*shift))


def after(value, earlier):
    return lax.optimization_barrier((value, earlier))[0]


def shape_of(shape, dtype):
    return jax.ShapeDtypeStruct(shape, dtype)


HANDED = 10


def pack_kernel(dim, step, spot, ids, cotangents, features, own, ahead, back, *scratch):
    held, words, grads, sems = scratch
    tokens, shard = own.shape[1:]
    part = tokens // 4
    small = [
        pltpu.make_async_copy(ids, words, sems.at[4]),
        pltpu.make_async_copy(cotangents.at[0, step], grads, sems.at[5]),
    ]
    loads = []
    for q in range(4):
        rows = pl.ds(q * part, part)
        loads.append(pltpu.make_async_copy(features.at[0, step, rows], held.at[rows], sems.at[q]))
    for load in small + loads:
        load.start()
    for load in small:
        load.wait()
    live = jnp.sum((words[0, step : step + 1, :] != 0).astype(jnp.int32))
    alive = lax.broadcasted_iota(jnp.int32, (tokens, shard), 0) < live
    for n in range(4):
        block = grads[:, n * shard : (n + 1) * shard]
        block = jnp.where(alive, block, jnp.zeros_like(block))
        own[8 + n] = block
        ahead[8 + (n + 2) % 4] = block
        back[8 + n] = block
    x, y, z = spot[0], spot[1], spot[4]
    for q, load in enumerate(loads):
        load.wait()
        rows = slice(q * part, (q + 1) * part)
        for turn in range(4):
            for side in range(2):
                for u in range(4):
                    to_x, to_y = (u, turn) if dim == "y" else (turn, u)
                    owner = (lax.rem(z + 1 + side, NZ) * NX + lax.rem(x + to_x, NX)) * NY
                    owner = owner + lax.rem(y + to_y, NY)
                    at = pl.ds(pl.multiple_of(owner * shard, shard), shard)
                    out, slot = (own, ahead, back if side else ahead, back)[turn], side * 4 + u
                    out[12 + u if turn == 2 else slot, rows, :] = held[rows, at]


def pack(dim, step, spot, ids, cotangents, features):
    tokens, rows = features.shape[2:]
    shard = rows // (NZ * NX * NY)
    return pl.pallas_call(
        functools.partial(pack_kernel, dim, step),
        in_specs=[SMEM, HBM, HBM, HBM],
        out_specs=[VMEM] * 3,
        out_shape=[shape_of((blocks, tokens, shard), features.dtype) for blocks in (12, 16, 16)],
        scratch_shapes=[
            pltpu.VMEM((tokens, rows), features.dtype),
            pltpu.VMEM(ids.shape, ids.dtype),
            pltpu.VMEM(cotangents.shape[2:], cotangents.dtype),
            pltpu.SemaphoreType.DMA((6,)),
        ],
        cost_estimate=SHORT,
        compiler_params=PARAMS,
    )(spot, ids, cotangents, features)


def products(side, turn, pieces):
    own, ahead, back, handed_ahead, handed_back = pieces
    slot = side * 4 + turn
    handed = handed_back if side else handed_ahead
    left = jnp.concatenate([own[slot], ahead[slot], back[slot], handed[2 + turn]], axis=0)
    for n in range(4):
        far = (handed_back if n // 2 else handed_ahead)[n % 2]
        right = jnp.concatenate([own[8 + n], ahead[8 + (n + 2) % 4], back[8 + n], far], axis=0)
        yield n, lax.dot_general(
            left, right, (((0,), (0,)), ((), ())), preferred_element_type=jnp.float32
        )


def opposite_kernel(side, *refs):
    for step in range(2):
        pieces, (low, high) = refs[5 * step : 5 * step + 5], refs[10 + 2 * step : 12 + 2 * step]
        shard, half = pieces[0].shape[2], low.shape[0]
        for n, value in products(side, 2, pieces):
            low[:, n * shard : (n + 1) * shard] = value[:half].astype(low.dtype)
            high[:, n * shard : (n + 1) * shard] = value[half:].astype(high.dtype)


def opposite(side, pieces):
    _, _, shard = pieces[0].shape
    out = shape_of((shard // 2, 4 * shard), pieces[0].dtype)
    return pl.pallas_call(
        functools.partial(opposite_kernel, side),
        in_specs=[VMEM] * 10, out_specs=[VMEM] * 4, out_shape=[out] * 4,
        cost_estimate=SHORT, compiler_params=PARAMS,
    )(*pieces)


def nearest_kernel(side, *refs):
    for step in range(2):
        pieces, (low, high) = refs[5 * step : 5 * step + 5], refs[10 + 2 * step : 12 + 2 * step]
        own, ahead, back = refs[14 + 3 * step : 17 + 3 * step]
        shard, half = pieces[0].shape[2], low.shape[0]
        for n, value in products(side, 1, pieces):
            at = slice(n * shard, (n + 1) * shard)
            ahead[:half, at] = (value[:half] + low[:, at].astype(jnp.float32)).astype(ahead.dtype)
            ahead[half:, at] = value[half:].astype(ahead.dtype)
        for n, value in products(side, 3, pieces):
            at = slice(n * shard, (n + 1) * shard)
            back[:half, at] = value[:half].astype(back.dtype)
            back[half:, at] = (value[half:] + high[:, at].astype(jnp.float32)).astype(back.dtype)
        for n, value in products(side, 0, pieces):
            own[:, n * shard : (n + 1) * shard] = value


def nearest(side, pieces, halves):
    _, _, shard = pieces[0].shape
    shape = (shard, 4 * shard)
    sent = shape_of(shape, pieces[0].dtype)
    out = [shape_of(shape, jnp.float32), sent, sent]
    return pl.pallas_call(
        functools.partial(nearest_kernel, side),
        in_specs=[VMEM] * 14, out_specs=[VMEM] * 6, out_shape=out * 2,
        cost_estimate=SHORT, compiler_params=PARAMS,
    )(*pieces, *halves)


def total_kernel(*refs):
    ins, out = refs[:-1], refs[-1]

    @pl.loop(0, out.shape[1], step=16)
    def _(r):
        rows = pl.ds(pl.multiple_of(r, 16), 16)
        for step in range(2):
            total = ins[3 * step][rows, :]
            for ref in ins[3 * step + 1 : 3 * step + 3]:
                total = total + ref[rows, :].astype(jnp.float32)
            out[step, rows, :] = total.astype(out.dtype)


def totals(parts, dtype):
    return pl.pallas_call(
        total_kernel, in_specs=[VMEM] * 6, out_specs=VMEM,
        out_shape=shape_of((2,) + parts[0].shape, dtype), cost_estimate=SHORT, compiler_params=PARAMS,
    )(*parts)


def add_kernel(*refs):
    ins, out = refs[:-1], refs[-1]

    @pl.loop(0, out.shape[0], step=16)
    def _(r):
        rows = pl.ds(pl.multiple_of(r, 16), 16)
        total = ins[0][rows, :].astype(jnp.float32)
        for ref in ins[1:]:
            total = total + ref[rows, :].astype(jnp.float32)
        out[rows, :] = total.astype(out.dtype)


def add(parts, dtype):
    return pl.pallas_call(
        add_kernel, in_specs=[VMEM] * len(parts), out_specs=VMEM,
        out_shape=shape_of(parts[0].shape, dtype), cost_estimate=SHORT, compiler_params=PARAMS,
    )(*parts)


def adam_update(weights, first, second, gradient):
    first = BETA_ONE * first + (1.0 - BETA_ONE) * gradient
    second = BETA_TWO * second + (1.0 - BETA_TWO) * gradient * gradient
    weights = weights - INNER_RATE * (first / (jnp.sqrt(second) + EPSILON) + DECAY * weights)
    return weights, first, second


def gradient_of(step, own, got, here):
    here = (step,) + here
    return own[here] + got[here].astype(jnp.float32)


def early_kernel(anchor, first, second, own, got, mid_weights, mid_first, mid_second):
    @pl.loop(0, anchor.shape[0], step=16)
    def _(r):
        rows = pl.ds(pl.multiple_of(r, 16), 16)
        for c in range(0, anchor.shape[1], 256):
            here = (rows, pl.ds(c, 256))
            mid_weights[here], mid_first[here], mid_second[here] = adam_update(
                anchor[here], first[(0,) + here], second[(0,) + here], gradient_of(0, own, got, here)
            )


def early_step(anchor, first, second, own, got):
    out = shape_of(anchor.shape, jnp.float32)
    return pl.pallas_call(
        early_kernel, in_specs=[VMEM] * 5, out_specs=[VMEM] * 3, out_shape=[out] * 3,
        cost_estimate=SHORT, compiler_params=PARAMS,
    )(anchor, first, second, own, got)


def code_kernel(spot, anchor, weights, first, second, own, got, scale, send, keep):
    half = anchor.shape[0] // CORES
    for side, out in ((1, send), (0, keep)):
        base = lax.rem(spot[2] + side, CORES) * half

        @pl.loop(0, half, step=16)
        def _(r, base=base, out=out):
            rows = pl.ds(pl.multiple_of(base + r, 16), 16)
            for c in range(0, anchor.shape[1], 256):
                here = (rows, pl.ds(c, 256))
                gradient = gradient_of(1, own, got, here)
                end = adam_update(weights[here], first[here], second[here], gradient)[0]
                delta = anchor[here] - end
                for block in range(2):
                    at = c // 128 + block
                    power = jnp.broadcast_to(scale[0, rows, at : at + 1], (16, 128))
                    ones = jnp.ones_like(power)
                    factor = jnp.left_shift(ones, -power).astype(jnp.float32)
                    back = jnp.left_shift(ones, power + LOWEST).astype(jnp.float32) * 2.0**-LOWEST
                    coded = delta[:, block * 128 : (block + 1) * 128] * factor
                    coded = jnp.clip(coded, -CODE_LIMIT, CODE_LIMIT).astype(jnp.bfloat16)
                    out[pl.ds(pl.multiple_of(r, 16), 16), pl.ds(at * 128, 128)] = (
                        coded.astype(jnp.float32) * back
                    ).astype(jnp.bfloat16)


def code(spot, anchor, weights, first, second, own, got, exponents):
    rows, width = anchor.shape
    part = shape_of((rows // CORES, width), jnp.bfloat16)
    return pl.pallas_call(
        code_kernel, in_specs=[SMEM] + [VMEM] * 7, out_specs=[VMEM] * 2, out_shape=[part] * 2,
        cost_estimate=SHORT, compiler_params=PARAMS,
    )(spot, anchor, weights, first, second, own, got, exponents)


def moment_kernel(first, second, own, got, new_first, new_second):
    @pl.loop(0, first.shape[0], step=16)
    def _(r):
        rows = pl.ds(pl.multiple_of(r, 16), 16)
        for c in range(0, first.shape[1], 256):
            here = (rows, pl.ds(c, 256))
            gradient = gradient_of(1, own, got, here)
            _, one, two = adam_update(first[here], first[here], second[here], gradient)
            new_first[(0,) + here] = one
            new_second[(0,) + here] = two


def moments(first, second, own, got):
    out = shape_of((1,) + first.shape, first.dtype)
    return pl.pallas_call(
        moment_kernel, in_specs=[VMEM] * 4, out_specs=[VMEM] * 2, out_shape=[out] * 2,
        cost_estimate=SHORT, compiler_params=PARAMS,
    )(first, second, own, got)


def pair_kernel(spot, keep, got, *outs):
    rows = outs[0].shape[0]
    for turn, out in enumerate(outs):
        at = pl.ds(pl.multiple_of(lax.rem(spot[3] + turn, LINE) * rows, rows), rows)
        total = keep[at, :].astype(jnp.float32) + got[at, :].astype(jnp.float32)
        out[...] = total.astype(out.dtype)


def pair_sum(spot, keep, got):
    rows, width = keep.shape
    out = shape_of((rows // LINE, width), keep.dtype)
    return pl.pallas_call(
        pair_kernel, in_specs=[SMEM, VMEM, VMEM], out_specs=[VMEM] * LINE, out_shape=[out] * LINE,
        cost_estimate=SHORT, compiler_params=PARAMS,
    )(spot, keep, got)


def join_kernel(spot, *refs):
    out = refs[-1]
    rows = refs[0].shape[0]
    for turn, ref in enumerate(refs[:-1]):
        at = pl.ds(pl.multiple_of(lax.rem(spot[3] - turn + LINE, LINE) * rows, rows), rows)
        out[at, :] = ref[...]


def join(spot, parts):
    rows, width = parts[0].shape
    return pl.pallas_call(
        join_kernel, in_specs=[SMEM] + [VMEM] * len(parts), out_specs=VMEM,
        out_shape=shape_of((rows * len(parts), width), parts[0].dtype), cost_estimate=SHORT, compiler_params=PARAMS,
    )(spot, *parts)


def replica_sum(spot, got, keep, late):
    parts = pair_sum(spot, keep, got)
    total = [parts[0]]
    for turn in (1, 2, 3):
        total.append(lax.ppermute(parts[turn], "replica", replica_shift(turn, 0)))
    total = add(total, jnp.bfloat16)
    whole = [total]
    for turn in (1, 2, 3):
        whole.append(lax.ppermute(total, "replica", replica_shift(turn, 0)))
    half = join(after(spot, late), whole)
    other = lax.ppermute(half, "replica", replica_shift(0, 1))
    even = spot[2] == 0
    return jnp.concatenate([jnp.where(even, half, other), jnp.where(even, other, half)])


def on_device(
    anchor, first_moment, second_moment, outer_momentum, activations, cotangents, token_ids, exponents
):
    place = lax.axis_index("fsdp").astype(jnp.int32)
    z, x, y = place // PLANE, (place // NY) % NX, place % NY
    copy = lax.axis_index("replica").astype(jnp.int32)
    spot = jnp.stack([x, y, copy % CORES, copy // CORES, z])

    rings = ("y", "x")

    sent = [pack("y", 0, spot, token_ids, cotangents, activations)]
    sent.append(pack("x", 1, spot, token_ids, cotangents, activations))
    ahead = [along(ring, block[1], 1) for ring, block in zip(rings, sent)]
    back = [along(ring, block[2], -1) for ring, block in zip(rings, sent)]
    handed_ahead = [along(ring, block[HANDED:], 1) for ring, block in zip(rings, ahead)]
    handed_back = [along(ring, block[HANDED:], -1) for ring, block in zip(rings, back)]
    pieces = []
    for step in range(2):
        pieces += [sent[step][0], ahead[step], back[step], handed_ahead[step], handed_back[step]]

    def reduce(side, pieces, dtype):
        low_a, high_a, low_b, high_b = opposite(side, pieces)
        halves = along("x", low_a, 1), along("x", high_a, -1), along("y", low_b, 1), along("y", high_b, -1)
        own_a, ahead_a, back_a, own_b, ahead_b, back_b = nearest(side, pieces, halves)
        parts = own_a, along("x", ahead_a, 1), along("x", back_a, -1)
        parts += own_b, along("y", ahead_b, 1), along("y", back_b, -1)
        return totals(parts, dtype)

    theirs = reduce(0, pieces, jnp.bfloat16)
    got = lax.ppermute(theirs, "fsdp", fsdp_shift(1, 0, 0))
    own = reduce(1, lax.optimization_barrier(pieces + [theirs])[:-1], jnp.float32)

    weights, first, second = early_step(anchor, first_moment, second_moment, own, got)
    send, keep = code(spot, anchor, weights, first, second, own, got, exponents)
    other = lax.ppermute(send, "replica", replica_shift(0, 1))
    new_first, new_second = moments(first, second, own, after(got, other))
    replicas = lax.axis_size("replica")
    average = replica_sum(spot, other, keep, new_first).astype(jnp.float32) / replicas
    new_momentum = MOMENTUM * outer_momentum + average
    new_weights = anchor - OUTER_RATE * (average + MOMENTUM * new_momentum)
    return new_weights, new_momentum, new_first, new_second


def solution(mesh):
    in_specs = (
        P("fsdp", None),
        P("replica", "fsdp", None),
        P("replica", "fsdp", None),
        P("fsdp", None),
        P("replica", None, "fsdp", None),
        P("replica", None, "fsdp", None),
        P("replica", None, "fsdp"),
        P("replica", "fsdp", None),
    )
    out_specs = (
        P("fsdp", None),
        P("fsdp", None),
        P("replica", "fsdp", None),
        P("replica", "fsdp", None),
    )
    return jax.shard_map(
        on_device, mesh=mesh, in_specs=in_specs, out_specs=out_specs, check_vma=False
    )
```

time: 476 us -> 150 us (0.32)
  waiting for transfers between devices: 385 us -> 52.4 us
  starting transfers between devices: 14.9 us -> 69.2 us
  local copies, waits for them, and re-layouts: 38 us -> 8.63 us
  Pallas kernels: 0 us -> 17.2 us
  matrix products: 16.5 us -> 0 us
  between operations: 13.8 us -> 0.93 us
    all_gather x2 -> x0, waiting for transfers between devices: 216 us -> none  [on_device(): lax.all_gather(masked[step], 'fsdp', axis=0, tiled=True)]
    all_to_all x1 -> x0, waiting for transfers between devices: 106 us -> none  [on_device(): lax.all_to_all(activations[0], 'fsdp', split_axis=2, concat_axis=1, tiled...]
    ppermute x0 -> x33, starting transfers between devices: none -> 69.2 us  [the longest x24 35.3 us: along(): return lax.ppermute(block, 'fsdp', fsdp_shift(*shift))]
    psum x1 -> x0, waiting for transfers between devices: 62.6 us -> none  [on_device(): lax.psum(decoded.astype(jnp.bfloat16), 'replica').astype(jnp.float32)]
    ppermute x0 -> x33, waiting for transfers between devices: none -> 52.4 us  [the longest x24 45.9 us: along(): return lax.ppermute(block, 'fsdp', fsdp_shift(*shift))]
    pallas_call x0 -> x14, Pallas kernels: none -> 17.2 us  [the longest x2 4.73 us: nearest(): pl.pallas_call(functools.partial(nearest_kernel, side), in_specs=[VMEM] *...]
    dot_general x2 -> x0, matrix products: 16.5 us -> none  [contract_tokens(): lax.dot_general(left, right, (((0,), (0,)), ((), ())), preferred_element_...]
    unnamed x17 -> x25, local copies, waits for them, and re-layouts: 24.6 us -> 8.44 us
  transfers between devices with their start and end apart: 4 -> 33, of which waited for: 4 -> 19; matrix products, arithmetic and copies ran while one was open for 8% -> 0% of each run, Pallas kernels for 0% -> 6%
where the time goes in v2:
time: 150 us
  starting transfers between devices  69.2 us (46%)
  waiting for transfers between devices  52.4 us (35%)
  Pallas kernels  17.2 us (11%)
  local copies, waits for them, and re-layouts  8.63 us (6%)
  other arithmetic  1.68 us (1%)
    ppermute x24, waiting for transfers between devices, along(): return lax.ppermute(block, 'fsdp', fsdp_shift(*shift))  45.9 us
    ppermute x24, starting transfers between devices, along(): return lax.ppermute(block, 'fsdp', fsdp_shift(*shift))  35.3 us
    ppermute x1, starting transfers between devices, on_device(): other = lax.ppermute(send, 'replica', replica_shift(0, 1))  13.5 us
    unnamed x25, local copies, waits for them, and re-layouts  8.44 us
    ppermute x1, starting transfers between devices, on_device(): got = lax.ppermute(theirs, 'fsdp', fsdp_shift(1, 0, 0))  8.01 us
    ppermute x3, starting transfers between devices, replica_sum(): total.append(lax.ppermute(parts[turn], 'replica', replica_shift(turn, 0)))  5.33 us
    pallas_call x2, Pallas kernels, nearest(): pl.pallas_call(functools.partial(nearest_kernel, side), in_specs=[VMEM] *...  4.73 us
    ppermute x3, starting transfers between devices, replica_sum(): whole.append(lax.ppermute(total, 'replica', replica_shift(turn, 0)))  4.14 us
  transfers between devices with their start and end apart: 33, of which 19 were waited for; matrix products, arithmetic and copies ran while one was open for 0% of the time, Pallas kernels for 6%

profile of v2, /device:TPU:1, one launch (start us, length us, event | category | flops | bytes accessed | tf_op | source)
XLA Modules:
  0.0 150.0 jit_solution(13578045172040570401)
XLA Ops:
  0.8 2.2 %copy-done = bf16[1,2,128,8192]{3,2,1,0:T(8,128)(2,1)S(1)} copy-done((bf16[1,2,128,8192]{3,2,1,0:T(8,128)(2,1)S(1)}, bf16[1,2,128,8192]{3,2,1,0:T(8,128)(2,1)}, u32[]{:S(2)}) %copy-start) | copy-done | bytes 4194328
  4.7 1.2 shard_map.111
  5.9 2.2 %collective-permute-start = (bf16[16,128,256]{2,1,0:T(8,128)(2,1)S(1)}, bf16[16,128,256]{2,1,0:T(8,128)(2,1)S(1)}, u32[]{:S(2)}, u32[]{:S(2)}) collective-permute-start(bf16[16,128,256]{2,1,0:T(8,128)(2,1)S(1)} %get-tuple-element.54), channel_id=1, source_target_pairs={{0,1},{1,2},{2,3},{3,0},{4,5},{5,6},{6,7},{7,4},{8,9},{9,10},{10,1... | collective-permute-start | bytes 3145736 | tf_op jit(solution)/shard_map/ppermute | solution.py:54
  8.1 1.5 %collective-permute-start.1 = (bf16[16,128,256]{2,1,0:T(8,128)(2,1)S(1)}, bf16[16,128,256]{2,1,0:T(8,128)(2,1)S(1)}, u32[]{:S(2)}, u32[]{:S(2)}) collective-permute-start(bf16[16,128,256]{2,1,0:T(8,128)(2,1)S(1)} %get-tuple-element.55), channel_id=1, source_target_pairs={{0,3},{1,0},{2,1},{3,2},{4,7},{5,4},{6,5},{7,6},{8,11},{9,8},{10,9... | collective-permute-start | bytes 3145736 | tf_op jit(solution)/shard_map/ppermute | solution.py:54
  9.7 1.2 shard_map.112
  10.9 1.3 collective-permute-start.4
  12.2 1.5 collective-permute-start.5
  13.6 16.8 %collective-permute-done.refs_1_ = bf16[16,128,256]{2,1,0:T(8,128)(2,1)S(1)} collective-permute-done((bf16[16,128,256]{2,1,0:T(8,128)(2,1)S(1)}, bf16[16,128,256]{2,1,0:T(8,128)(2,1)S(1)}, u32[]{:S(2)}, u32[]{:S(2)}) %collective-permute-start) | collective-permute-done | bytes 1048608 | tf_op jit(solution)/shard_map/ppermute | solution.py:54
  30.4 1.6 %collective-permute-start.2 = (bf16[6,128,256]{2,1,0:T(8,128)(2,1)S(1)}, bf16[6,128,256]{2,1,0:T(8,128)(2,1)S(1)}, u32[]{:S(2)}, u32[]{:S(2)}) collective-permute-start(bf16[6,128,256]{2,1,0:T(8,128)(2,1)S(1)} %slice.16), channel_id=1, source_target_pairs={{0,1},{1,2},{2,3},{3,0},{4,5},{5,6},{6,7},{7,4},{8,9},{9,10},{10,1... | collective-permute-start | bytes 1179656 | tf_op jit(solution)/shard_map/ppermute | solution.py:54
  32.1 1.7 %collective-permute-start.3 = (bf16[6,128,256]{2,1,0:T(8,128)(2,1)S(1)}, bf16[6,128,256]{2,1,0:T(8,128)(2,1)S(1)}, u32[]{:S(2)}, u32[]{:S(2)}) collective-permute-start(bf16[6,128,256]{2,1,0:T(8,128)(2,1)S(1)} %slice.17), channel_id=1, source_target_pairs={{0,3},{1,0},{2,1},{3,2},{4,7},{5,4},{6,5},{7,6},{8,11},{9,8},{10,9... | collective-permute-start | bytes 1179656 | tf_op jit(solution)/shard_map/ppermute | solution.py:54
  34.0 2.4 %collective-permute-start.6 = (bf16[6,128,256]{2,1,0:T(8,128)(2,1)S(1)}, bf16[6,128,256]{2,1,0:T(8,128)(2,1)S(1)}, u32[]{:S(2)}, u32[]{:S(2)}) collective-permute-start(bf16[6,128,256]{2,1,0:T(8,128)(2,1)S(1)} %slice.18), channel_id=1, source_target_pairs={{0,4},{1,5},{2,6},{3,7},{4,8},{5,9},{6,10},{7,11},{8,12},{9,13},{1... | collective-permute-start | bytes 1179656 | tf_op jit(solution)/shard_map/ppermute | solution.py:54
  36.5 1.4 collective-permute-start.7
  37.8 2.3 %collective-permute-done.2.refs_3_ = bf16[6,128,256]{2,1,0:T(8,128)(2,1)S(1)} collective-permute-done((bf16[6,128,256]{2,1,0:T(8,128)(2,1)S(1)}, bf16[6,128,256]{2,1,0:T(8,128)(2,1)S(1)}, u32[]{:S(2)}, u32[]{:S(2)}) %collective-permute-start.2) | collective-permute-done | bytes 393248 | tf_op jit(solution)/shard_map/ppermute | solution.py:54
  40.8 3.2 %collective-permute-done.6.refs_8_ = bf16[6,128,256]{2,1,0:T(8,128)(2,1)S(1)} collective-permute-done((bf16[6,128,256]{2,1,0:T(8,128)(2,1)S(1)}, bf16[6,128,256]{2,1,0:T(8,128)(2,1)S(1)}, u32[]{:S(2)}, u32[]{:S(2)}) %collective-permute-start.6) | collective-permute-done | bytes 393248 | tf_op jit(solution)/shard_map/ppermute | solution.py:54
  45.7 2.7 %collective-permute-start.11 = (bf16[128,1024]{1,0:T(8,128)(2,1)S(1)}, bf16[128,1024]{1,0:T(8,128)(2,1)S(1)}, u32[]{:S(2)}, u32[]{:S(2)}) collective-permute-start(bf16[128,1024]{1,0:T(8,128)(2,1)S(1)} %get-tuple-element.62), channel_id=1, source_target_pairs={{0,3},{1,0},{2,1},{3,2},{4,7},{5,4},{6,5},{7,6},{8,11},{9,8},{10,9... | collective-permute-start | bytes 786440 | tf_op jit(solution)/shard_map/ppermute | solution.py:54
  48.3 1.2 collective-permute-start.8
  49.5 1.5 collective-permute-start.9
  52.1 3.0 %collective-permute-done.8.refs_10_ = bf16[128,1024]{1,0:T(8,128)(2,1)S(1)} collective-permute-done((bf16[128,1024]{1,0:T(8,128)(2,1)S(1)}, bf16[128,1024]{1,0:T(8,128)(2,1)S(1)}, u32[]{:S(2)}, u32[]{:S(2)}) %collective-permute-start.8) | collective-permute-done | bytes 262176 | tf_op jit(solution)/shard_map/ppermute | solution.py:54
  55.0 1.8 %shard_map.114 = (f32[256,1024]{1,0:T(8,128)S(1)}, bf16[256,1024]{1,0:T(8,128)(2,1)S(1)}, bf16[256,1024]{1,0:T(8,128)(2,1)S(1)}, f32[256,1024]{1,0:T(8,128)S(1)}...) custom-call(bf16[12,128,256]{2,1,0:T(8,128)(2,1)S(1)} %get-tuple-element.69.refs_0_, ...), custom_call_target="tpu_custom_call" | custom-call | flops 1 | bytes 1 | tf_op jit(solution)/shard_map/pallas_call | solution.py:180
  57.9 1.8 %collective-permute-start.13 = (bf16[256,1024]{1,0:T(8,128)(2,1)S(1)}, bf16[256,1024]{1,0:T(8,128)(2,1)S(1)}, u32[]{:S(2)}, u32[]{:S(2)}) collective-permute-start(bf16[256,1024]{1,0:T(8,128)(2,1)S(1)} %get-tuple-element.65), channel_id=1, source_target_pairs={{0,12},{1,13},{2,14},{3,15},{4,0},{5,1},{6,2},{7,3},{8,4},{9,5},{1... | collective-permute-start | bytes 1572872 | tf_op jit(solution)/shard_map/ppermute | solution.py:54
  59.7 2.7 %collective-permute-start.15 = (bf16[256,1024]{1,0:T(8,128)(2,1)S(1)}, bf16[256,1024]{1,0:T(8,128)(2,1)S(1)}, u32[]{:S(2)}, u32[]{:S(2)}) collective-permute-start(bf16[256,1024]{1,0:T(8,128)(2,1)S(1)} %get-tuple-element.68), channel_id=1, source_target_pairs={{0,3},{1,0},{2,1},{3,2},{4,7},{5,4},{6,5},{7,6},{8,11},{9,8},{10,9... | collective-permute-start | bytes 1572872 | tf_op jit(solution)/shard_map/ppermute | solution.py:54
  62.4 4.3 %collective-permute-done.12.refs_1_ = bf16[256,1024]{1,0:T(8,128)(2,1)S(1)} collective-permute-done((bf16[256,1024]{1,0:T(8,128)(2,1)S(1)}, bf16[256,1024]{1,0:T(8,128)(2,1)S(1)}, u32[]{:S(2)}, u32[]{:S(2)}) %collective-permute-start.12) | collective-permute-done | bytes 524320 | tf_op jit(solution)/shard_map/ppermute | solution.py:54
  66.7 2.6 %collective-permute-done.14.refs_4_ = bf16[256,1024]{1,0:T(8,128)(2,1)S(1)} collective-permute-done((bf16[256,1024]{1,0:T(8,128)(2,1)S(1)}, bf16[256,1024]{1,0:T(8,128)(2,1)S(1)}, u32[]{:S(2)}, u32[]{:S(2)}) %collective-permute-start.14) | collective-permute-done | bytes 524320 | tf_op jit(solution)/shard_map/ppermute | solution.py:54
  69.7 8.0 %collective-permute-start.24 = (bf16[2,256,1024]{2,1,0:T(8,128)(2,1)S(1)}, bf16[2,256,1024]{2,1,0:T(8,128)(2,1)S(1)}, u32[]{:S(2)}, u32[]{:S(2)}) collective-permute-start(bf16[2,256,1024]{2,1,0:T(8,128)(2,1)S(1)} %shard_map.115), channel_id=1, source_target_pairs={{0,16},{1,17},{2,18},{3,19},{4,20},{5,21},{6,22},{7,23},{8,24},{9,... | collective-permute-start | bytes 3145736 | tf_op jit(solution)/shard_map/ppermute | solution.py:389
  78.5 2.7 %collective-permute-start.17 = (bf16[128,1024]{1,0:T(8,128)(2,1)S(1)}, bf16[128,1024]{1,0:T(8,128)(2,1)S(1)}, u32[]{:S(2)}, u32[]{:S(2)}) collective-permute-start(bf16[128,1024]{1,0:T(8,128)(2,1)S(1)} %get-tuple-element.80), channel_id=1, source_target_pairs={{0,12},{1,13},{2,14},{3,15},{4,0},{5,1},{6,2},{7,3},{8,4},{9,5},{1... | collective-permute-start | bytes 786440 | tf_op jit(solution)/shard_map/ppermute | solution.py:54
  81.2 2.7 %collective-permute-start.19 = (bf16[128,1024]{1,0:T(8,128)(2,1)S(1)}, bf16[128,1024]{1,0:T(8,128)(2,1)S(1)}, u32[]{:S(2)}, u32[]{:S(2)}) collective-permute-start(bf16[128,1024]{1,0:T(8,128)(2,1)S(1)} %get-tuple-element.82), channel_id=1, source_target_pairs={{0,3},{1,0},{2,1},{3,2},{4,7},{5,4},{6,5},{7,6},{8,11},{9,8},{10,9... | collective-permute-start | bytes 786440 | tf_op jit(solution)/shard_map/ppermute | solution.py:54
  83.8 1.4 collective-permute-done.16.refs_10_
  85.2 2.7 %collective-permute-done.18.refs_12_ = bf16[128,1024]{1,0:T(8,128)(2,1)S(1)} collective-permute-done((bf16[128,1024]{1,0:T(8,128)(2,1)S(1)}, bf16[128,1024]{1,0:T(8,128)(2,1)S(1)}, u32[]{:S(2)}, u32[]{:S(2)}) %collective-permute-start.18) | collective-permute-done | bytes 262176 | tf_op jit(solution)/shard_map/ppermute | solution.py:54
  87.9 2.9 %shard_map.117 = (f32[256,1024]{1,0:T(8,128)S(1)}, bf16[256,1024]{1,0:T(8,128)(2,1)}, bf16[256,1024]{1,0:T(8,128)(2,1)}, f32[256,1024]{1,0:T(8,128)S(1)}, bf16[2...) custom-call(bf16[12,128,256]{2,1,0:T(8,128)(2,1)S(1)} %get-tuple-element.69.refs_0_, ...), custom_call_target="tpu_custom_call" | custom-call | flops 1 | bytes 1 | tf_op jit(solution)/shard_map/pallas_call | solution.py:180
  92.8 2.7 %collective-permute-start.21 = (bf16[256,1024]{1,0:T(8,128)(2,1)}, bf16[256,1024]{1,0:T(8,128)(2,1)}, u32[]{:S(2)}, u32[]{:S(2)}) collective-permute-start(bf16[256,1024]{1,0:T(8,128)(2,1)} %get-tuple-element.85), channel_id=1, source_target_pairs={{0,12},{1,13},{2,14},{3,15},{4,0},{5,1},{6,2},{7,3},{8,4},{9,5},{1... | collective-permute-start | bytes 1572872 | tf_op jit(solution)/shard_map/ppermute | solution.py:54
  96.0 2.1 %collective-permute-start.23 = (bf16[256,1024]{1,0:T(8,128)(2,1)}, bf16[256,1024]{1,0:T(8,128)(2,1)}, u32[]{:S(2)}, u32[]{:S(2)}) collective-permute-start(bf16[256,1024]{1,0:T(8,128)(2,1)} %get-tuple-element.88), channel_id=1, source_target_pairs={{0,3},{1,0},{2,1},{3,2},{4,7},{5,4},{6,5},{7,6},{8,11},{9,8},{10,9... | collective-permute-start | bytes 1572872 | tf_op jit(solution)/shard_map/ppermute | solution.py:54
  98.3 4.2 %collective-permute-done.20.refs_1_ = bf16[256,1024]{1,0:T(8,128)(2,1)} collective-permute-done((bf16[256,1024]{1,0:T(8,128)(2,1)}, bf16[256,1024]{1,0:T(8,128)(2,1)}, u32[]{:S(2)}, u32[]{:S(2)}) %collective-permute-start.20) | collective-permute-done | bytes 524320 | tf_op jit(solution)/shard_map/ppermute | solution.py:54
  102.5 2.8 %collective-permute-done.22.refs_4_ = bf16[256,1024]{1,0:T(8,128)(2,1)} collective-permute-done((bf16[256,1024]{1,0:T(8,128)(2,1)}, bf16[256,1024]{1,0:T(8,128)(2,1)}, u32[]{:S(2)}, u32[]{:S(2)}) %collective-permute-start.22) | collective-permute-done | bytes 524320 | tf_op jit(solution)/shard_map/ppermute | solution.py:54
  105.3 1.2 copy-done.6
  106.5 1.2 copy-done.8
  107.7 1.9 %shard_map.118.own = f32[2,256,1024]{2,1,0:T(8,128)S(1)} custom-call(f32[256,1024]{1,0:T(8,128)S(1)} %copy-done.6, bf16[256,1024]{1,0:T(8,128)(2,1)} %collective-permute-done.20.refs_1_, bf16[256,1024]{1,0:T(8,128)(2,1)} %collective-permute-done.21.refs_2_, f32[256,1024]{1,0:T(8,128)S(1)} %copy-done.8, bf16[256,1024]{1,0:T(8,128)(2,1)} %collective-permute-done.22.refs_4_, ...), custom_call_target="tpu_custom_call" | custom-call | flops 1 | bytes 1 | tf_op jit(solution)/shard_map/pallas_call | solution.py:201
  110.7 2.2 %shard_map.120 = (bf16[128,1024]{1,0:T(8,128)(2,1)S(1)}, bf16[128,1024]{1,0:T(8,128)(2,1)S(1)}) custom-call(s32[5]{0:T(128)S(1)} %stack.23.spot, f32[256,1024]{1,0:T(8,128)S(1)} %copy-done.1, f32[256,1024]{1,0:T(8,128)S(1)} %get-tuple-element.91.weights, f32[256,1024]{1,0:T(8,128)S(1)} %get-tuple-element.89.first, f32[256,1024]{1,0:T(8,128)S(1)} %get-tuple-element.90.second, ...), custom_call_target="tpu_custom_call" | custom-call | flops 1 | bytes 1 | tf_op jit(solution)/shard_map/pallas_call | solution.py:286
  112.9 13.5 %collective-permute-start.25 = (bf16[128,1024]{1,0:T(8,128)(2,1)S(1)}, bf16[128,1024]{1,0:T(8,128)(2,1)S(1)}, u32[]{:S(2)}, u32[]{:S(2)}) collective-permute-start(bf16[128,1024]{1,0:T(8,128)(2,1)S(1)} %get-tuple-element.92), channel_id=1, source_target_pairs={{0,32},{32,0},{64,96},{96,64},{128,160},{160,128},{192,224},{224,1... | collective-permute-start | bytes 786440 | tf_op jit(solution)/shard_map/ppermute | solution.py:394
  126.4 1.2 collective-permute-done.25.got
  128.2 2.3 %collective-permute-start.26 = (bf16[32,1024]{1,0:T(8,128)(2,1)S(1)}, bf16[32,1024]{1,0:T(8,128)(2,1)S(1)}, u32[]{:S(2)}, u32[]{:S(2)}) collective-permute-start(bf16[32,1024]{1,0:T(8,128)(2,1)S(1)} %get-tuple-element.98), channel_id=1, source_target_pairs={{0,64},{32,96},{64,128},{96,160},{128,192},{160,224},{192,0},{224,... | collective-permute-start | bytes 196616 | tf_op jit(solution)/shard_map/ppermute | solution.py:349
  131.2 2.3 %collective-permute-start.28 = (bf16[32,1024]{1,0:T(8,128)(2,1)S(1)}, bf16[32,1024]{1,0:T(8,128)(2,1)S(1)}, u32[]{:S(2)}, u32[]{:S(2)}) collective-permute-start(bf16[32,1024]{1,0:T(8,128)(2,1)S(1)} %get-tuple-element.100), channel_id=1, source_target_pairs={{0,192},{32,224},{64,0},{96,32},{128,64},{160,96},{192,128},{224,1... | collective-permute-start | bytes 196616 | tf_op jit(solution)/shard_map/ppermute | solution.py:349
  133.5 2.5 %collective-permute-done.27.refs_2_ = bf16[32,1024]{1,0:T(8,128)(2,1)S(1)} collective-permute-done((bf16[32,1024]{1,0:T(8,128)(2,1)S(1)}, bf16[32,1024]{1,0:T(8,128)(2,1)S(1)}, u32[]{:S(2)}, u32[]{:S(2)}) %collective-permute-start.27) | collective-permute-done | bytes 65568 | tf_op jit(solution)/shard_map/ppermute | solution.py:349
  136.5 2.0 %collective-permute-start.29 = (bf16[32,1024]{1,0:T(8,128)(2,1)S(1)}, bf16[32,1024]{1,0:T(8,128)(2,1)S(1)}, u32[]{:S(2)}, u32[]{:S(2)}) collective-permute-start(bf16[32,1024]{1,0:T(8,128)(2,1)S(1)} %shard_map.123.refs_0_), channel_id=1, source_target_pairs={{0,64},{32,96},{64,128},{96,160},{128,192},{160,224},{192,0},{224,... | collective-permute-start | bytes 196616 | tf_op jit(solution)/shard_map/ppermute | solution.py:353
  139.0 1.6 %collective-permute-start.31 = (bf16[32,1024]{1,0:T(8,128)(2,1)S(1)}, bf16[32,1024]{1,0:T(8,128)(2,1)S(1)}, u32[]{:S(2)}, u32[]{:S(2)}) collective-permute-start(bf16[32,1024]{1,0:T(8,128)(2,1)S(1)} %shard_map.123.refs_0_), channel_id=1, source_target_pairs={{0,192},{32,224},{64,0},{96,32},{128,64},{160,96},{192,128},{224,1... | collective-permute-start | bytes 196616 | tf_op jit(solution)/shard_map/ppermute | solution.py:353
  140.6 1.8 %shard_map.121 = (f32[1,256,1024]{2,1,0:T(8,128)}, f32[1,256,1024]{2,1,0:T(8,128)}) custom-call(f32[256,1024]{1,0:T(8,128)S(1)} %get-tuple-element.89.first, f32[256,1024]{1,0:T(8,128)S(1)} %get-tuple-element.90.second, f32[2,256,1024]{2,1,0:T(8,128)S(1)} %shard_map.118.own, bf16[2,256,1024]{2,1,0:T(8,128)(2,1)S(1)} %collective-permute-done.24.got), custom_call_target="tpu_custom_call" | custom-call | flops 1 | bytes 1 | tf_op jit(solution)/shard_map/pallas_call | solution.py:306
  142.4 1.3 collective-permute-done.30.refs_2_
  144.2 2.9 %collective-permute-start.32 = (bf16[128,1024]{1,0:T(8,128)(2,1)S(1)}, bf16[128,1024]{1,0:T(8,128)(2,1)S(1)}, u32[]{:S(2)}, u32[]{:S(2)}) collective-permute-start(bf16[128,1024]{1,0:T(8,128)(2,1)S(1)} %shard_map.124), channel_id=1, source_target_pairs={{0,32},{32,0},{64,96},{96,64},{128,160},{160,128},{192,224},{224,1... | collective-permute-start | bytes 786440 | tf_op jit(solution)/shard_map/ppermute | solution.py:355
  148.4 1.6 %multiply_subtract_fusion = (f32[256,1024]{1,0:T(8,128)}, f32[256,1024]{1,0:T(8,128)}) fusion(f32[256,1024]{1,0:T(8,128)S(1)} %copy-done.1, bf16[128,1024]{1,0:T(8,128)(2,1)S(1)} %get-tuple-element.105, bf16[128,1024]{1,0:T(8,128)(2,1)S(1)} %get-tuple-element.104, f32[256,1024]{1,0:T(8,128)S(1)} %copy-done.10), kind=kLoop, calls=%fused_computation | loop fusion | flops 2883584 | bytes 4718592 | tf_op jit(solution)/shard_map/sub | solution.py:399
  (64 shorter events, 15.7 us)
Async XLA Ops:
  0.8 2.2 %copy-start = (bf16[1,2,128,8192]{3,2,1,0:T(8,128)(2,1)S(1)}, bf16[1,2,128,8192]{3,2,1,0:T(8,128)(2,1)}, u32[]{:S(2)}) copy-start(bf16[1,2,128,8192]{3,2,1,0:T(8,128)(2,1)} %features.3) | copy-start | bytes 12582916
  3.0 1.0 copy-start.2
  4.0 0.7 copy-start.9
  5.9 24.5 %collective-permute-start = (bf16[16,128,256]{2,1,0:T(8,128)(2,1)S(1)}, bf16[16,128,256]{2,1,0:T(8,128)(2,1)S(1)}, u32[]{:S(2)}, u32[]{:S(2)}) collective-permute-start(bf16[16,128,256]{2,1,0:T(8,128)(2,1)S(1)} %get-tuple-element.54), channel_id=1, source_target_pairs={{0,1},{1,2},{2,3},{3,0},{4,5},{5,6},{6,7},{7,4},{8,9},{9,10},{10,1... | collective-permute-start | bytes 3145736 | tf_op jit(solution)/shard_map/ppermute | solution.py:54
  8.1 23.9 %collective-permute-start.1 = (bf16[16,128,256]{2,1,0:T(8,128)(2,1)S(1)}, bf16[16,128,256]{2,1,0:T(8,128)(2,1)S(1)}, u32[]{:S(2)}, u32[]{:S(2)}) collective-permute-start(bf16[16,128,256]{2,1,0:T(8,128)(2,1)S(1)} %get-tuple-element.55), channel_id=1, source_target_pairs={{0,3},{1,0},{2,1},{3,2},{4,7},{5,4},{6,5},{7,6},{8,11},{9,8},{10,9... | collective-permute-start | bytes 3145736 | tf_op jit(solution)/shard_map/ppermute | solution.py:54
  10.9 23.1 %collective-permute-start.4 = (bf16[16,128,256]{2,1,0:T(8,128)(2,1)S(1)}, bf16[16,128,256]{2,1,0:T(8,128)(2,1)S(1)}, u32[]{:S(2)}, u32[]{:S(2)}) collective-permute-start(bf16[16,128,256]{2,1,0:T(8,128)(2,1)S(1)} %get-tuple-element.57), channel_id=1, source_target_pairs={{0,4},{1,5},{2,6},{3,7},{4,8},{5,9},{6,10},{7,11},{8,12},{9,13},{1... | collective-permute-start | bytes 3145736 | tf_op jit(solution)/shard_map/ppermute | solution.py:54
  12.2 24.2 %collective-permute-start.5 = (bf16[16,128,256]{2,1,0:T(8,128)(2,1)S(1)}, bf16[16,128,256]{2,1,0:T(8,128)(2,1)S(1)}, u32[]{:S(2)}, u32[]{:S(2)}) collective-permute-start(bf16[16,128,256]{2,1,0:T(8,128)(2,1)S(1)} %get-tuple-element.58), channel_id=1, source_target_pairs={{0,12},{1,13},{2,14},{3,15},{4,0},{5,1},{6,2},{7,3},{8,4},{9,5},{1... | collective-permute-start | bytes 3145736 | tf_op jit(solution)/shard_map/ppermute | solution.py:54
  30.4 9.6 %collective-permute-start.2 = (bf16[6,128,256]{2,1,0:T(8,128)(2,1)S(1)}, bf16[6,128,256]{2,1,0:T(8,128)(2,1)S(1)}, u32[]{:S(2)}, u32[]{:S(2)}) collective-permute-start(bf16[6,128,256]{2,1,0:T(8,128)(2,1)S(1)} %slice.16), channel_id=1, source_target_pairs={{0,1},{1,2},{2,3},{3,0},{4,5},{5,6},{6,7},{7,4},{8,9},{9,10},{10,1... | collective-permute-start | bytes 1179656 | tf_op jit(solution)/shard_map/ppermute | solution.py:54
  32.1 8.7 %collective-permute-start.3 = (bf16[6,128,256]{2,1,0:T(8,128)(2,1)S(1)}, bf16[6,128,256]{2,1,0:T(8,128)(2,1)S(1)}, u32[]{:S(2)}, u32[]{:S(2)}) collective-permute-start(bf16[6,128,256]{2,1,0:T(8,128)(2,1)S(1)} %slice.17), channel_id=1, source_target_pairs={{0,3},{1,0},{2,1},{3,2},{4,7},{5,4},{6,5},{7,6},{8,11},{9,8},{10,9... | collective-permute-start | bytes 1179656 | tf_op jit(solution)/shard_map/ppermute | solution.py:54
  34.0 10.0 %collective-permute-start.6 = (bf16[6,128,256]{2,1,0:T(8,128)(2,1)S(1)}, bf16[6,128,256]{2,1,0:T(8,128)(2,1)S(1)}, u32[]{:S(2)}, u32[]{:S(2)}) collective-permute-start(bf16[6,128,256]{2,1,0:T(8,128)(2,1)S(1)} %slice.18), channel_id=1, source_target_pairs={{0,4},{1,5},{2,6},{3,7},{4,8},{5,9},{6,10},{7,11},{8,12},{9,13},{1... | collective-permute-start | bytes 1179656 | tf_op jit(solution)/shard_map/ppermute | solution.py:54
  36.5 8.4 %collective-permute-start.7 = (bf16[6,128,256]{2,1,0:T(8,128)(2,1)S(1)}, bf16[6,128,256]{2,1,0:T(8,128)(2,1)S(1)}, u32[]{:S(2)}, u32[]{:S(2)}) collective-permute-start(bf16[6,128,256]{2,1,0:T(8,128)(2,1)S(1)} %slice.19), channel_id=1, source_target_pairs={{0,12},{1,13},{2,14},{3,15},{4,0},{5,1},{6,2},{7,3},{8,4},{9,5},{1... | collective-permute-start | bytes 1179656 | tf_op jit(solution)/shard_map/ppermute | solution.py:54
  45.6 6.5 %collective-permute-start.10 = (bf16[128,1024]{1,0:T(8,128)(2,1)S(1)}, bf16[128,1024]{1,0:T(8,128)(2,1)S(1)}, u32[]{:S(2)}, u32[]{:S(2)}) collective-permute-start(bf16[128,1024]{1,0:T(8,128)(2,1)S(1)} %get-tuple-element.61), channel_id=1, source_target_pairs={{0,1},{1,2},{2,3},{3,0},{4,5},{5,6},{6,7},{7,4},{8,9},{9,10},{10,1... | collective-permute-start | bytes 786440 | tf_op jit(solution)/shard_map/ppermute | solution.py:54
  45.7 6.4 %collective-permute-start.11 = (bf16[128,1024]{1,0:T(8,128)(2,1)S(1)}, bf16[128,1024]{1,0:T(8,128)(2,1)S(1)}, u32[]{:S(2)}, u32[]{:S(2)}) collective-permute-start(bf16[128,1024]{1,0:T(8,128)(2,1)S(1)} %get-tuple-element.62), channel_id=1, source_target_pairs={{0,3},{1,0},{2,1},{3,2},{4,7},{5,4},{6,5},{7,6},{8,11},{9,8},{10,9... | collective-permute-start | bytes 786440 | tf_op jit(solution)/shard_map/ppermute | solution.py:54
  48.3 6.7 %collective-permute-start.8 = (bf16[128,1024]{1,0:T(8,128)(2,1)S(1)}, bf16[128,1024]{1,0:T(8,128)(2,1)S(1)}, u32[]{:S(2)}, u32[]{:S(2)}) collective-permute-start(bf16[128,1024]{1,0:T(8,128)(2,1)S(1)} %get-tuple-element.59), channel_id=1, source_target_pairs={{0,4},{1,5},{2,6},{3,7},{4,8},{5,9},{6,10},{7,11},{8,12},{9,13},{1... | collective-permute-start | bytes 786440 | tf_op jit(solution)/shard_map/ppermute | solution.py:54
  49.5 5.5 %collective-permute-start.9 = (bf16[128,1024]{1,0:T(8,128)(2,1)S(1)}, bf16[128,1024]{1,0:T(8,128)(2,1)S(1)}, u32[]{:S(2)}, u32[]{:S(2)}) collective-permute-start(bf16[128,1024]{1,0:T(8,128)(2,1)S(1)} %get-tuple-element.60), channel_id=1, source_target_pairs={{0,12},{1,13},{2,14},{3,15},{4,0},{5,1},{6,2},{7,3},{8,4},{9,5},{1... | collective-permute-start | bytes 786440 | tf_op jit(solution)/shard_map/ppermute | solution.py:54
  56.9 9.8 %collective-permute-start.12 = (bf16[256,1024]{1,0:T(8,128)(2,1)S(1)}, bf16[256,1024]{1,0:T(8,128)(2,1)S(1)}, u32[]{:S(2)}, u32[]{:S(2)}) collective-permute-start(bf16[256,1024]{1,0:T(8,128)(2,1)S(1)} %get-tuple-element.64), channel_id=1, source_target_pairs={{0,4},{1,5},{2,6},{3,7},{4,8},{5,9},{6,10},{7,11},{8,12},{9,13},{1... | collective-permute-start | bytes 1572872 | tf_op jit(solution)/shard_map/ppermute | solution.py:54
  57.9 8.8 %collective-permute-start.13 = (bf16[256,1024]{1,0:T(8,128)(2,1)S(1)}, bf16[256,1024]{1,0:T(8,128)(2,1)S(1)}, u32[]{:S(2)}, u32[]{:S(2)}) collective-permute-start(bf16[256,1024]{1,0:T(8,128)(2,1)S(1)} %get-tuple-element.65), channel_id=1, source_target_pairs={{0,12},{1,13},{2,14},{3,15},{4,0},{5,1},{6,2},{7,3},{8,4},{9,5},{1... | collective-permute-start | bytes 1572872 | tf_op jit(solution)/shard_map/ppermute | solution.py:54
  59.7 9.5 %collective-permute-start.14 = (bf16[256,1024]{1,0:T(8,128)(2,1)S(1)}, bf16[256,1024]{1,0:T(8,128)(2,1)S(1)}, u32[]{:S(2)}, u32[]{:S(2)}) collective-permute-start(bf16[256,1024]{1,0:T(8,128)(2,1)S(1)} %get-tuple-element.67), channel_id=1, source_target_pairs={{0,1},{1,2},{2,3},{3,0},{4,5},{5,6},{6,7},{7,4},{8,9},{9,10},{10,1... | collective-permute-start | bytes 1572872 | tf_op jit(solution)/shard_map/ppermute | solution.py:54
  59.7 9.5 %collective-permute-start.15 = (bf16[256,1024]{1,0:T(8,128)(2,1)S(1)}, bf16[256,1024]{1,0:T(8,128)(2,1)S(1)}, u32[]{:S(2)}, u32[]{:S(2)}) collective-permute-start(bf16[256,1024]{1,0:T(8,128)(2,1)S(1)} %get-tuple-element.68), channel_id=1, source_target_pairs={{0,3},{1,0},{2,1},{3,2},{4,7},{5,4},{6,5},{7,6},{8,11},{9,8},{10,9... | collective-permute-start | bytes 1572872 | tf_op jit(solution)/shard_map/ppermute | solution.py:54
  69.7 40.0 %collective-permute-start.24 = (bf16[2,256,1024]{2,1,0:T(8,128)(2,1)S(1)}, bf16[2,256,1024]{2,1,0:T(8,128)(2,1)S(1)}, u32[]{:S(2)}, u32[]{:S(2)}) collective-permute-start(bf16[2,256,1024]{2,1,0:T(8,128)(2,1)S(1)} %shard_map.115), channel_id=1, source_target_pairs={{0,16},{1,17},{2,18},{3,19},{4,20},{5,21},{6,22},{7,23},{8,24},{9,... | collective-permute-start | bytes 3145736 | tf_op jit(solution)/shard_map/ppermute | solution.py:389
  78.4 6.8 %collective-permute-start.16 = (bf16[128,1024]{1,0:T(8,128)(2,1)S(1)}, bf16[128,1024]{1,0:T(8,128)(2,1)S(1)}, u32[]{:S(2)}, u32[]{:S(2)}) collective-permute-start(bf16[128,1024]{1,0:T(8,128)(2,1)S(1)} %get-tuple-element.79), channel_id=1, source_target_pairs={{0,4},{1,5},{2,6},{3,7},{4,8},{5,9},{6,10},{7,11},{8,12},{9,13},{1... | collective-permute-start | bytes 786440 | tf_op jit(solution)/shard_map/ppermute | solution.py:54
  78.5 6.7 %collective-permute-start.17 = (bf16[128,1024]{1,0:T(8,128)(2,1)S(1)}, bf16[128,1024]{1,0:T(8,128)(2,1)S(1)}, u32[]{:S(2)}, u32[]{:S(2)}) collective-permute-start(bf16[128,1024]{1,0:T(8,128)(2,1)S(1)} %get-tuple-element.80), channel_id=1, source_target_pairs={{0,12},{1,13},{2,14},{3,15},{4,0},{5,1},{6,2},{7,3},{8,4},{9,5},{1... | collective-permute-start | bytes 786440 | tf_op jit(solution)/shard_map/ppermute | solution.py:54
  81.2 6.7 %collective-permute-start.18 = (bf16[128,1024]{1,0:T(8,128)(2,1)S(1)}, bf16[128,1024]{1,0:T(8,128)(2,1)S(1)}, u32[]{:S(2)}, u32[]{:S(2)}) collective-permute-start(bf16[128,1024]{1,0:T(8,128)(2,1)S(1)} %get-tuple-element.81), channel_id=1, source_target_pairs={{0,1},{1,2},{2,3},{3,0},{4,5},{5,6},{6,7},{7,4},{8,9},{9,10},{10,1... | collective-permute-start | bytes 786440 | tf_op jit(solution)/shard_map/ppermute | solution.py:54
  81.2 16.9 %copy-start.11 = (s32[1,256,8]{1,2,0:T(8,128)S(1)}, s32[1,256,8]{1,2,0:T(8,128)}, u32[]{:S(2)}) copy-start(s32[1,256,8]{1,2,0:T(8,128)} %param.15) | copy-start | bytes 24580
  81.2 6.7 %collective-permute-start.19 = (bf16[128,1024]{1,0:T(8,128)(2,1)S(1)}, bf16[128,1024]{1,0:T(8,128)(2,1)S(1)}, u32[]{:S(2)}, u32[]{:S(2)}) collective-permute-start(bf16[128,1024]{1,0:T(8,128)(2,1)S(1)} %get-tuple-element.82), channel_id=1, source_target_pairs={{0,3},{1,0},{2,1},{3,2},{4,7},{5,4},{6,5},{7,6},{8,11},{9,8},{10,9... | collective-permute-start | bytes 786440 | tf_op jit(solution)/shard_map/ppermute | solution.py:54
  90.8 1.0 copy-start.5
  91.8 1.0 copy-start.7
  92.7 16.9 %copy-start.1 = (f32[256,1024]{1,0:T(8,128)S(1)}, f32[256,1024]{1,0:T(8,128)}, u32[]{:S(2)}) copy-start(f32[256,1024]{1,0:T(8,128)} %anchor.3) | copy-start | bytes 3145732
  92.7 9.7 %collective-permute-start.20 = (bf16[256,1024]{1,0:T(8,128)(2,1)}, bf16[256,1024]{1,0:T(8,128)(2,1)}, u32[]{:S(2)}, u32[]{:S(2)}) collective-permute-start(bf16[256,1024]{1,0:T(8,128)(2,1)} %get-tuple-element.84), channel_id=1, source_target_pairs={{0,4},{1,5},{2,6},{3,7},{4,8},{5,9},{6,10},{7,11},{8,12},{9,13},{1... | collective-permute-start | bytes 1572872 | tf_op jit(solution)/shard_map/ppermute | solution.py:54
  92.8 9.7 %collective-permute-start.21 = (bf16[256,1024]{1,0:T(8,128)(2,1)}, bf16[256,1024]{1,0:T(8,128)(2,1)}, u32[]{:S(2)}, u32[]{:S(2)}) collective-permute-start(bf16[256,1024]{1,0:T(8,128)(2,1)} %get-tuple-element.85), channel_id=1, source_target_pairs={{0,12},{1,13},{2,14},{3,15},{4,0},{5,1},{6,2},{7,3},{8,4},{9,5},{1... | collective-permute-start | bytes 1572872 | tf_op jit(solution)/shard_map/ppermute | solution.py:54
  95.4 9.9 %collective-permute-start.22 = (bf16[256,1024]{1,0:T(8,128)(2,1)}, bf16[256,1024]{1,0:T(8,128)(2,1)}, u32[]{:S(2)}, u32[]{:S(2)}) collective-permute-start(bf16[256,1024]{1,0:T(8,128)(2,1)} %get-tuple-element.87), channel_id=1, source_target_pairs={{0,1},{1,2},{2,3},{3,0},{4,5},{5,6},{6,7},{7,4},{8,9},{9,10},{10,1... | collective-permute-start | bytes 1572872 | tf_op jit(solution)/shard_map/ppermute | solution.py:54
  96.0 9.3 %collective-permute-start.23 = (bf16[256,1024]{1,0:T(8,128)(2,1)}, bf16[256,1024]{1,0:T(8,128)(2,1)}, u32[]{:S(2)}, u32[]{:S(2)}) collective-permute-start(bf16[256,1024]{1,0:T(8,128)(2,1)} %get-tuple-element.88), channel_id=1, source_target_pairs={{0,3},{1,0},{2,1},{3,2},{4,7},{5,4},{6,5},{7,6},{8,11},{9,8},{10,9... | collective-permute-start | bytes 1572872 | tf_op jit(solution)/shard_map/ppermute | solution.py:54
  98.2 11.4 %copy-start.3 = (f32[1,256,1024]{2,1,0:T(8,128)S(1)}, f32[1,256,1024]{2,1,0:T(8,128)}, u32[]{:S(2)}) copy-start(f32[1,256,1024]{2,1,0:T(8,128)} %first.1) | copy-start | bytes 3145732
  98.2 11.4 %copy-start.4 = (f32[1,256,1024]{2,1,0:T(8,128)S(1)}, f32[1,256,1024]{2,1,0:T(8,128)}, u32[]{:S(2)}) copy-start(f32[1,256,1024]{2,1,0:T(8,128)} %second.1) | copy-start | bytes 3145732
  105.3 1.2 copy-start.6
  106.5 1.2 copy-start.8
  112.9 35.4 %copy-start.10 = (f32[256,1024]{1,0:T(8,128)S(1)}, f32[256,1024]{1,0:T(8,128)}, u32[]{:S(2)}) copy-start(f32[256,1024]{1,0:T(8,128)} %param.11) | copy-start | bytes 3145732
  112.9 14.6 %collective-permute-start.25 = (bf16[128,1024]{1,0:T(8,128)(2,1)S(1)}, bf16[128,1024]{1,0:T(8,128)(2,1)S(1)}, u32[]{:S(2)}, u32[]{:S(2)}) collective-permute-start(bf16[128,1024]{1,0:T(8,128)(2,1)S(1)} %get-tuple-element.92), channel_id=1, source_target_pairs={{0,32},{32,0},{64,96},{96,64},{128,160},{160,128},{192,224},{224,1... | collective-permute-start | bytes 786440 | tf_op jit(solution)/shard_map/ppermute | solution.py:394
  128.2 5.3 %collective-permute-start.26 = (bf16[32,1024]{1,0:T(8,128)(2,1)S(1)}, bf16[32,1024]{1,0:T(8,128)(2,1)S(1)}, u32[]{:S(2)}, u32[]{:S(2)}) collective-permute-start(bf16[32,1024]{1,0:T(8,128)(2,1)S(1)} %get-tuple-element.98), channel_id=1, source_target_pairs={{0,64},{32,96},{64,128},{96,160},{128,192},{160,224},{192,0},{224,... | collective-permute-start | bytes 196616 | tf_op jit(solution)/shard_map/ppermute | solution.py:349
  130.5 5.5 %collective-permute-start.27 = (bf16[32,1024]{1,0:T(8,128)(2,1)S(1)}, bf16[32,1024]{1,0:T(8,128)(2,1)S(1)}, u32[]{:S(2)}, u32[]{:S(2)}) collective-permute-start(bf16[32,1024]{1,0:T(8,128)(2,1)S(1)} %get-tuple-element.99), channel_id=1, source_target_pairs={{0,128},{32,160},{64,192},{96,224},{128,0},{160,32},{192,64},{224,... | collective-permute-start | bytes 196616 | tf_op jit(solution)/shard_map/ppermute | solution.py:349
  131.2 5.2 %collective-permute-start.28 = (bf16[32,1024]{1,0:T(8,128)(2,1)S(1)}, bf16[32,1024]{1,0:T(8,128)(2,1)S(1)}, u32[]{:S(2)}, u32[]{:S(2)}) collective-permute-start(bf16[32,1024]{1,0:T(8,128)(2,1)S(1)} %get-tuple-element.100), channel_id=1, source_target_pairs={{0,192},{32,224},{64,0},{96,32},{128,64},{160,96},{192,128},{224,1... | collective-permute-start | bytes 196616 | tf_op jit(solution)/shard_map/ppermute | solution.py:349
  136.5 5.9 %collective-permute-start.29 = (bf16[32,1024]{1,0:T(8,128)(2,1)S(1)}, bf16[32,1024]{1,0:T(8,128)(2,1)S(1)}, u32[]{:S(2)}, u32[]{:S(2)}) collective-permute-start(bf16[32,1024]{1,0:T(8,128)(2,1)S(1)} %shard_map.123.refs_0_), channel_id=1, source_target_pairs={{0,64},{32,96},{64,128},{96,160},{128,192},{160,224},{192,0},{224,... | collective-permute-start | bytes 196616 | tf_op jit(solution)/shard_map/ppermute | solution.py:353
  138.4 5.2 %collective-permute-start.30 = (bf16[32,1024]{1,0:T(8,128)(2,1)S(1)}, bf16[32,1024]{1,0:T(8,128)(2,1)S(1)}, u32[]{:S(2)}, u32[]{:S(2)}) collective-permute-start(bf16[32,1024]{1,0:T(8,128)(2,1)S(1)} %shard_map.123.refs_0_), channel_id=1, source_target_pairs={{0,128},{32,160},{64,192},{96,224},{128,0},{160,32},{192,64},{224,... | collective-permute-start | bytes 196616 | tf_op jit(solution)/shard_map/ppermute | solution.py:353
  139.0 4.7 %collective-permute-start.31 = (bf16[32,1024]{1,0:T(8,128)(2,1)S(1)}, bf16[32,1024]{1,0:T(8,128)(2,1)S(1)}, u32[]{:S(2)}, u32[]{:S(2)}) collective-permute-start(bf16[32,1024]{1,0:T(8,128)(2,1)S(1)} %shard_map.123.refs_0_), channel_id=1, source_target_pairs={{0,192},{32,224},{64,0},{96,32},{128,64},{160,96},{192,128},{224,1... | collective-permute-start | bytes 196616 | tf_op jit(solution)/shard_map/ppermute | solution.py:353
  144.2 4.1 %collective-permute-start.32 = (bf16[128,1024]{1,0:T(8,128)(2,1)S(1)}, bf16[128,1024]{1,0:T(8,128)(2,1)S(1)}, u32[]{:S(2)}, u32[]{:S(2)}) collective-permute-start(bf16[128,1024]{1,0:T(8,128)(2,1)S(1)} %shard_map.124), channel_id=1, source_target_pairs={{0,32},{32,0},{64,96},{96,64},{128,160},{160,128},{192,224},{224,1... | collective-permute-start | bytes 786440 | tf_op jit(solution)/shard_map/ppermute | solution.py:355

commit v3 on v0

v3 whole, which is shorter than its diff:
```python
import functools

import jax
import jax.numpy as jnp
from jax import lax
from jax.experimental import pallas as pl
from jax.experimental.pallas import tpu as pltpu
from jax.sharding import PartitionSpec as P

BETA_ONE = 0.9
BETA_TWO = 0.95
EPSILON = 1e-08
INNER_RATE = 0.1
DECAY = 0.1
OUTER_RATE = 0.7
MOMENTUM = 0.9
CODE_LIMIT = 448.0
LOWEST = 13

NZ, NX, NY = 2, 4, 4
PLANE = NX * NY
LINE, CORES = 4, 2
LIMIT = 12 * 1024 * 1024

HBM = pl.BlockSpec(memory_space=pltpu.HBM)
VMEM = pl.BlockSpec(memory_space=pltpu.VMEM)
SMEM = pl.BlockSpec(memory_space=pltpu.SMEM)
PARAMS = pltpu.CompilerParams(vmem_limit_bytes=LIMIT)
SHORT = pl.CostEstimate(flops=1, bytes_accessed=1, transcendentals=0)


def fsdp_shift(dz, dx, dy):
    def at(z, x, y):
        return ((z % NZ) * NX + x % NX) * NY + y % NY

    return [
        (at(z, x, y), at(z + dz, x + dx, y + dy))
        for z in range(NZ)
        for x in range(NX)
        for y in range(NY)
    ]


def along(dim, block, turn):
    shift = (0, turn, 0) if dim == "x" else (0, 0, turn)
    return lax.ppermute(block, "fsdp", fsdp_shift(*shift))


def after(value, earlier):
    return lax.optimization_barrier((value, earlier))[0]


def shape_of(shape, dtype):
    return jax.ShapeDtypeStruct(shape, dtype)


def pack_kernel(dim, step, spot, ids, cotangents, features, own, ahead, back, ahead_late, back_late, *scratch):
    held, words, grads, sems = scratch
    tokens, shard = own.shape[1:]
    part = tokens // 4
    small = [
        pltpu.make_async_copy(ids, words, sems.at[4]),
        pltpu.make_async_copy(cotangents.at[0, step], grads, sems.at[5]),
    ]
    loads = []
    for q in range(4):
        rows = pl.ds(q * part, part)
        loads.append(pltpu.make_async_copy(features.at[0, step, rows], held.at[rows], sems.at[q]))
    for load in small + loads:
        load.start()
    for load in small:
        load.wait()
    live = jnp.sum((words[0, step : step + 1, :] != 0).astype(jnp.int32))
    alive = lax.broadcasted_iota(jnp.int32, (tokens, shard), 0) < live
    for n in range(4):
        block = grads[:, n * shard : (n + 1) * shard]
        block = jnp.where(alive, block, jnp.zeros_like(block))
        own[8 + n] = block
        ahead[4 + (n + 2) % 4] = block
        back[4 + n] = block
    x, y, z = spot[0], spot[1], spot[4]
    places = {}
    for u in range(4):
        for side, (to_ahead, to_back) in enumerate(((ahead, back), (ahead_late, back_late))):
            far = (to_ahead, to_back)[u // 2]
            places[side, 0, u] = own, 4 * side + u
            places[side, 1, u] = to_ahead, u
            places[side, 2, u] = far, far.shape[0] - 2 + u % 2
            places[side, 3, u] = to_back, u
    for q, load in enumerate(loads):
        load.wait()
        rows = slice(q * part, (q + 1) * part)
        for (side, turn, u), (out, slot) in places.items():
            to_x, to_y = (u, turn) if dim == "y" else (turn, u)
            owner = (lax.rem(z + 1 + side, NZ) * NX + lax.rem(x + to_x, NX)) * NY
            owner = owner + lax.rem(y + to_y, NY)
            at = pl.ds(pl.multiple_of(owner * shard, shard), shard)
            out[slot, rows, :] = held[rows, at]


def pack(dim, step, spot, ids, cotangents, features):
    tokens, rows = features.shape[2:]
    shard = rows // (NZ * NX * NY)
    return pl.pallas_call(
        functools.partial(pack_kernel, dim, step),
        in_specs=[SMEM, HBM, HBM, HBM],
        out_specs=[VMEM] * 5,
        out_shape=[shape_of((blocks, tokens, shard), features.dtype) for blocks in (12, 10, 10, 6, 6)],
        scratch_shapes=[
            pltpu.VMEM((tokens, rows), features.dtype),
            pltpu.VMEM(ids.shape, ids.dtype),
            pltpu.VMEM(cotangents.shape[2:], cotangents.dtype),
            pltpu.SemaphoreType.DMA((6,)),
        ],
        cost_estimate=SHORT,
        compiler_params=PARAMS,
    )(spot, ids, cotangents, features)


def products(turn, pieces):
    own, ahead, back = pieces[:3]
    handed = pieces[3:5]
    if len(pieces) == 5:
        left = [own[turn], ahead[turn], back[turn], handed[turn // 2][2 + turn % 2]]
    else:
        late = pieces[5:]
        left = [own[4 + turn], late[0][turn], late[1][turn], late[2 + turn // 2][turn % 2]]
    left = jnp.concatenate(left, axis=0)
    for n in range(4):
        right = [own[8 + n], ahead[4 + (n + 2) % 4], back[4 + n], handed[n // 2][n % 2]]
        yield n, lax.dot_general(
            left,
            jnp.concatenate(right, axis=0),
            (((0,), (0,)), ((), ())),
            preferred_element_type=jnp.float32,
        )


def opposite_kernel(*refs):
    pieces, (low, high) = refs[:-2], refs[-2:]
    shard, half = pieces[0].shape[2], low.shape[0]
    for n, value in products(2, pieces):
        low[:, n * shard : (n + 1) * shard] = value[:half].astype(low.dtype)
        high[:, n * shard : (n + 1) * shard] = value[half:].astype(high.dtype)


def opposite(pieces):
    _, _, shard = pieces[0].shape
    out = shape_of((shard // 2, 4 * shard), pieces[0].dtype)
    return pl.pallas_call(
        opposite_kernel, in_specs=[VMEM] * len(pieces), out_specs=[VMEM] * 2, out_shape=[out] * 2,
        cost_estimate=SHORT, compiler_params=PARAMS,
    )(*pieces)


def nearest_kernel(*refs):
    pieces, (low, high, own, ahead, back) = refs[:-5], refs[-5:]
    shard, half = pieces[0].shape[2], low.shape[0]
    for n, value in products(1, pieces):
        at = slice(n * shard, (n + 1) * shard)
        ahead[:half, at] = (value[:half] + low[:, at].astype(jnp.float32)).astype(ahead.dtype)
        ahead[half:, at] = value[half:].astype(ahead.dtype)
    for n, value in products(3, pieces):
        at = slice(n * shard, (n + 1) * shard)
        back[:half, at] = value[:half].astype(back.dtype)
        back[half:, at] = (value[half:] + high[:, at].astype(jnp.float32)).astype(back.dtype)
    for n, value in products(0, pieces):
        own[:, n * shard : (n + 1) * shard] = value


def nearest(pieces, low, high):
    _, _, shard = pieces[0].shape
    shape = (shard, 4 * shard)
    sent = shape_of(shape, pieces[0].dtype)
    return pl.pallas_call(
        nearest_kernel, in_specs=[VMEM] * (len(pieces) + 2), out_specs=[VMEM] * 3,
        out_shape=[shape_of(shape, jnp.float32), sent, sent],
        cost_estimate=SHORT, compiler_params=PARAMS,
    )(*pieces, low, high)


def total_kernel(*refs):
    ins, out = refs[:-1], refs[-1]

    @pl.loop(0, out.shape[1], step=16)
    def _(r):
        rows = pl.ds(pl.multiple_of(r, 16), 16)
        for step in range(2):
            total = ins[3 * step][rows, :]
            for ref in ins[3 * step + 1 : 3 * step + 3]:
                total = total + ref[rows, :].astype(jnp.float32)
            out[step, rows, :] = total.astype(out.dtype)


def totals(parts, dtype):
    return pl.pallas_call(
        total_kernel, in_specs=[VMEM] * 6, out_specs=VMEM,
        out_shape=shape_of((2,) + parts[0].shape, dtype), cost_estimate=SHORT, compiler_params=PARAMS,
    )(*parts)


def add_kernel(*refs):
    total = refs[0][...].astype(jnp.float32)
    for ref in refs[1:-1]:
        total = total + ref[...].astype(jnp.float32)
    refs[-1][...] = total.astype(refs[-1].dtype)


def add(parts):
    return pl.pallas_call(
        add_kernel, in_specs=[VMEM] * len(parts), out_specs=VMEM,
        out_shape=shape_of(parts[0].shape, parts[0].dtype), cost_estimate=SHORT, compiler_params=PARAMS,
    )(*parts)


def adam_update(weights, first, second, gradient):
    first = BETA_ONE * first + (1.0 - BETA_ONE) * gradient
    second = BETA_TWO * second + (1.0 - BETA_TWO) * gradient * gradient
    weights = weights - INNER_RATE * (first / (jnp.sqrt(second) + EPSILON) + DECAY * weights)
    return weights, first, second


def inner_steps(anchor, first, second, own, got, here):
    weights, one, two = anchor[here], first[(0,) + here], second[(0,) + here]
    for step in range(own.shape[0]):
        at = (step,) + here
        gradient = own[at] + got[at].astype(jnp.float32)
        weights, one, two = adam_update(weights, one, two, gradient)
    return weights, one, two


def code_kernel(turn, spot, anchor, first, second, own, got, scale, out):
    half = out.shape[0]
    base = lax.rem(spot[2] + turn, CORES) * half

    @pl.loop(0, half, step=16)
    def _(r):
        rows = pl.ds(pl.multiple_of(base + r, 16), 16)
        for c in range(0, anchor.shape[1], 256):
            here = (rows, pl.ds(c, 256))
            delta = anchor[here] - inner_steps(anchor, first, second, own, got, here)[0]
            for block in range(2):
                at = c // 128 + block
                power = jnp.broadcast_to(scale[0, rows, at : at + 1], (16, 128))
                ones = jnp.ones_like(power)
                factor = jnp.left_shift(ones, -power).astype(jnp.float32)
                back = jnp.left_shift(ones, power + LOWEST).astype(jnp.float32) * 2.0**-LOWEST
                coded = delta[:, block * 128 : (block + 1) * 128] * factor
                coded = jnp.clip(coded, -CODE_LIMIT, CODE_LIMIT).astype(jnp.bfloat16)
                out[pl.ds(pl.multiple_of(r, 16), 16), pl.ds(at * 128, 128)] = (
                    coded.astype(jnp.float32) * back
                ).astype(jnp.bfloat16)


def code(turn, spot, anchor, first, second, own, got, exponents):
    rows, width = anchor.shape
    return pl.pallas_call(
        functools.partial(code_kernel, turn),
        in_specs=[SMEM] + [VMEM] * 6, out_specs=VMEM,
        out_shape=shape_of((rows // CORES, width), jnp.bfloat16),
        cost_estimate=SHORT, compiler_params=PARAMS,
    )(spot, anchor, first, second, own, got, exponents)


def moment_kernel(anchor, first, second, own, got, new_first, new_second):
    @pl.loop(0, anchor.shape[0], step=16)
    def _(r):
        rows = pl.ds(pl.multiple_of(r, 16), 16)
        for c in range(0, anchor.shape[1], 256):
            here = (rows, pl.ds(c, 256))
            _, one, two = inner_steps(anchor, first, second, own, got, here)
            new_first[(0,) + here] = one
            new_second[(0,) + here] = two


def moments(anchor, first, second, own, got):
    out = shape_of(first.shape, first.dtype)
    return pl.pallas_call(
        moment_kernel, in_specs=[VMEM] * 5, out_specs=[VMEM] * 2, out_shape=[out] * 2,
        cost_estimate=SHORT, compiler_params=PARAMS,
    )(anchor, first, second, own, got)


def pair_kernel(spot, ours, got, keep, send):
    rows = keep.shape[0]
    for turn, out in ((1, send), (0, keep)):
        at = pl.ds(pl.multiple_of(lax.rem(spot[3] + turn, 2) * rows, rows), rows)
        total = ours[at, :].astype(jnp.float32) + got[at, :].astype(jnp.float32)
        out[...] = total.astype(out.dtype)


def pair_sum(spot, ours, got):
    rows, width = ours.shape
    out = shape_of((rows // 2, width), ours.dtype)
    return pl.pallas_call(
        pair_kernel, in_specs=[SMEM, VMEM, VMEM], out_specs=[VMEM] * 2, out_shape=[out] * 2,
        cost_estimate=SHORT, compiler_params=PARAMS,
    )(spot, ours, got)


def join_kernel(spot, ours, got, out):
    rows = ours.shape[0]
    for turn, ref in ((0, ours), (1, got)):
        at = pl.ds(pl.multiple_of(lax.rem(spot[3] + turn, 2) * rows, rows), rows)
        out[at, :] = ref[...]


def join(spot, ours, got):
    rows, width = ours.shape
    return pl.pallas_call(
        join_kernel, in_specs=[SMEM, VMEM, VMEM], out_specs=VMEM,
        out_shape=shape_of((2 * rows, width), ours.dtype), cost_estimate=SHORT, compiler_params=PARAMS,
    )(spot, ours, got)


def swap(block, line, core):
    pairs = [
        (z * CORES + c, (z ^ line) * CORES + (c ^ core)) for z in range(LINE) for c in range(CORES)
    ]
    return lax.ppermute(block, "replica", pairs)


def outer_kernel(turn, spot, total, anchor, momentum, *refs):
    new_weights, new_momentum, weights, moving, sems = refs[-5:]
    rows = total.shape[0]
    base = lax.rem(spot[2] + turn, CORES) * rows
    tile = rows // 4
    stores = []
    for r in range(0, rows, tile):
        here = pl.ds(pl.multiple_of(base + r, tile), tile)
        average = total[r : r + tile, :].astype(jnp.float32) * (1.0 / (LINE * CORES))
        moved = MOMENTUM * momentum[here, :] + average
        moving[r : r + tile, :] = moved
        weights[r : r + tile, :] = anchor[here, :] - OUTER_RATE * (average + MOMENTUM * moved)
        for k, (held, out) in enumerate(((moving, new_momentum), (weights, new_weights))):
            store = pltpu.make_async_copy(
                held.at[pl.ds(r, tile)], out.at[here], sems.at[k, r // tile]
            )
            store.start()
            stores.append(store)
    for store in stores:
        store.wait()


def outer_step(turn, spot, total, anchor, momentum, outs=()):
    rows, width = total.shape
    return pl.pallas_call(
        functools.partial(outer_kernel, turn),
        in_specs=[SMEM] + [VMEM] * 3 + [HBM] * len(outs),
        out_specs=[HBM] * 2,
        out_shape=[shape_of(anchor.shape, anchor.dtype)] * 2,
        scratch_shapes=[
            pltpu.VMEM((rows, width), jnp.float32),
            pltpu.VMEM((rows, width), jnp.float32),
            pltpu.SemaphoreType.DMA((2, 4)),
        ],
        input_output_aliases={4 + k: k for k in range(len(outs))},
        cost_estimate=SHORT,
        compiler_params=PARAMS,
    )(spot, total, anchor, momentum, *outs)


def replica_sum(spot, ours, got, late):
    keep, send = pair_sum(spot, ours, got)
    total = add([keep, swap(send, 1, 0)])
    total = add([after(total, late), swap(total, 2, 0)])
    return join(spot, total, swap(total, 1, 0))


def on_device(
    anchor, first_moment, second_moment, outer_momentum, activations, cotangents, token_ids, exponents
):
    place = lax.axis_index("fsdp").astype(jnp.int32)
    z, x, y = place // PLANE, (place // NY) % NX, place % NY
    copy = lax.axis_index("replica").astype(jnp.int32)
    spot = jnp.stack([x, y, copy % CORES, copy // CORES, z])

    rings = ("y", "x")

    sent = [pack("y", 0, spot, token_ids, cotangents, activations)]
    sent.append(pack("x", 1, spot, token_ids, cotangents, activations))

    def gather(ahead, back, handed):
        ahead = [along(ring, block, 1) for ring, block in zip(rings, ahead)]
        back = [along(ring, block, -1) for ring, block in zip(rings, back)]
        on = [along(ring, block[-handed:], 1) for ring, block in zip(rings, ahead)]
        off = [along(ring, block[-handed:], -1) for ring, block in zip(rings, back)]
        return [[ahead[step], back[step], on[step], off[step]] for step in range(2)]

    def reduce(pieces, dtype):
        parts = []
        for ring, piece in zip(("x", "y"), pieces):
            low, high = opposite(piece)
            own, ahead, back = nearest(piece, along(ring, low, 1), along(ring, high, -1))
            parts += [own, along(ring, ahead, 1), along(ring, back, -1)]
        return totals(parts, dtype)

    soon = gather([block[1] for block in sent], [block[2] for block in sent], 4)
    soon = [[sent[step][0]] + soon[step] for step in range(2)]
    theirs = reduce(soon, jnp.bfloat16)
    got = lax.ppermute(theirs, "fsdp", fsdp_shift(1, 0, 0))
    late = gather([block[3] for block in sent], [block[4] for block in sent], 2)
    own = reduce([soon[step] + late[step] for step in range(2)], jnp.float32)

    state = anchor, first_moment, second_moment, own, got
    other = swap(code(1, spot, *state, exponents), 0, 1)
    keep = code(0, spot, *state, exponents)
    new_first, new_second = moments(*state[:4], after(got, other))
    total = replica_sum(spot, keep, other, new_first)
    other = swap(total, 0, 1)
    outs = outer_step(0, spot, total, anchor, outer_momentum)
    new_weights, new_momentum = outer_step(1, spot, other, anchor, outer_momentum, outs)
    return new_weights, new_momentum, new_first, new_second


def solution(mesh):
    in_specs = (
        P("fsdp", None),
        P("replica", "fsdp", None),
        P("replica", "fsdp", None),
        P("fsdp", None),
        P("replica", None, "fsdp", None),
        P("replica", None, "fsdp", None),
        P("replica", None, "fsdp"),
        P("replica", "fsdp", None),
    )
    out_specs = (
        P("fsdp", None),
        P("fsdp", None),
        P("replica", "fsdp", None),
        P("replica", "fsdp", None),
    )
    return jax.shard_map(
        on_device, mesh=mesh, in_specs=in_specs, out_specs=out_specs, check_vma=False
    )
```

time: 476 us -> 148 us (0.31)
  waiting for transfers between devices: 385 us -> 44.7 us
  starting transfers between devices: 14.9 us -> 67.4 us
  local copies, waits for them, and re-layouts: 38 us -> 8.63 us
  Pallas kernels: 0 us -> 25.4 us
  matrix products: 16.5 us -> 0 us
  between operations: 13.8 us -> 1.17 us
  other arithmetic: 5.12 us -> 0 us
    all_gather x2 -> x0, waiting for transfers between devices: 216 us -> none  [on_device(): lax.all_gather(masked[step], 'fsdp', axis=0, tiled=True)]
    all_to_all x1 -> x0, waiting for transfers between devices: 106 us -> none  [on_device(): lax.all_to_all(activations[0], 'fsdp', split_axis=2, concat_axis=1, tiled...]
    ppermute x0 -> x38, starting transfers between devices: none -> 67.4 us  [the longest x32 45 us: along(): return lax.ppermute(block, 'fsdp', fsdp_shift(*shift))]
    psum x1 -> x0, waiting for transfers between devices: 62.6 us -> none  [on_device(): lax.psum(decoded.astype(jnp.bfloat16), 'replica').astype(jnp.float32)]
    ppermute x0 -> x38, waiting for transfers between devices: none -> 44.7 us  [the longest x32 30.8 us: along(): return lax.ppermute(block, 'fsdp', fsdp_shift(*shift))]
    pallas_call x0 -> x21, Pallas kernels: none -> 25.4 us  [the longest x4 5.3 us: nearest(): pl.pallas_call(nearest_kernel, in_specs=[VMEM] * (len(pieces) + 2), out_s...]
    dot_general x2 -> x0, matrix products: 16.5 us -> none  [contract_tokens(): lax.dot_general(left, right, (((0,), (0,)), ((), ())), preferred_element_...]
    unnamed x17 -> x25, local copies, waits for them, and re-layouts: 24.6 us -> 8.44 us
  transfers between devices with their start and end apart: 4 -> 38, of which waited for: 4 -> 12; matrix products, arithmetic and copies ran while one was open for 8% -> 0% of each run, Pallas kernels for 0% -> 13%
where the time goes in v3:
time: 148 us; the launch traced here: 147 us
  starting transfers between devices  67.4 us (46%)
  waiting for transfers between devices  44.7 us (30%)
  Pallas kernels  25.4 us (17%)
  local copies, waits for them, and re-layouts  8.63 us (6%)
    ppermute x32, starting transfers between devices, along(): return lax.ppermute(block, 'fsdp', fsdp_shift(*shift))  45 us
    ppermute x32, waiting for transfers between devices, along(): return lax.ppermute(block, 'fsdp', fsdp_shift(*shift))  30.8 us
    ppermute x5, starting transfers between devices, swap(): return lax.ppermute(block, 'replica', pairs)  16 us
    ppermute x5, waiting for transfers between devices, swap(): return lax.ppermute(block, 'replica', pairs)  13.9 us
    unnamed x25, local copies, waits for them, and re-layouts  8.44 us
    ppermute x1, starting transfers between devices, on_device(): got = lax.ppermute(theirs, 'fsdp', fsdp_shift(1, 0, 0))  6.36 us
    pallas_call x4, Pallas kernels, nearest(): pl.pallas_call(nearest_kernel, in_specs=[VMEM] * (len(pieces) + 2), out_s...  5.3 us
    pallas_call x2, Pallas kernels, code(): pl.pallas_call(functools.partial(code_kernel, turn), in_specs=[SMEM] + [V...  4.84 us
  transfers between devices with their start and end apart: 38, of which 12 were waited for; matrix products, arithmetic and copies ran while one was open for 0% of the time, Pallas kernels for 13%

profile of v3, /device:TPU:1, one launch (start us, length us, event | category | flops | bytes accessed | tf_op | source)
XLA Modules:
  0.0 147.3 jit_solution(2855848590310700886)
XLA Ops:
  0.8 2.2 %copy-done.1 = bf16[1,2,128,8192]{3,2,1,0:T(8,128)(2,1)S(1)} copy-done((bf16[1,2,128,8192]{3,2,1,0:T(8,128)(2,1)S(1)}, bf16[1,2,128,8192]{3,2,1,0:T(8,128)(2,1)}, u32[]{:S(2)}) %copy-start.1) | copy-done | bytes 4194328
  3.0 1.0 copy-done.5
  4.7 1.2 shard_map.111
  5.9 2.2 %collective-permute-start = (bf16[10,128,256]{2,1,0:T(8,128)(2,1)S(1)}, bf16[10,128,256]{2,1,0:T(8,128)(2,1)S(1)}, u32[]{:S(2)}, u32[]{:S(2)}) collective-permute-start(bf16[10,128,256]{2,1,0:T(8,128)(2,1)S(1)} %get-tuple-element.45), channel_id=1, source_target_pairs={{0,1},{1,2},{2,3},{3,0},{4,5},{5,6},{6,7},{7,4},{8,9},{9,10},{10,1... | collective-permute-start | bytes 1966088 | tf_op jit(solution)/shard_map/ppermute | solution.py:46
  8.1 1.5 %collective-permute-start.1 = (bf16[10,128,256]{2,1,0:T(8,128)(2,1)S(1)}, bf16[10,128,256]{2,1,0:T(8,128)(2,1)S(1)}, u32[]{:S(2)}, u32[]{:S(2)}) collective-permute-start(bf16[10,128,256]{2,1,0:T(8,128)(2,1)S(1)} %get-tuple-element.46), channel_id=1, source_target_pairs={{0,3},{1,0},{2,1},{3,2},{4,7},{5,4},{6,5},{7,6},{8,11},{9,8},{10,9... | collective-permute-start | bytes 1966088 | tf_op jit(solution)/shard_map/ppermute | solution.py:46
  9.7 1.2 shard_map.114
  10.9 1.3 collective-permute-start.12
  12.2 1.5 collective-permute-start.13
  13.7 8.3 %collective-permute-done.refs_1_ = bf16[10,128,256]{2,1,0:T(8,128)(2,1)S(1)} collective-permute-done((bf16[10,128,256]{2,1,0:T(8,128)(2,1)S(1)}, bf16[10,128,256]{2,1,0:T(8,128)(2,1)S(1)}, u32[]{:S(2)}, u32[]{:S(2)}) %collective-permute-start) | collective-permute-done | bytes 655392 | tf_op jit(solution)/shard_map/ppermute | solution.py:46
  22.0 1.6 %collective-permute-start.2 = (bf16[4,128,256]{2,1,0:T(8,128)(2,1)S(1)}, bf16[4,128,256]{2,1,0:T(8,128)(2,1)S(1)}, u32[]{:S(2)}, u32[]{:S(2)}) collective-permute-start(bf16[4,128,256]{2,1,0:T(8,128)(2,1)S(1)} %slice.32), channel_id=1, source_target_pairs={{0,1},{1,2},{2,3},{3,0},{4,5},{5,6},{6,7},{7,4},{8,9},{9,10},{10,1... | collective-permute-start | bytes 786440 | tf_op jit(solution)/shard_map/ppermute | solution.py:46
  23.7 1.7 %collective-permute-start.3 = (bf16[4,128,256]{2,1,0:T(8,128)(2,1)S(1)}, bf16[4,128,256]{2,1,0:T(8,128)(2,1)S(1)}, u32[]{:S(2)}, u32[]{:S(2)}) collective-permute-start(bf16[4,128,256]{2,1,0:T(8,128)(2,1)S(1)} %slice.33), channel_id=1, source_target_pairs={{0,3},{1,0},{2,1},{3,2},{4,7},{5,4},{6,5},{7,6},{8,11},{9,8},{10,9... | collective-permute-start | bytes 786440 | tf_op jit(solution)/shard_map/ppermute | solution.py:46
  25.6 2.4 %collective-permute-start.14 = (bf16[4,128,256]{2,1,0:T(8,128)(2,1)S(1)}, bf16[4,128,256]{2,1,0:T(8,128)(2,1)S(1)}, u32[]{:S(2)}, u32[]{:S(2)}) collective-permute-start(bf16[4,128,256]{2,1,0:T(8,128)(2,1)S(1)} %slice.36), channel_id=1, source_target_pairs={{0,4},{1,5},{2,6},{3,7},{4,8},{5,9},{6,10},{7,11},{8,12},{9,13},{1... | collective-permute-start | bytes 786440 | tf_op jit(solution)/shard_map/ppermute | solution.py:46
  28.0 1.4 collective-permute-start.15
  30.0 3.1 %collective-permute-start.24 = (bf16[128,1024]{1,0:T(8,128)(2,1)S(1)}, bf16[128,1024]{1,0:T(8,128)(2,1)S(1)}, u32[]{:S(2)}, u32[]{:S(2)}) collective-permute-start(bf16[128,1024]{1,0:T(8,128)(2,1)S(1)} %get-tuple-element.64), channel_id=1, source_target_pairs={{0,4},{1,5},{2,6},{3,7},{4,8},{5,9},{6,10},{7,11},{8,12},{9,13},{1... | collective-permute-start | bytes 786440 | tf_op jit(solution)/shard_map/ppermute | solution.py:46
  33.2 1.4 collective-permute-start.25
  35.1 2.7 %collective-permute-start.29 = (bf16[128,1024]{1,0:T(8,128)(2,1)S(1)}, bf16[128,1024]{1,0:T(8,128)(2,1)S(1)}, u32[]{:S(2)}, u32[]{:S(2)}) collective-permute-start(bf16[128,1024]{1,0:T(8,128)(2,1)S(1)} %get-tuple-element.70), channel_id=1, source_target_pairs={{0,3},{1,0},{2,1},{3,2},{4,7},{5,4},{6,5},{7,6},{8,11},{9,8},{10,9... | collective-permute-start | bytes 786440 | tf_op jit(solution)/shard_map/ppermute | solution.py:46
  37.8 2.8 %collective-permute-done.24.refs_5_ = bf16[128,1024]{1,0:T(8,128)(2,1)S(1)} collective-permute-done((bf16[128,1024]{1,0:T(8,128)(2,1)S(1)}, bf16[128,1024]{1,0:T(8,128)(2,1)S(1)}, u32[]{:S(2)}, u32[]{:S(2)}) %collective-permute-start.24) | collective-permute-done | bytes 262176 | tf_op jit(solution)/shard_map/ppermute | solution.py:46
  40.6 1.0 shard_map.119
  41.8 3.1 %collective-permute-start.27 = (bf16[256,1024]{1,0:T(8,128)(2,1)S(1)}, bf16[256,1024]{1,0:T(8,128)(2,1)S(1)}, u32[]{:S(2)}, u32[]{:S(2)}) collective-permute-start(bf16[256,1024]{1,0:T(8,128)(2,1)S(1)} %get-tuple-element.68), channel_id=1, source_target_pairs={{0,12},{1,13},{2,14},{3,15},{4,0},{5,1},{6,2},{7,3},{8,4},{9,5},{1... | collective-permute-start | bytes 1572872 | tf_op jit(solution)/shard_map/ppermute | solution.py:46
  45.0 1.0 shard_map.121
  46.1 2.7 %collective-permute-start.31 = (bf16[256,1024]{1,0:T(8,128)(2,1)S(1)}, bf16[256,1024]{1,0:T(8,128)(2,1)S(1)}, u32[]{:S(2)}, u32[]{:S(2)}) collective-permute-start(bf16[256,1024]{1,0:T(8,128)(2,1)S(1)} %get-tuple-element.73), channel_id=1, source_target_pairs={{0,3},{1,0},{2,1},{3,2},{4,7},{5,4},{6,5},{7,6},{8,11},{9,8},{10,9... | collective-permute-start | bytes 1572872 | tf_op jit(solution)/shard_map/ppermute | solution.py:46
  48.8 6.3 %collective-permute-done.26.refs_1_ = bf16[256,1024]{1,0:T(8,128)(2,1)S(1)} collective-permute-done((bf16[256,1024]{1,0:T(8,128)(2,1)S(1)}, bf16[256,1024]{1,0:T(8,128)(2,1)S(1)}, u32[]{:S(2)}, u32[]{:S(2)}) %collective-permute-start.26) | collective-permute-done | bytes 524320 | tf_op jit(solution)/shard_map/ppermute | solution.py:46
  55.6 2.7 %collective-permute-done.30.refs_4_ = bf16[256,1024]{1,0:T(8,128)(2,1)S(1)} collective-permute-done((bf16[256,1024]{1,0:T(8,128)(2,1)S(1)}, bf16[256,1024]{1,0:T(8,128)(2,1)S(1)}, u32[]{:S(2)}, u32[]{:S(2)}) %collective-permute-start.30) | collective-permute-done | bytes 524320 | tf_op jit(solution)/shard_map/ppermute | solution.py:46
  59.1 1.4 shard_map.122
  60.5 6.4 %collective-permute-start.32 = (bf16[2,256,1024]{2,1,0:T(8,128)(2,1)}, bf16[2,256,1024]{2,1,0:T(8,128)(2,1)}, u32[]{:S(2)}, u32[]{:S(2)}) collective-permute-start(bf16[2,256,1024]{2,1,0:T(8,128)(2,1)} %shard_map.122), channel_id=1, source_target_pairs={{0,16},{1,17},{2,18},{3,19},{4,20},{5,21},{6,22},{7,23},{8,24},{9,... | collective-permute-start | bytes 3145736 | tf_op jit(solution)/shard_map/ppermute | solution.py:401
  67.0 2.7 %collective-permute-start.7 = (bf16[2,128,256]{2,1,0:T(8,128)(2,1)S(1)}, bf16[2,128,256]{2,1,0:T(8,128)(2,1)S(1)}, u32[]{:S(2)}, u32[]{:S(2)}) collective-permute-start(bf16[2,128,256]{2,1,0:T(8,128)(2,1)S(1)} %slice.35), channel_id=1, source_target_pairs={{0,3},{1,0},{2,1},{3,2},{4,7},{5,4},{6,5},{7,6},{8,11},{9,8},{10,9... | collective-permute-start | bytes 393224 | tf_op jit(solution)/shard_map/ppermute | solution.py:46
  70.4 2.1 %collective-permute-start.19 = (bf16[2,128,256]{2,1,0:T(8,128)(2,1)S(1)}, bf16[2,128,256]{2,1,0:T(8,128)(2,1)S(1)}, u32[]{:S(2)}, u32[]{:S(2)}) collective-permute-start(bf16[2,128,256]{2,1,0:T(8,128)(2,1)S(1)} %slice.39), channel_id=1, source_target_pairs={{0,12},{1,13},{2,14},{3,15},{4,0},{5,1},{6,2},{7,3},{8,4},{9,5},{1... | collective-permute-start | bytes 393224 | tf_op jit(solution)/shard_map/ppermute | solution.py:46
  73.1 2.7 %collective-permute-start.9 = (bf16[128,1024]{1,0:T(8,128)(2,1)S(1)}, bf16[128,1024]{1,0:T(8,128)(2,1)S(1)}, u32[]{:S(2)}, u32[]{:S(2)}) collective-permute-start(bf16[128,1024]{1,0:T(8,128)(2,1)S(1)} %get-tuple-element.50), channel_id=1, source_target_pairs={{0,12},{1,13},{2,14},{3,15},{4,0},{5,1},{6,2},{7,3},{8,4},{9,5},{1... | collective-permute-start | bytes 786440 | tf_op jit(solution)/shard_map/ppermute | solution.py:46
  76.6 2.7 %collective-permute-start.21 = (bf16[128,1024]{1,0:T(8,128)(2,1)S(1)}, bf16[128,1024]{1,0:T(8,128)(2,1)S(1)}, u32[]{:S(2)}, u32[]{:S(2)}) collective-permute-start(bf16[128,1024]{1,0:T(8,128)(2,1)S(1)} %get-tuple-element.60), channel_id=1, source_target_pairs={{0,3},{1,0},{2,1},{3,2},{4,7},{5,4},{6,5},{7,6},{8,11},{9,8},{10,9... | collective-permute-start | bytes 786440 | tf_op jit(solution)/shard_map/ppermute | solution.py:46
  79.9 1.6 %shard_map.113 = (f32[256,1024]{1,0:T(8,128)S(1)}, bf16[256,1024]{1,0:T(8,128)(2,1)}, bf16[256,1024]{1,0:T(8,128)(2,1)}) custom-call(bf16[12,128,256]{2,1,0:T(8,128)(2,1)S(1)} %get-tuple-element.44.refs_0_, bf16[10,128,256]{2,1,0:T(8,128)(2,1)S(1)} %collective-permute-done.refs_1_, bf16[10,128,256]{2,1,0:T(8,128)(2,1)S(1)} %collective-permute-done.1.refs_2_, ...), custom_call_target="tpu_custom_call" | custom-call | flops 1 | bytes 1 | tf_op jit(solution)/shard_map/pallas_call | solution.py:175
  82.5 2.7 %collective-permute-start.11 = (bf16[256,1024]{1,0:T(8,128)(2,1)}, bf16[256,1024]{1,0:T(8,128)(2,1)}, u32[]{:S(2)}, u32[]{:S(2)}) collective-permute-start(bf16[256,1024]{1,0:T(8,128)(2,1)} %get-tuple-element.53), channel_id=1, source_target_pairs={{0,12},{1,13},{2,14},{3,15},{4,0},{5,1},{6,2},{7,3},{8,4},{9,5},{1... | collective-permute-start | bytes 1572872 | tf_op jit(solution)/shard_map/ppermute | solution.py:46
  85.2 1.7 %shard_map.116 = (f32[256,1024]{1,0:T(8,128)S(1)}, bf16[256,1024]{1,0:T(8,128)(2,1)}, bf16[256,1024]{1,0:T(8,128)(2,1)}) custom-call(bf16[12,128,256]{2,1,0:T(8,128)(2,1)S(1)} %get-tuple-element.54.refs_0_, bf16[10,128,256]{2,1,0:T(8,128)(2,1)S(1)} %collective-permute-done.12.refs_1_, bf16[10,128,256]{2,1,0:T(8,128)(2,1)S(1)} %collective-permute-done.13.refs_2_, ...), custom_call_target="tpu_custom_call" | custom-call | flops 1 | bytes 1 | tf_op jit(solution)/shard_map/pallas_call | solution.py:175
  87.8 2.7 %collective-permute-start.23 = (bf16[256,1024]{1,0:T(8,128)(2,1)}, bf16[256,1024]{1,0:T(8,128)(2,1)}, u32[]{:S(2)}, u32[]{:S(2)}) collective-permute-start(bf16[256,1024]{1,0:T(8,128)(2,1)} %get-tuple-element.63), channel_id=1, source_target_pairs={{0,3},{1,0},{2,1},{3,2},{4,7},{5,4},{6,5},{7,6},{8,11},{9,8},{10,9... | collective-permute-start | bytes 1572872 | tf_op jit(solution)/shard_map/ppermute | solution.py:46
  90.6 4.5 %collective-permute-done.10.refs_1_ = bf16[256,1024]{1,0:T(8,128)(2,1)} collective-permute-done((bf16[256,1024]{1,0:T(8,128)(2,1)}, bf16[256,1024]{1,0:T(8,128)(2,1)}, u32[]{:S(2)}, u32[]{:S(2)}) %collective-permute-start.10) | collective-permute-done | bytes 524320 | tf_op jit(solution)/shard_map/ppermute | solution.py:46
  95.2 5.0 %collective-permute-done.22.refs_4_ = bf16[256,1024]{1,0:T(8,128)(2,1)} collective-permute-done((bf16[256,1024]{1,0:T(8,128)(2,1)}, bf16[256,1024]{1,0:T(8,128)(2,1)}, u32[]{:S(2)}, u32[]{:S(2)}) %collective-permute-start.22) | collective-permute-done | bytes 524320 | tf_op jit(solution)/shard_map/ppermute | solution.py:46
  100.2 1.2 copy-done.7
  101.4 1.2 copy-done.9
  102.6 1.9 %shard_map.117.own = f32[2,256,1024]{2,1,0:T(8,128)S(1)} custom-call(f32[256,1024]{1,0:T(8,128)S(1)} %copy-done.7, bf16[256,1024]{1,0:T(8,128)(2,1)} %collective-permute-done.10.refs_1_, bf16[256,1024]{1,0:T(8,128)(2,1)} %collective-permute-done.11.refs_2_, f32[256,1024]{1,0:T(8,128)S(1)} %copy-done.9, bf16[256,1024]{1,0:T(8,128)(2,1)} %collective-permute-done.22.refs_4_, ...), custom_call_target="tpu_custom_call" | custom-call | flops 1 | bytes 1 | tf_op jit(solution)/shard_map/pallas_call | solution.py:196
  104.5 2.4 %shard_map.124 = bf16[128,1024]{1,0:T(8,128)(2,1)S(1)} custom-call(s32[5]{0:T(128)S(1)} %stack.23.spot, f32[256,1024]{1,0:T(8,128)S(1)} %copy-done, f32[1,256,1024]{2,1,0:T(8,128)S(1)} %copy-done.2, f32[1,256,1024]{2,1,0:T(8,128)S(1)} %copy-done.3, f32[2,256,1024]{2,1,0:T(8,128)S(1)} %shard_map.117.own, bf16[2,256,1024]{2,1,0:T(8,128)(2,1)} %collective-permute-done.32.got, ...), custom_call_target="tpu_custom_call" | custom-call | flops 1 | bytes 1 | tf_op jit(solution)/shard_map/pallas_call | solution.py:257
  107.0 13.1 %collective-permute-start.33 = (bf16[128,1024]{1,0:T(8,128)(2,1)S(1)}, bf16[128,1024]{1,0:T(8,128)(2,1)S(1)}, u32[]{:S(2)}, u32[]{:S(2)}) collective-permute-start(bf16[128,1024]{1,0:T(8,128)(2,1)S(1)} %shard_map.124), channel_id=1, source_target_pairs={{0,32},{32,0},{64,96},{96,64},{128,160},{160,128},{192,224},{224,1... | collective-permute-start | bytes 786440 | tf_op jit(solution)/shard_map/ppermute | solution.py:320
  120.0 2.4 %shard_map.123.ours = bf16[128,1024]{1,0:T(8,128)(2,1)S(1)} custom-call(s32[5]{0:T(128)S(1)} %stack.23.spot, f32[256,1024]{1,0:T(8,128)S(1)} %copy-done, f32[1,256,1024]{2,1,0:T(8,128)S(1)} %copy-done.2, f32[1,256,1024]{2,1,0:T(8,128)S(1)} %copy-done.3, f32[2,256,1024]{2,1,0:T(8,128)S(1)} %shard_map.117.own, ...), custom_call_target="tpu_custom_call" | custom-call | flops 1 | bytes 1 | tf_op jit(solution)/shard_map/pallas_call | solution.py:257
  123.8 4.5 %collective-permute-done.34.refs_1_ = bf16[64,1024]{1,0:T(8,128)(2,1)S(1)} collective-permute-done((bf16[64,1024]{1,0:T(8,128)(2,1)S(1)}, bf16[64,1024]{1,0:T(8,128)(2,1)S(1)}, u32[]{:S(2)}, u32[]{:S(2)}) %collective-permute-start.34) | collective-permute-done | bytes 131104 | tf_op jit(solution)/shard_map/ppermute | solution.py:320
  128.6 3.3 %shard_map.127 = (f32[1,256,1024]{2,1,0:T(8,128)}, f32[1,256,1024]{2,1,0:T(8,128)}) custom-call(f32[256,1024]{1,0:T(8,128)S(1)} %copy-done, f32[1,256,1024]{2,1,0:T(8,128)S(1)} %copy-done.2, f32[1,256,1024]{2,1,0:T(8,128)S(1)} %copy-done.3, f32[2,256,1024]{2,1,0:T(8,128)S(1)} %shard_map.117.own, bf16[2,256,1024]{2,1,0:T(8,128)(2,1)} %collective-permute-done.32.got), custom_call_target="tpu_custom_call" | custom-call | flops 1 | bytes 1 | tf_op jit(solution)/shard_map/pallas_call | solution.py:278
  131.9 5.3 %collective-permute-done.35.refs_1_ = bf16[64,1024]{1,0:T(8,128)(2,1)S(1)} collective-permute-done((bf16[64,1024]{1,0:T(8,128)(2,1)S(1)}, bf16[64,1024]{1,0:T(8,128)(2,1)S(1)}, u32[]{:S(2)}, u32[]{:S(2)}) %collective-permute-start.35) | collective-permute-done | bytes 131104 | tf_op jit(solution)/shard_map/ppermute | solution.py:320
  137.3 4.1 %collective-permute-done.36.got = bf16[64,1024]{1,0:T(8,128)(2,1)S(1)} collective-permute-done((bf16[64,1024]{1,0:T(8,128)(2,1)S(1)}, bf16[64,1024]{1,0:T(8,128)(2,1)S(1)}, u32[]{:S(2)}, u32[]{:S(2)}) %collective-permute-start.36) | collective-permute-done | bytes 131104 | tf_op jit(solution)/shard_map/ppermute | solution.py:320
  142.0 1.9 %collective-permute-start.37 = (bf16[128,1024]{1,0:T(8,128)(2,1)S(1)}, bf16[128,1024]{1,0:T(8,128)(2,1)S(1)}, u32[]{:S(2)}, u32[]{:S(2)}) collective-permute-start(bf16[128,1024]{1,0:T(8,128)(2,1)S(1)} %shard_map.129.total), channel_id=1, source_target_pairs={{0,32},{32,0},{64,96},{96,64},{128,160},{160,128},{192,224},{224,1... | collective-permute-start | bytes 786440 | tf_op jit(solution)/shard_map/ppermute | solution.py:320
  143.9 1.6 %shard_map.130 = (f32[256,1024]{1,0:T(8,128)}, f32[256,1024]{1,0:T(8,128)}) custom-call(s32[5]{0:T(128)S(1)} %stack.23.spot, bf16[128,1024]{1,0:T(8,128)(2,1)S(1)} %shard_map.129.total, f32[256,1024]{1,0:T(8,128)S(1)} %copy-done, f32[256,1024]{1,0:T(8,128)S(1)} %copy-done.4), custom_call_target="tpu_custom_call" | custom-call | flops 1 | bytes 1 | tf_op jit(solution)/shard_map/pallas_call | solution.py:347
  145.5 1.6 %shard_map.131 = (f32[256,1024]{1,0:T(8,128)}, f32[256,1024]{1,0:T(8,128)}) custom-call(s32[5]{0:T(128)S(1)} %stack.23.spot, bf16[128,1024]{1,0:T(8,128)(2,1)S(1)} %collective-permute-done.37.total, f32[256,1024]{1,0:T(8,128)S(1)} %copy-done, f32[256,1024]{1,0:T(8,128)S(1)} %copy-done.4, ...), custom_call_target="tpu_custom_call", output_to_operand_aliasing={{0}: (4, {}), {1}: (5, {})} | custom-call | flops 1 | bytes 1 | tf_op jit(solution)/shard_map/pallas_call | solution.py:347
  (83 shorter events, 11.2 us)
Async XLA Ops:
  0.8 2.2 %copy-start.1 = (bf16[1,2,128,8192]{3,2,1,0:T(8,128)(2,1)S(1)}, bf16[1,2,128,8192]{3,2,1,0:T(8,128)(2,1)}, u32[]{:S(2)}) copy-start(bf16[1,2,128,8192]{3,2,1,0:T(8,128)(2,1)} %features.3) | copy-start | bytes 12582916
  3.0 1.0 copy-start.5
  5.9 16.1 %collective-permute-start = (bf16[10,128,256]{2,1,0:T(8,128)(2,1)S(1)}, bf16[10,128,256]{2,1,0:T(8,128)(2,1)S(1)}, u32[]{:S(2)}, u32[]{:S(2)}) collective-permute-start(bf16[10,128,256]{2,1,0:T(8,128)(2,1)S(1)} %get-tuple-element.45), channel_id=1, source_target_pairs={{0,1},{1,2},{2,3},{3,0},{4,5},{5,6},{6,7},{7,4},{8,9},{9,10},{10,1... | collective-permute-start | bytes 1966088 | tf_op jit(solution)/shard_map/ppermute | solution.py:46
  8.1 15.5 %collective-permute-start.1 = (bf16[10,128,256]{2,1,0:T(8,128)(2,1)S(1)}, bf16[10,128,256]{2,1,0:T(8,128)(2,1)S(1)}, u32[]{:S(2)}, u32[]{:S(2)}) collective-permute-start(bf16[10,128,256]{2,1,0:T(8,128)(2,1)S(1)} %get-tuple-element.46), channel_id=1, source_target_pairs={{0,3},{1,0},{2,1},{3,2},{4,7},{5,4},{6,5},{7,6},{8,11},{9,8},{10,9... | collective-permute-start | bytes 1966088 | tf_op jit(solution)/shard_map/ppermute | solution.py:46
  10.9 14.7 %collective-permute-start.12 = (bf16[10,128,256]{2,1,0:T(8,128)(2,1)S(1)}, bf16[10,128,256]{2,1,0:T(8,128)(2,1)S(1)}, u32[]{:S(2)}, u32[]{:S(2)}) collective-permute-start(bf16[10,128,256]{2,1,0:T(8,128)(2,1)S(1)} %get-tuple-element.55), channel_id=1, source_target_pairs={{0,4},{1,5},{2,6},{3,7},{4,8},{5,9},{6,10},{7,11},{8,12},{9,13},{1... | collective-permute-start | bytes 1966088 | tf_op jit(solution)/shard_map/ppermute | solution.py:46
  12.2 15.8 %collective-permute-start.13 = (bf16[10,128,256]{2,1,0:T(8,128)(2,1)S(1)}, bf16[10,128,256]{2,1,0:T(8,128)(2,1)S(1)}, u32[]{:S(2)}, u32[]{:S(2)}) collective-permute-start(bf16[10,128,256]{2,1,0:T(8,128)(2,1)S(1)} %get-tuple-element.56), channel_id=1, source_target_pairs={{0,12},{1,13},{2,14},{3,15},{4,0},{5,1},{6,2},{7,3},{8,4},{9,5},{1... | collective-permute-start | bytes 1966088 | tf_op jit(solution)/shard_map/ppermute | solution.py:46
  22.0 7.4 %collective-permute-start.2 = (bf16[4,128,256]{2,1,0:T(8,128)(2,1)S(1)}, bf16[4,128,256]{2,1,0:T(8,128)(2,1)S(1)}, u32[]{:S(2)}, u32[]{:S(2)}) collective-permute-start(bf16[4,128,256]{2,1,0:T(8,128)(2,1)S(1)} %slice.32), channel_id=1, source_target_pairs={{0,1},{1,2},{2,3},{3,0},{4,5},{5,6},{6,7},{7,4},{8,9},{9,10},{10,1... | collective-permute-start | bytes 786440 | tf_op jit(solution)/shard_map/ppermute | solution.py:46
  23.7 5.9 %collective-permute-start.3 = (bf16[4,128,256]{2,1,0:T(8,128)(2,1)S(1)}, bf16[4,128,256]{2,1,0:T(8,128)(2,1)S(1)}, u32[]{:S(2)}, u32[]{:S(2)}) collective-permute-start(bf16[4,128,256]{2,1,0:T(8,128)(2,1)S(1)} %slice.33), channel_id=1, source_target_pairs={{0,3},{1,0},{2,1},{3,2},{4,7},{5,4},{6,5},{7,6},{8,11},{9,8},{10,9... | collective-permute-start | bytes 786440 | tf_op jit(solution)/shard_map/ppermute | solution.py:46
  25.6 8.9 %collective-permute-start.14 = (bf16[4,128,256]{2,1,0:T(8,128)(2,1)S(1)}, bf16[4,128,256]{2,1,0:T(8,128)(2,1)S(1)}, u32[]{:S(2)}, u32[]{:S(2)}) collective-permute-start(bf16[4,128,256]{2,1,0:T(8,128)(2,1)S(1)} %slice.36), channel_id=1, source_target_pairs={{0,4},{1,5},{2,6},{3,7},{4,8},{5,9},{6,10},{7,11},{8,12},{9,13},{1... | collective-permute-start | bytes 786440 | tf_op jit(solution)/shard_map/ppermute | solution.py:46
  28.0 6.5 %collective-permute-start.15 = (bf16[4,128,256]{2,1,0:T(8,128)(2,1)S(1)}, bf16[4,128,256]{2,1,0:T(8,128)(2,1)S(1)}, u32[]{:S(2)}, u32[]{:S(2)}) collective-permute-start(bf16[4,128,256]{2,1,0:T(8,128)(2,1)S(1)} %slice.37), channel_id=1, source_target_pairs={{0,12},{1,13},{2,14},{3,15},{4,0},{5,1},{6,2},{7,3},{8,4},{9,5},{1... | collective-permute-start | bytes 786440 | tf_op jit(solution)/shard_map/ppermute | solution.py:46
  30.0 10.5 %collective-permute-start.24 = (bf16[128,1024]{1,0:T(8,128)(2,1)S(1)}, bf16[128,1024]{1,0:T(8,128)(2,1)S(1)}, u32[]{:S(2)}, u32[]{:S(2)}) collective-permute-start(bf16[128,1024]{1,0:T(8,128)(2,1)S(1)} %get-tuple-element.64), channel_id=1, source_target_pairs={{0,4},{1,5},{2,6},{3,7},{4,8},{5,9},{6,10},{7,11},{8,12},{9,13},{1... | collective-permute-start | bytes 786440 | tf_op jit(solution)/shard_map/ppermute | solution.py:46
  33.2 7.4 %collective-permute-start.25 = (bf16[128,1024]{1,0:T(8,128)(2,1)S(1)}, bf16[128,1024]{1,0:T(8,128)(2,1)S(1)}, u32[]{:S(2)}, u32[]{:S(2)}) collective-permute-start(bf16[128,1024]{1,0:T(8,128)(2,1)S(1)} %get-tuple-element.65), channel_id=1, source_target_pairs={{0,12},{1,13},{2,14},{3,15},{4,0},{5,1},{6,2},{7,3},{8,4},{9,5},{1... | collective-permute-start | bytes 786440 | tf_op jit(solution)/shard_map/ppermute | solution.py:46
  35.0 10.0 %collective-permute-start.28 = (bf16[128,1024]{1,0:T(8,128)(2,1)S(1)}, bf16[128,1024]{1,0:T(8,128)(2,1)S(1)}, u32[]{:S(2)}, u32[]{:S(2)}) collective-permute-start(bf16[128,1024]{1,0:T(8,128)(2,1)S(1)} %get-tuple-element.69), channel_id=1, source_target_pairs={{0,1},{1,2},{2,3},{3,0},{4,5},{5,6},{6,7},{7,4},{8,9},{9,10},{10,1... | collective-permute-start | bytes 786440 | tf_op jit(solution)/shard_map/ppermute | solution.py:46
  35.1 9.9 %collective-permute-start.29 = (bf16[128,1024]{1,0:T(8,128)(2,1)S(1)}, bf16[128,1024]{1,0:T(8,128)(2,1)S(1)}, u32[]{:S(2)}, u32[]{:S(2)}) collective-permute-start(bf16[128,1024]{1,0:T(8,128)(2,1)S(1)} %get-tuple-element.70), channel_id=1, source_target_pairs={{0,3},{1,0},{2,1},{3,2},{4,7},{5,4},{6,5},{7,6},{8,11},{9,8},{10,9... | collective-permute-start | bytes 786440 | tf_op jit(solution)/shard_map/ppermute | solution.py:46
  41.6 13.5 %collective-permute-start.26 = (bf16[256,1024]{1,0:T(8,128)(2,1)S(1)}, bf16[256,1024]{1,0:T(8,128)(2,1)S(1)}, u32[]{:S(2)}, u32[]{:S(2)}) collective-permute-start(bf16[256,1024]{1,0:T(8,128)(2,1)S(1)} %get-tuple-element.67), channel_id=1, source_target_pairs={{0,4},{1,5},{2,6},{3,7},{4,8},{5,9},{6,10},{7,11},{8,12},{9,13},{1... | collective-permute-start | bytes 1572872 | tf_op jit(solution)/shard_map/ppermute | solution.py:46
  41.8 13.2 %collective-permute-start.27 = (bf16[256,1024]{1,0:T(8,128)(2,1)S(1)}, bf16[256,1024]{1,0:T(8,128)(2,1)S(1)}, u32[]{:S(2)}, u32[]{:S(2)}) collective-permute-start(bf16[256,1024]{1,0:T(8,128)(2,1)S(1)} %get-tuple-element.68), channel_id=1, source_target_pairs={{0,12},{1,13},{2,14},{3,15},{4,0},{5,1},{6,2},{7,3},{8,4},{9,5},{1... | collective-permute-start | bytes 1572872 | tf_op jit(solution)/shard_map/ppermute | solution.py:46
  46.0 12.3 %collective-permute-start.30 = (bf16[256,1024]{1,0:T(8,128)(2,1)S(1)}, bf16[256,1024]{1,0:T(8,128)(2,1)S(1)}, u32[]{:S(2)}, u32[]{:S(2)}) collective-permute-start(bf16[256,1024]{1,0:T(8,128)(2,1)S(1)} %get-tuple-element.72), channel_id=1, source_target_pairs={{0,1},{1,2},{2,3},{3,0},{4,5},{5,6},{6,7},{7,4},{8,9},{9,10},{10,1... | collective-permute-start | bytes 1572872 | tf_op jit(solution)/shard_map/ppermute | solution.py:46
  46.1 13.0 %collective-permute-start.31 = (bf16[256,1024]{1,0:T(8,128)(2,1)S(1)}, bf16[256,1024]{1,0:T(8,128)(2,1)S(1)}, u32[]{:S(2)}, u32[]{:S(2)}) collective-permute-start(bf16[256,1024]{1,0:T(8,128)(2,1)S(1)} %get-tuple-element.73), channel_id=1, source_target_pairs={{0,3},{1,0},{2,1},{3,2},{4,7},{5,4},{6,5},{7,6},{8,11},{9,8},{10,9... | collective-permute-start | bytes 1572872 | tf_op jit(solution)/shard_map/ppermute | solution.py:46
  48.8 18.0 %collective-permute-start.4 = (bf16[6,128,256]{2,1,0:T(8,128)(2,1)S(1)}, bf16[6,128,256]{2,1,0:T(8,128)(2,1)S(1)}, u32[]{:S(2)}, u32[]{:S(2)}) collective-permute-start(bf16[6,128,256]{2,1,0:T(8,128)(2,1)S(1)} %get-tuple-element.47), channel_id=1, source_target_pairs={{0,1},{1,2},{2,3},{3,0},{4,5},{5,6},{6,7},{7,4},{8,9},{9,10},{10,1... | collective-permute-start | bytes 1179656 | tf_op jit(solution)/shard_map/ppermute | solution.py:46
  55.1 11.9 %collective-permute-start.5 = (bf16[6,128,256]{2,1,0:T(8,128)(2,1)S(1)}, bf16[6,128,256]{2,1,0:T(8,128)(2,1)S(1)}, u32[]{:S(2)}, u32[]{:S(2)}) collective-permute-start(bf16[6,128,256]{2,1,0:T(8,128)(2,1)S(1)} %get-tuple-element.48), channel_id=1, source_target_pairs={{0,3},{1,0},{2,1},{3,2},{4,7},{5,4},{6,5},{7,6},{8,11},{9,8},{10,9... | collective-permute-start | bytes 1179656 | tf_op jit(solution)/shard_map/ppermute | solution.py:46
  55.1 14.6 %collective-permute-start.16 = (bf16[6,128,256]{2,1,0:T(8,128)(2,1)S(1)}, bf16[6,128,256]{2,1,0:T(8,128)(2,1)S(1)}, u32[]{:S(2)}, u32[]{:S(2)}) collective-permute-start(bf16[6,128,256]{2,1,0:T(8,128)(2,1)S(1)} %get-tuple-element.57), channel_id=1, source_target_pairs={{0,4},{1,5},{2,6},{3,7},{4,8},{5,9},{6,10},{7,11},{8,12},{9,13},{1... | collective-permute-start | bytes 1179656 | tf_op jit(solution)/shard_map/ppermute | solution.py:46
  58.4 12.0 %collective-permute-start.17 = (bf16[6,128,256]{2,1,0:T(8,128)(2,1)S(1)}, bf16[6,128,256]{2,1,0:T(8,128)(2,1)S(1)}, u32[]{:S(2)}, u32[]{:S(2)}) collective-permute-start(bf16[6,128,256]{2,1,0:T(8,128)(2,1)S(1)} %get-tuple-element.58), channel_id=1, source_target_pairs={{0,12},{1,13},{2,14},{3,15},{4,0},{5,1},{6,2},{7,3},{8,4},{9,5},{1... | collective-permute-start | bytes 1179656 | tf_op jit(solution)/shard_map/ppermute | solution.py:46
  60.5 44.0 %collective-permute-start.32 = (bf16[2,256,1024]{2,1,0:T(8,128)(2,1)}, bf16[2,256,1024]{2,1,0:T(8,128)(2,1)}, u32[]{:S(2)}, u32[]{:S(2)}) collective-permute-start(bf16[2,256,1024]{2,1,0:T(8,128)(2,1)} %shard_map.122), channel_id=1, source_target_pairs={{0,16},{1,17},{2,18},{3,19},{4,20},{5,21},{6,22},{7,23},{8,24},{9,... | collective-permute-start | bytes 3145736 | tf_op jit(solution)/shard_map/ppermute | solution.py:401
  66.8 5.7 %collective-permute-start.6 = (bf16[2,128,256]{2,1,0:T(8,128)(2,1)S(1)}, bf16[2,128,256]{2,1,0:T(8,128)(2,1)S(1)}, u32[]{:S(2)}, u32[]{:S(2)}) collective-permute-start(bf16[2,128,256]{2,1,0:T(8,128)(2,1)S(1)} %slice.34), channel_id=1, source_target_pairs={{0,1},{1,2},{2,3},{3,0},{4,5},{5,6},{6,7},{7,4},{8,9},{9,10},{10,1... | collective-permute-start | bytes 393224 | tf_op jit(solution)/shard_map/ppermute | solution.py:46
  67.0 5.6 %collective-permute-start.7 = (bf16[2,128,256]{2,1,0:T(8,128)(2,1)S(1)}, bf16[2,128,256]{2,1,0:T(8,128)(2,1)S(1)}, u32[]{:S(2)}, u32[]{:S(2)}) collective-permute-start(bf16[2,128,256]{2,1,0:T(8,128)(2,1)S(1)} %slice.35), channel_id=1, source_target_pairs={{0,3},{1,0},{2,1},{3,2},{4,7},{5,4},{6,5},{7,6},{8,11},{9,8},{10,9... | collective-permute-start | bytes 393224 | tf_op jit(solution)/shard_map/ppermute | solution.py:46
  69.7 6.1 %collective-permute-start.18 = (bf16[2,128,256]{2,1,0:T(8,128)(2,1)S(1)}, bf16[2,128,256]{2,1,0:T(8,128)(2,1)S(1)}, u32[]{:S(2)}, u32[]{:S(2)}) collective-permute-start(bf16[2,128,256]{2,1,0:T(8,128)(2,1)S(1)} %slice.38), channel_id=1, source_target_pairs={{0,4},{1,5},{2,6},{3,7},{4,8},{5,9},{6,10},{7,11},{8,12},{9,13},{1... | collective-permute-start | bytes 393224 | tf_op jit(solution)/shard_map/ppermute | solution.py:46
  70.4 5.4 %collective-permute-start.19 = (bf16[2,128,256]{2,1,0:T(8,128)(2,1)S(1)}, bf16[2,128,256]{2,1,0:T(8,128)(2,1)S(1)}, u32[]{:S(2)}, u32[]{:S(2)}) collective-permute-start(bf16[2,128,256]{2,1,0:T(8,128)(2,1)S(1)} %slice.39), channel_id=1, source_target_pairs={{0,12},{1,13},{2,14},{3,15},{4,0},{5,1},{6,2},{7,3},{8,4},{9,5},{1... | collective-permute-start | bytes 393224 | tf_op jit(solution)/shard_map/ppermute | solution.py:46
  73.0 6.9 %collective-permute-start.8 = (bf16[128,1024]{1,0:T(8,128)(2,1)S(1)}, bf16[128,1024]{1,0:T(8,128)(2,1)S(1)}, u32[]{:S(2)}, u32[]{:S(2)}) collective-permute-start(bf16[128,1024]{1,0:T(8,128)(2,1)S(1)} %get-tuple-element.49), channel_id=1, source_target_pairs={{0,4},{1,5},{2,6},{3,7},{4,8},{5,9},{6,10},{7,11},{8,12},{9,13},{1... | collective-permute-start | bytes 786440 | tf_op jit(solution)/shard_map/ppermute | solution.py:46
  73.1 6.8 %collective-permute-start.9 = (bf16[128,1024]{1,0:T(8,128)(2,1)S(1)}, bf16[128,1024]{1,0:T(8,128)(2,1)S(1)}, u32[]{:S(2)}, u32[]{:S(2)}) collective-permute-start(bf16[128,1024]{1,0:T(8,128)(2,1)S(1)} %get-tuple-element.50), channel_id=1, source_target_pairs={{0,12},{1,13},{2,14},{3,15},{4,0},{5,1},{6,2},{7,3},{8,4},{9,5},{1... | collective-permute-start | bytes 786440 | tf_op jit(solution)/shard_map/ppermute | solution.py:46
  76.2 8.9 %collective-permute-start.20 = (bf16[128,1024]{1,0:T(8,128)(2,1)S(1)}, bf16[128,1024]{1,0:T(8,128)(2,1)S(1)}, u32[]{:S(2)}, u32[]{:S(2)}) collective-permute-start(bf16[128,1024]{1,0:T(8,128)(2,1)S(1)} %get-tuple-element.59), channel_id=1, source_target_pairs={{0,1},{1,2},{2,3},{3,0},{4,5},{5,6},{6,7},{7,4},{8,9},{9,10},{10,1... | collective-permute-start | bytes 786440 | tf_op jit(solution)/shard_map/ppermute | solution.py:46
  76.5 14.0 %copy-start.11 = (s32[1,256,8]{1,2,0:T(8,128)S(1)}, s32[1,256,8]{1,2,0:T(8,128)}, u32[]{:S(2)}) copy-start(s32[1,256,8]{1,2,0:T(8,128)} %param.15) | copy-start | bytes 24580
  76.6 8.6 %collective-permute-start.21 = (bf16[128,1024]{1,0:T(8,128)(2,1)S(1)}, bf16[128,1024]{1,0:T(8,128)(2,1)S(1)}, u32[]{:S(2)}, u32[]{:S(2)}) collective-permute-start(bf16[128,1024]{1,0:T(8,128)(2,1)S(1)} %get-tuple-element.60), channel_id=1, source_target_pairs={{0,3},{1,0},{2,1},{3,2},{4,7},{5,4},{6,5},{7,6},{8,11},{9,8},{10,9... | collective-permute-start | bytes 786440 | tf_op jit(solution)/shard_map/ppermute | solution.py:46
  81.5 1.0 copy-start.6
  82.5 12.7 %collective-permute-start.10 = (bf16[256,1024]{1,0:T(8,128)(2,1)}, bf16[256,1024]{1,0:T(8,128)(2,1)}, u32[]{:S(2)}, u32[]{:S(2)}) collective-permute-start(bf16[256,1024]{1,0:T(8,128)(2,1)} %get-tuple-element.52), channel_id=1, source_target_pairs={{0,4},{1,5},{2,6},{3,7},{4,8},{5,9},{6,10},{7,11},{8,12},{9,13},{1... | collective-permute-start | bytes 1572872 | tf_op jit(solution)/shard_map/ppermute | solution.py:46
  82.5 12.7 %collective-permute-start.11 = (bf16[256,1024]{1,0:T(8,128)(2,1)}, bf16[256,1024]{1,0:T(8,128)(2,1)}, u32[]{:S(2)}, u32[]{:S(2)}) collective-permute-start(bf16[256,1024]{1,0:T(8,128)(2,1)} %get-tuple-element.53), channel_id=1, source_target_pairs={{0,12},{1,13},{2,14},{3,15},{4,0},{5,1},{6,2},{7,3},{8,4},{9,5},{1... | collective-permute-start | bytes 1572872 | tf_op jit(solution)/shard_map/ppermute | solution.py:46
  87.8 16.7 %copy-start = (f32[256,1024]{1,0:T(8,128)S(1)}, f32[256,1024]{1,0:T(8,128)}, u32[]{:S(2)}) copy-start(f32[256,1024]{1,0:T(8,128)} %anchor.9) | copy-start | bytes 3145732
  87.8 16.7 %copy-start.2 = (f32[1,256,1024]{2,1,0:T(8,128)S(1)}, f32[1,256,1024]{2,1,0:T(8,128)}, u32[]{:S(2)}) copy-start(f32[1,256,1024]{2,1,0:T(8,128)} %first.5) | copy-start | bytes 3145732
  87.8 16.7 %copy-start.3 = (f32[1,256,1024]{2,1,0:T(8,128)S(1)}, f32[1,256,1024]{2,1,0:T(8,128)}, u32[]{:S(2)}) copy-start(f32[1,256,1024]{2,1,0:T(8,128)} %second.5) | copy-start | bytes 3145732
  87.8 12.3 %collective-permute-start.22 = (bf16[256,1024]{1,0:T(8,128)(2,1)}, bf16[256,1024]{1,0:T(8,128)(2,1)}, u32[]{:S(2)}, u32[]{:S(2)}) collective-permute-start(bf16[256,1024]{1,0:T(8,128)(2,1)} %get-tuple-element.62), channel_id=1, source_target_pairs={{0,1},{1,2},{2,3},{3,0},{4,5},{5,6},{6,7},{7,4},{8,9},{9,10},{10,1... | collective-permute-start | bytes 1572872 | tf_op jit(solution)/shard_map/ppermute | solution.py:46
  87.8 12.3 %collective-permute-start.23 = (bf16[256,1024]{1,0:T(8,128)(2,1)}, bf16[256,1024]{1,0:T(8,128)(2,1)}, u32[]{:S(2)}, u32[]{:S(2)}) collective-permute-start(bf16[256,1024]{1,0:T(8,128)(2,1)} %get-tuple-element.63), channel_id=1, source_target_pairs={{0,3},{1,0},{2,1},{3,2},{4,7},{5,4},{6,5},{7,6},{8,11},{9,8},{10,9... | collective-permute-start | bytes 1572872 | tf_op jit(solution)/shard_map/ppermute | solution.py:46
  100.2 1.2 copy-start.7
  101.4 1.2 copy-start.9
  107.0 15.5 %collective-permute-start.33 = (bf16[128,1024]{1,0:T(8,128)(2,1)S(1)}, bf16[128,1024]{1,0:T(8,128)(2,1)S(1)}, u32[]{:S(2)}, u32[]{:S(2)}) collective-permute-start(bf16[128,1024]{1,0:T(8,128)(2,1)S(1)} %shard_map.124), channel_id=1, source_target_pairs={{0,32},{32,0},{64,96},{96,64},{128,160},{160,128},{192,224},{224,1... | collective-permute-start | bytes 786440 | tf_op jit(solution)/shard_map/ppermute | solution.py:320
  122.5 21.4 %copy-start.4 = (f32[256,1024]{1,0:T(8,128)S(1)}, f32[256,1024]{1,0:T(8,128)}, u32[]{:S(2)}) copy-start(f32[256,1024]{1,0:T(8,128)} %momentum.3) | copy-start | bytes 3145732
  123.1 5.2 %collective-permute-start.34 = (bf16[64,1024]{1,0:T(8,128)(2,1)S(1)}, bf16[64,1024]{1,0:T(8,128)(2,1)S(1)}, u32[]{:S(2)}, u32[]{:S(2)}) collective-permute-start(bf16[64,1024]{1,0:T(8,128)(2,1)S(1)} %get-tuple-element.75), channel_id=1, source_target_pairs={{0,64},{32,96},{64,0},{96,32},{128,192},{160,224},{192,128},{224,1... | collective-permute-start | bytes 393224 | tf_op jit(solution)/shard_map/ppermute | solution.py:320
  128.3 8.8 %collective-permute-start.35 = (bf16[64,1024]{1,0:T(8,128)(2,1)S(1)}, bf16[64,1024]{1,0:T(8,128)(2,1)S(1)}, u32[]{:S(2)}, u32[]{:S(2)}) collective-permute-start(bf16[64,1024]{1,0:T(8,128)(2,1)S(1)} %shard_map.126.refs_0_), channel_id=1, source_target_pairs={{0,128},{32,160},{64,192},{96,224},{128,0},{160,32},{192,64},{224,... | collective-permute-start | bytes 393224 | tf_op jit(solution)/shard_map/ppermute | solution.py:320
  137.2 4.2 %collective-permute-start.36 = (bf16[64,1024]{1,0:T(8,128)(2,1)S(1)}, bf16[64,1024]{1,0:T(8,128)(2,1)S(1)}, u32[]{:S(2)}, u32[]{:S(2)}) collective-permute-start(bf16[64,1024]{1,0:T(8,128)(2,1)S(1)} %shard_map.128.ours), channel_id=1, source_target_pairs={{0,64},{32,96},{64,0},{96,32},{128,192},{160,224},{192,128},{224,1... | collective-permute-start | bytes 393224 | tf_op jit(solution)/shard_map/ppermute | solution.py:320
  142.0 3.5 %collective-permute-start.37 = (bf16[128,1024]{1,0:T(8,128)(2,1)S(1)}, bf16[128,1024]{1,0:T(8,128)(2,1)S(1)}, u32[]{:S(2)}, u32[]{:S(2)}) collective-permute-start(bf16[128,1024]{1,0:T(8,128)(2,1)S(1)} %shard_map.129.total), channel_id=1, source_target_pairs={{0,32},{32,0},{64,96},{96,64},{128,160},{160,128},{192,224},{224,1... | collective-permute-start | bytes 786440 | tf_op jit(solution)/shard_map/ppermute | solution.py:320
  (2 other events, 1.6 us)

commit v4 on v3

--- a/solution.py
+++ b/solution.py
@@ -185,7 +185,7 @@
     @pl.loop(0, out.shape[1], step=16)
     def _(r):
         rows = pl.ds(pl.multiple_of(r, 16), 16)
-        for step in range(2):
+        for step in range(out.shape[0]):
             total = ins[3 * step][rows, :]
             for ref in ins[3 * step + 1 : 3 * step + 3]:
                 total = total + ref[rows, :].astype(jnp.float32)
@@ -194,8 +194,9 @@
 
 def totals(parts, dtype):
     return pl.pallas_call(
-        total_kernel, in_specs=[VMEM] * 6, out_specs=VMEM,
-        out_shape=shape_of((2,) + parts[0].shape, dtype), cost_estimate=SHORT, compiler_params=PARAMS,
+        total_kernel, in_specs=[VMEM] * len(parts), out_specs=VMEM,
+        out_shape=shape_of((len(parts) // 3,) + parts[0].shape, dtype),
+        cost_estimate=SHORT, compiler_params=PARAMS,
     )(*parts)
 
 
@@ -216,20 +217,21 @@
 def adam_update(weights, first, second, gradient):
     first = BETA_ONE * first + (1.0 - BETA_ONE) * gradient
     second = BETA_TWO * second + (1.0 - BETA_TWO) * gradient * gradient
-    weights = weights - INNER_RATE * (first / (jnp.sqrt(second) + EPSILON) + DECAY * weights)
+    root = second * lax.rsqrt(second)
+    weights = weights - INNER_RATE * (first / (root + EPSILON) + DECAY * weights)
     return weights, first, second
 
 
 def inner_steps(anchor, first, second, own, got, here):
     weights, one, two = anchor[here], first[(0,) + here], second[(0,) + here]
-    for step in range(own.shape[0]):
-        at = (step,) + here
-        gradient = own[at] + got[at].astype(jnp.float32)
+    for step, ref in enumerate(own):
+        gradient = ref[(0,) + here] + got[(step,) + here].astype(jnp.float32)
         weights, one, two = adam_update(weights, one, two, gradient)
     return weights, one, two
 
 
-def code_kernel(turn, spot, anchor, first, second, own, got, scale, out):
+def code_kernel(turn, spot, anchor, first, second, own_a, own_b, got, scale, out):
+    own = own_a, own_b
     half = out.shape[0]
     base = lax.rem(spot[2] + turn, CORES) * half
 
@@ -256,13 +258,15 @@
     rows, width = anchor.shape
     return pl.pallas_call(
         functools.partial(code_kernel, turn),
-        in_specs=[SMEM] + [VMEM] * 6, out_specs=VMEM,
+        in_specs=[SMEM] + [VMEM] * 7, out_specs=VMEM,
         out_shape=shape_of((rows // CORES, width), jnp.bfloat16),
         cost_estimate=SHORT, compiler_params=PARAMS,
-    )(spot, anchor, first, second, own, got, exponents)
-
-
-def moment_kernel(anchor, first, second, own, got, new_first, new_second):
+    )(spot, anchor, first, second, *own, got, exponents)
+
+
+def moment_kernel(anchor, first, second, own_a, own_b, got, new_first, new_second):
+    own = own_a, own_b
+
     @pl.loop(0, anchor.shape[0], step=16)
     def _(r):
         rows = pl.ds(pl.multiple_of(r, 16), 16)
@@ -276,9 +280,9 @@
 def moments(anchor, first, second, own, got):
     out = shape_of(first.shape, first.dtype)
     return pl.pallas_call(
-        moment_kernel, in_specs=[VMEM] * 5, out_specs=[VMEM] * 2, out_shape=[out] * 2,
-        cost_estimate=SHORT, compiler_params=PARAMS,
-    )(anchor, first, second, own, got)
+        moment_kernel, in_specs=[VMEM] * 6, out_specs=[VMEM] * 2, out_shape=[out] * 2,
+        cost_estimate=SHORT, compiler_params=PARAMS,
+    )(anchor, first, second, *own, got)
 
 
 def pair_kernel(spot, ours, got, keep, send):
@@ -298,21 +302,6 @@
     )(spot, ours, got)
 
 
-def join_kernel(spot, ours, got, out):
-    rows = ours.shape[0]
-    for turn, ref in ((0, ours), (1, got)):
-        at = pl.ds(pl.multiple_of(lax.rem(spot[3] + turn, 2) * rows, rows), rows)
-        out[at, :] = ref[...]
-
-
-def join(spot, ours, got):
-    rows, width = ours.shape
-    return pl.pallas_call(
-        join_kernel, in_specs=[SMEM, VMEM, VMEM], out_specs=VMEM,
-        out_shape=shape_of((2 * rows, width), ours.dtype), cost_estimate=SHORT, compiler_params=PARAMS,
-    )(spot, ours, got)
-
-
 def swap(block, line, core):
     pairs = [
         (z * CORES + c, (z ^ line) * CORES + (c ^ core)) for z in range(LINE) for c in range(CORES)
@@ -320,51 +309,45 @@
     return lax.ppermute(block, "replica", pairs)
 
 
-def outer_kernel(turn, spot, total, anchor, momentum, *refs):
-    new_weights, new_momentum, weights, moving, sems = refs[-5:]
-    rows = total.shape[0]
-    base = lax.rem(spot[2] + turn, CORES) * rows
-    tile = rows // 4
+def outer_kernel(turns, spot, anchor, momentum, *refs):
+    totals, (new_weights, new_momentum, weights, moving, sems) = refs[: len(turns)], refs[-5:]
+    rows = totals[0].shape[0]
     stores = []
-    for r in range(0, rows, tile):
-        here = pl.ds(pl.multiple_of(base + r, tile), tile)
-        average = total[r : r + tile, :].astype(jnp.float32) * (1.0 / (LINE * CORES))
-        moved = MOMENTUM * momentum[here, :] + average
-        moving[r : r + tile, :] = moved
-        weights[r : r + tile, :] = anchor[here, :] - OUTER_RATE * (average + MOMENTUM * moved)
-        for k, (held, out) in enumerate(((moving, new_momentum), (weights, new_weights))):
-            store = pltpu.make_async_copy(
-                held.at[pl.ds(r, tile)], out.at[here], sems.at[k, r // tile]
-            )
-            store.start()
-            stores.append(store)
+    for part, ((core, line), total) in enumerate(zip(turns, totals)):
+        quarter = lax.rem(spot[2] + core, CORES) * 2 + lax.rem(spot[3] + line, 2)
+        tile = rows // 2
+        for r in range(0, rows, tile):
+            here = pl.ds(pl.multiple_of(quarter * rows + r, tile), tile)
+            average = total[r : r + tile, :].astype(jnp.float32) * (1.0 / (LINE * CORES))
+            moved = MOMENTUM * momentum[here, :] + average
+            moving[part, r : r + tile, :] = moved
+            weights[part, r : r + tile, :] = anchor[here, :] - OUTER_RATE * (average + MOMENTUM * moved)
+            for k, (held, out) in enumerate(((moving, new_momentum), (weights, new_weights))):
+                store = pltpu.make_async_copy(
+                    held.at[part, pl.ds(r, tile)], out.at[here], sems.at[k, part, r // tile]
+                )
+                store.start()
+                stores.append(store)
     for store in stores:
         store.wait()
 
 
-def outer_step(turn, spot, total, anchor, momentum, outs=()):
-    rows, width = total.shape
-    return pl.pallas_call(
-        functools.partial(outer_kernel, turn),
-        in_specs=[SMEM] + [VMEM] * 3 + [HBM] * len(outs),
+def outer_step(turns, spot, anchor, momentum, totals, outs=()):
+    count, (rows, width) = len(turns), totals[0].shape
+    return pl.pallas_call(
+        functools.partial(outer_kernel, turns),
+        in_specs=[SMEM] + [VMEM] * (2 + count) + [HBM] * len(outs),
         out_specs=[HBM] * 2,
         out_shape=[shape_of(anchor.shape, anchor.dtype)] * 2,
         scratch_shapes=[
-            pltpu.VMEM((rows, width), jnp.float32),
-            pltpu.VMEM((rows, width), jnp.float32),
-            pltpu.SemaphoreType.DMA((2, 4)),
+            pltpu.VMEM((count, rows, width), jnp.float32),
+            pltpu.VMEM((count, rows, width), jnp.float32),
+            pltpu.SemaphoreType.DMA((2, count, 2)),
         ],
-        input_output_aliases={4 + k: k for k in range(len(outs))},
+        input_output_aliases={3 + count + k: k for k in range(len(outs))},
         cost_estimate=SHORT,
         compiler_params=PARAMS,
-    )(spot, total, anchor, momentum, *outs)
-
-
-def replica_sum(spot, ours, got, late):
-    keep, send = pair_sum(spot, ours, got)
-    total = add([keep, swap(send, 1, 0)])
-    total = add([after(total, late), swap(total, 2, 0)])
-    return join(spot, total, swap(total, 1, 0))
+    )(spot, anchor, momentum, *totals, *outs)
 
 
 def on_device(
@@ -387,29 +370,34 @@
         off = [along(ring, block[-handed:], -1) for ring, block in zip(rings, back)]
         return [[ahead[step], back[step], on[step], off[step]] for step in range(2)]
 
-    def reduce(pieces, dtype):
+    def reduce(pieces):
         parts = []
         for ring, piece in zip(("x", "y"), pieces):
             low, high = opposite(piece)
             own, ahead, back = nearest(piece, along(ring, low, 1), along(ring, high, -1))
-            parts += [own, along(ring, ahead, 1), along(ring, back, -1)]
-        return totals(parts, dtype)
+            parts.append([own, along(ring, ahead, 1), along(ring, back, -1)])
+        return parts
 
     soon = gather([block[1] for block in sent], [block[2] for block in sent], 4)
     soon = [[sent[step][0]] + soon[step] for step in range(2)]
-    theirs = reduce(soon, jnp.bfloat16)
+    theirs = totals(sum(reduce(soon), []), jnp.bfloat16)
     got = lax.ppermute(theirs, "fsdp", fsdp_shift(1, 0, 0))
     late = gather([block[3] for block in sent], [block[4] for block in sent], 2)
-    own = reduce([soon[step] + late[step] for step in range(2)], jnp.float32)
+    own = [totals(part, jnp.float32) for part in reduce([soon[step] + late[step] for step in range(2)])]
 
     state = anchor, first_moment, second_moment, own, got
     other = swap(code(1, spot, *state, exponents), 0, 1)
     keep = code(0, spot, *state, exponents)
     new_first, new_second = moments(*state[:4], after(got, other))
-    total = replica_sum(spot, keep, other, new_first)
-    other = swap(total, 0, 1)
-    outs = outer_step(0, spot, total, anchor, outer_momentum)
-    new_weights, new_momentum = outer_step(1, spot, other, anchor, outer_momentum, outs)
+    kept, sent = pair_sum(spot, keep, other)
+    total = add([kept, swap(sent, 1, 0)])
+    total = add([after(total, new_first), swap(total, 2, 0)])
+    across = swap(total, 0, 1)
+    beside = swap(total, 1, 0)
+    outs = outer_step([(0, 0)], spot, anchor, outer_momentum, [total])
+    last = swap(after(beside, outs), 0, 1)
+    outs = outer_step([(0, 1), (1, 0)], spot, anchor, outer_momentum, [beside, across], outs)
+    new_weights, new_momentum = outer_step([(1, 1)], spot, anchor, outer_momentum, [last], outs)
     return new_weights, new_momentum, new_first, new_second
 
 

time: 148 us -> 145 us (0.980)
  waiting for transfers between devices: 44.7 us -> 39.7 us
    ppermute x32, waiting for transfers between devices: 30.8 us -> 28.2 us  [along(): return lax.ppermute(block, 'fsdp', fsdp_shift(*shift))]
    ppermute x5 -> x6, waiting for transfers between devices: 13.9 us -> 11.5 us  [swap(): return lax.ppermute(block, 'replica', pairs)]
    pallas_call x6 -> x7, Pallas kernels: 10.3 us -> 11.9 us  [the longest x3 4.38 us: outer_step(): pl.pallas_call(functools.partial(outer_kernel, turns), in_specs=[SMEM] +...]
    ppermute x5 -> x6, starting transfers between devices: 16 us -> 16.9 us  [swap(): return lax.ppermute(block, 'replica', pairs)]
  transfers between devices with their start and end apart: 38 -> 39, of which waited for: 12 -> 12; matrix products, arithmetic and copies ran while one was open for 0% -> 0% of each run, Pallas kernels for 13% -> 15%
where the time goes in v4:
time: 145 us; the launch traced here: 144 us
  starting transfers between devices  68.2 us (47%)
  waiting for transfers between devices  39.7 us (27%)
  Pallas kernels  26.7 us (18%)
  local copies, waits for them, and re-layouts  8.63 us (6%)
    ppermute x32, starting transfers between devices, along(): return lax.ppermute(block, 'fsdp', fsdp_shift(*shift))  45 us
    ppermute x32, waiting for transfers between devices, along(): return lax.ppermute(block, 'fsdp', fsdp_shift(*shift))  28.2 us
    ppermute x6, starting transfers between devices, swap(): return lax.ppermute(block, 'replica', pairs)  16.9 us
    ppermute x6, waiting for transfers between devices, swap(): return lax.ppermute(block, 'replica', pairs)  11.5 us
    unnamed x25, local copies, waits for them, and re-layouts  8.44 us
    ppermute x1, starting transfers between devices, on_device(): got = lax.ppermute(theirs, 'fsdp', fsdp_shift(1, 0, 0))  6.36 us
    pallas_call x4, Pallas kernels, nearest(): pl.pallas_call(nearest_kernel, in_specs=[VMEM] * (len(pieces) + 2), out_s...  5.25 us
    pallas_call x2, Pallas kernels, code(): pl.pallas_call(functools.partial(code_kernel, turn), in_specs=[SMEM] + [V...  4.59 us
  transfers between devices with their start and end apart: 39, of which 12 were waited for; matrix products, arithmetic and copies ran while one was open for 0% of the time, Pallas kernels for 15%

profile of v4, /device:TPU:1, one launch (start us, length us, event | category | flops | bytes accessed | tf_op | source)
XLA Modules:
  0.0 144.4 jit_solution(6383274032518385665)
XLA Ops:
  0.8 2.2 %copy-done.1 = bf16[1,2,128,8192]{3,2,1,0:T(8,128)(2,1)S(1)} copy-done((bf16[1,2,128,8192]{3,2,1,0:T(8,128)(2,1)S(1)}, bf16[1,2,128,8192]{3,2,1,0:T(8,128)(2,1)}, u32[]{:S(2)}) %copy-start.1) | copy-done | bytes 4194328
  3.0 1.0 copy-done.5
  4.7 1.2 shard_map.111
  5.9 2.2 %collective-permute-start = (bf16[10,128,256]{2,1,0:T(8,128)(2,1)S(1)}, bf16[10,128,256]{2,1,0:T(8,128)(2,1)S(1)}, u32[]{:S(2)}, u32[]{:S(2)}) collective-permute-start(bf16[10,128,256]{2,1,0:T(8,128)(2,1)S(1)} %get-tuple-element.48), channel_id=1, source_target_pairs={{0,1},{1,2},{2,3},{3,0},{4,5},{5,6},{6,7},{7,4},{8,9},{9,10},{10,1... | collective-permute-start | bytes 1966088 | tf_op jit(solution)/shard_map/ppermute | solution.py:46
  8.1 1.5 %collective-permute-start.1 = (bf16[10,128,256]{2,1,0:T(8,128)(2,1)S(1)}, bf16[10,128,256]{2,1,0:T(8,128)(2,1)S(1)}, u32[]{:S(2)}, u32[]{:S(2)}) collective-permute-start(bf16[10,128,256]{2,1,0:T(8,128)(2,1)S(1)} %get-tuple-element.49), channel_id=1, source_target_pairs={{0,3},{1,0},{2,1},{3,2},{4,7},{5,4},{6,5},{7,6},{8,11},{9,8},{10,9... | collective-permute-start | bytes 1966088 | tf_op jit(solution)/shard_map/ppermute | solution.py:46
  9.7 1.2 shard_map.115
  10.9 1.3 collective-permute-start.12
  12.2 1.5 %collective-permute-start.13 = (bf16[10,128,256]{2,1,0:T(8,128)(2,1)S(1)}, bf16[10,128,256]{2,1,0:T(8,128)(2,1)S(1)}, u32[]{:S(2)}, u32[]{:S(2)}) collective-permute-start(bf16[10,128,256]{2,1,0:T(8,128)(2,1)S(1)} %get-tuple-element.59), channel_id=1, source_target_pairs={{0,12},{1,13},{2,14},{3,15},{4,0},{5,1},{6,2},{7,3},{8,4},{9,5},{1... | collective-permute-start | bytes 1966088 | tf_op jit(solution)/shard_map/ppermute | solution.py:46
  13.7 8.3 %collective-permute-done.refs_1_ = bf16[10,128,256]{2,1,0:T(8,128)(2,1)S(1)} collective-permute-done((bf16[10,128,256]{2,1,0:T(8,128)(2,1)S(1)}, bf16[10,128,256]{2,1,0:T(8,128)(2,1)S(1)}, u32[]{:S(2)}, u32[]{:S(2)}) %collective-permute-start) | collective-permute-done | bytes 655392 | tf_op jit(solution)/shard_map/ppermute | solution.py:46
  22.0 1.6 %collective-permute-start.2 = (bf16[4,128,256]{2,1,0:T(8,128)(2,1)S(1)}, bf16[4,128,256]{2,1,0:T(8,128)(2,1)S(1)}, u32[]{:S(2)}, u32[]{:S(2)}) collective-permute-start(bf16[4,128,256]{2,1,0:T(8,128)(2,1)S(1)} %slice.32), channel_id=1, source_target_pairs={{0,1},{1,2},{2,3},{3,0},{4,5},{5,6},{6,7},{7,4},{8,9},{9,10},{10,1... | collective-permute-start | bytes 786440 | tf_op jit(solution)/shard_map/ppermute | solution.py:46
  23.7 1.7 %collective-permute-start.3 = (bf16[4,128,256]{2,1,0:T(8,128)(2,1)S(1)}, bf16[4,128,256]{2,1,0:T(8,128)(2,1)S(1)}, u32[]{:S(2)}, u32[]{:S(2)}) collective-permute-start(bf16[4,128,256]{2,1,0:T(8,128)(2,1)S(1)} %slice.33), channel_id=1, source_target_pairs={{0,3},{1,0},{2,1},{3,2},{4,7},{5,4},{6,5},{7,6},{8,11},{9,8},{10,9... | collective-permute-start | bytes 786440 | tf_op jit(solution)/shard_map/ppermute | solution.py:46
  25.6 2.4 %collective-permute-start.14 = (bf16[4,128,256]{2,1,0:T(8,128)(2,1)S(1)}, bf16[4,128,256]{2,1,0:T(8,128)(2,1)S(1)}, u32[]{:S(2)}, u32[]{:S(2)}) collective-permute-start(bf16[4,128,256]{2,1,0:T(8,128)(2,1)S(1)} %slice.36), channel_id=1, source_target_pairs={{0,4},{1,5},{2,6},{3,7},{4,8},{5,9},{6,10},{7,11},{8,12},{9,13},{1... | collective-permute-start | bytes 786440 | tf_op jit(solution)/shard_map/ppermute | solution.py:46
  28.0 1.4 collective-permute-start.15
  30.0 3.1 %collective-permute-start.24 = (bf16[128,1024]{1,0:T(8,128)(2,1)S(1)}, bf16[128,1024]{1,0:T(8,128)(2,1)S(1)}, u32[]{:S(2)}, u32[]{:S(2)}) collective-permute-start(bf16[128,1024]{1,0:T(8,128)(2,1)S(1)} %get-tuple-element.67), channel_id=1, source_target_pairs={{0,4},{1,5},{2,6},{3,7},{4,8},{5,9},{6,10},{7,11},{8,12},{9,13},{1... | collective-permute-start | bytes 786440 | tf_op jit(solution)/shard_map/ppermute | solution.py:46
  33.2 1.4 collective-permute-start.25
  35.1 2.7 %collective-permute-start.29 = (bf16[128,1024]{1,0:T(8,128)(2,1)S(1)}, bf16[128,1024]{1,0:T(8,128)(2,1)S(1)}, u32[]{:S(2)}, u32[]{:S(2)}) collective-permute-start(bf16[128,1024]{1,0:T(8,128)(2,1)S(1)} %get-tuple-element.73), channel_id=1, source_target_pairs={{0,3},{1,0},{2,1},{3,2},{4,7},{5,4},{6,5},{7,6},{8,11},{9,8},{10,9... | collective-permute-start | bytes 786440 | tf_op jit(solution)/shard_map/ppermute | solution.py:46
  37.8 2.8 %collective-permute-done.24.refs_5_ = bf16[128,1024]{1,0:T(8,128)(2,1)S(1)} collective-permute-done((bf16[128,1024]{1,0:T(8,128)(2,1)S(1)}, bf16[128,1024]{1,0:T(8,128)(2,1)S(1)}, u32[]{:S(2)}, u32[]{:S(2)}) %collective-permute-start.24) | collective-permute-done | bytes 262176 | tf_op jit(solution)/shard_map/ppermute | solution.py:46
  41.8 3.1 %collective-permute-start.27 = (bf16[256,1024]{1,0:T(8,128)(2,1)S(1)}, bf16[256,1024]{1,0:T(8,128)(2,1)S(1)}, u32[]{:S(2)}, u32[]{:S(2)}) collective-permute-start(bf16[256,1024]{1,0:T(8,128)(2,1)S(1)} %get-tuple-element.71), channel_id=1, source_target_pairs={{0,12},{1,13},{2,14},{3,15},{4,0},{5,1},{6,2},{7,3},{8,4},{9,5},{1... | collective-permute-start | bytes 1572872 | tf_op jit(solution)/shard_map/ppermute | solution.py:46
  46.1 2.7 %collective-permute-start.31 = (bf16[256,1024]{1,0:T(8,128)(2,1)S(1)}, bf16[256,1024]{1,0:T(8,128)(2,1)S(1)}, u32[]{:S(2)}, u32[]{:S(2)}) collective-permute-start(bf16[256,1024]{1,0:T(8,128)(2,1)S(1)} %get-tuple-element.76), channel_id=1, source_target_pairs={{0,3},{1,0},{2,1},{3,2},{4,7},{5,4},{6,5},{7,6},{8,11},{9,8},{10,9... | collective-permute-start | bytes 1572872 | tf_op jit(solution)/shard_map/ppermute | solution.py:46
  48.8 6.3 %collective-permute-done.26.refs_1_ = bf16[256,1024]{1,0:T(8,128)(2,1)S(1)} collective-permute-done((bf16[256,1024]{1,0:T(8,128)(2,1)S(1)}, bf16[256,1024]{1,0:T(8,128)(2,1)S(1)}, u32[]{:S(2)}, u32[]{:S(2)}) %collective-permute-start.26) | collective-permute-done | bytes 524320 | tf_op jit(solution)/shard_map/ppermute | solution.py:46
  55.6 2.7 %collective-permute-done.30.refs_4_ = bf16[256,1024]{1,0:T(8,128)(2,1)S(1)} collective-permute-done((bf16[256,1024]{1,0:T(8,128)(2,1)S(1)}, bf16[256,1024]{1,0:T(8,128)(2,1)S(1)}, u32[]{:S(2)}, u32[]{:S(2)}) %collective-permute-start.30) | collective-permute-done | bytes 524320 | tf_op jit(solution)/shard_map/ppermute | solution.py:46
  59.1 1.4 shard_map.123
  60.5 6.4 %collective-permute-start.32 = (bf16[2,256,1024]{2,1,0:T(8,128)(2,1)}, bf16[2,256,1024]{2,1,0:T(8,128)(2,1)}, u32[]{:S(2)}, u32[]{:S(2)}) collective-permute-start(bf16[2,256,1024]{2,1,0:T(8,128)(2,1)} %shard_map.123), channel_id=1, source_target_pairs={{0,16},{1,17},{2,18},{3,19},{4,20},{5,21},{6,22},{7,23},{8,24},{9,... | collective-permute-start | bytes 3145736 | tf_op jit(solution)/shard_map/ppermute | solution.py:384
  67.0 2.7 %collective-permute-start.7 = (bf16[2,128,256]{2,1,0:T(8,128)(2,1)S(1)}, bf16[2,128,256]{2,1,0:T(8,128)(2,1)S(1)}, u32[]{:S(2)}, u32[]{:S(2)}) collective-permute-start(bf16[2,128,256]{2,1,0:T(8,128)(2,1)S(1)} %slice.35), channel_id=1, source_target_pairs={{0,3},{1,0},{2,1},{3,2},{4,7},{5,4},{6,5},{7,6},{8,11},{9,8},{10,9... | collective-permute-start | bytes 393224 | tf_op jit(solution)/shard_map/ppermute | solution.py:46
  70.4 2.1 %collective-permute-start.19 = (bf16[2,128,256]{2,1,0:T(8,128)(2,1)S(1)}, bf16[2,128,256]{2,1,0:T(8,128)(2,1)S(1)}, u32[]{:S(2)}, u32[]{:S(2)}) collective-permute-start(bf16[2,128,256]{2,1,0:T(8,128)(2,1)S(1)} %slice.39), channel_id=1, source_target_pairs={{0,12},{1,13},{2,14},{3,15},{4,0},{5,1},{6,2},{7,3},{8,4},{9,5},{1... | collective-permute-start | bytes 393224 | tf_op jit(solution)/shard_map/ppermute | solution.py:46
  73.1 2.7 %collective-permute-start.9 = (bf16[128,1024]{1,0:T(8,128)(2,1)S(1)}, bf16[128,1024]{1,0:T(8,128)(2,1)S(1)}, u32[]{:S(2)}, u32[]{:S(2)}) collective-permute-start(bf16[128,1024]{1,0:T(8,128)(2,1)S(1)} %get-tuple-element.53), channel_id=1, source_target_pairs={{0,12},{1,13},{2,14},{3,15},{4,0},{5,1},{6,2},{7,3},{8,4},{9,5},{1... | collective-permute-start | bytes 786440 | tf_op jit(solution)/shard_map/ppermute | solution.py:46
  76.6 2.7 %collective-permute-start.21 = (bf16[128,1024]{1,0:T(8,128)(2,1)S(1)}, bf16[128,1024]{1,0:T(8,128)(2,1)S(1)}, u32[]{:S(2)}, u32[]{:S(2)}) collective-permute-start(bf16[128,1024]{1,0:T(8,128)(2,1)S(1)} %get-tuple-element.63), channel_id=1, source_target_pairs={{0,3},{1,0},{2,1},{3,2},{4,7},{5,4},{6,5},{7,6},{8,11},{9,8},{10,9... | collective-permute-start | bytes 786440 | tf_op jit(solution)/shard_map/ppermute | solution.py:46
  79.9 1.6 %shard_map.113 = (f32[256,1024]{1,0:T(8,128)S(1)}, bf16[256,1024]{1,0:T(8,128)(2,1)}, bf16[256,1024]{1,0:T(8,128)(2,1)}) custom-call(bf16[12,128,256]{2,1,0:T(8,128)(2,1)S(1)} %get-tuple-element.47.refs_0_, bf16[10,128,256]{2,1,0:T(8,128)(2,1)S(1)} %collective-permute-done.refs_1_, bf16[10,128,256]{2,1,0:T(8,128)(2,1)S(1)} %collective-permute-done.1.refs_2_, ...), custom_call_target="tpu_custom_call" | custom-call | flops 1 | bytes 1 | tf_op jit(solution)/shard_map/pallas_call | solution.py:175
  82.5 2.7 %collective-permute-start.11 = (bf16[256,1024]{1,0:T(8,128)(2,1)}, bf16[256,1024]{1,0:T(8,128)(2,1)}, u32[]{:S(2)}, u32[]{:S(2)}) collective-permute-start(bf16[256,1024]{1,0:T(8,128)(2,1)} %get-tuple-element.56), channel_id=1, source_target_pairs={{0,12},{1,13},{2,14},{3,15},{4,0},{5,1},{6,2},{7,3},{8,4},{9,5},{1... | collective-permute-start | bytes 1572872 | tf_op jit(solution)/shard_map/ppermute | solution.py:46
  85.2 1.6 %shard_map.117 = (f32[256,1024]{1,0:T(8,128)S(1)}, bf16[256,1024]{1,0:T(8,128)(2,1)}, bf16[256,1024]{1,0:T(8,128)(2,1)}) custom-call(bf16[12,128,256]{2,1,0:T(8,128)(2,1)S(1)} %get-tuple-element.57.refs_0_, bf16[10,128,256]{2,1,0:T(8,128)(2,1)S(1)} %collective-permute-done.12.refs_1_, bf16[10,128,256]{2,1,0:T(8,128)(2,1)S(1)} %collective-permute-done.13.refs_2_, ...), custom_call_target="tpu_custom_call" | custom-call | flops 1 | bytes 1 | tf_op jit(solution)/shard_map/pallas_call | solution.py:175
  87.8 2.7 %collective-permute-start.23 = (bf16[256,1024]{1,0:T(8,128)(2,1)}, bf16[256,1024]{1,0:T(8,128)(2,1)}, u32[]{:S(2)}, u32[]{:S(2)}) collective-permute-start(bf16[256,1024]{1,0:T(8,128)(2,1)} %get-tuple-element.66), channel_id=1, source_target_pairs={{0,3},{1,0},{2,1},{3,2},{4,7},{5,4},{6,5},{7,6},{8,11},{9,8},{10,9... | collective-permute-start | bytes 1572872 | tf_op jit(solution)/shard_map/ppermute | solution.py:46
  90.6 4.6 %collective-permute-done.10.refs_1_ = bf16[256,1024]{1,0:T(8,128)(2,1)} collective-permute-done((bf16[256,1024]{1,0:T(8,128)(2,1)}, bf16[256,1024]{1,0:T(8,128)(2,1)}, u32[]{:S(2)}, u32[]{:S(2)}) %collective-permute-start.10) | collective-permute-done | bytes 524320 | tf_op jit(solution)/shard_map/ppermute | solution.py:46
  95.2 1.2 copy-done.7
  96.4 1.4 shard_map.114.own_a
  97.8 2.3 %collective-permute-done.22.refs_1_ = bf16[256,1024]{1,0:T(8,128)(2,1)} collective-permute-done((bf16[256,1024]{1,0:T(8,128)(2,1)}, bf16[256,1024]{1,0:T(8,128)(2,1)}, u32[]{:S(2)}, u32[]{:S(2)}) %collective-permute-start.22) | collective-permute-done | bytes 524320 | tf_op jit(solution)/shard_map/ppermute | solution.py:46
  100.2 1.2 copy-done.9
  101.4 1.4 shard_map.118.own_b
  102.8 2.3 %shard_map.125 = bf16[128,1024]{1,0:T(8,128)(2,1)S(1)} custom-call(s32[5]{0:T(128)S(1)} %stack.23.spot, f32[256,1024]{1,0:T(8,128)S(1)} %copy-done, f32[1,256,1024]{2,1,0:T(8,128)S(1)} %copy-done.3, f32[1,256,1024]{2,1,0:T(8,128)S(1)} %copy-done.4, f32[1,256,1024]{2,1,0:T(8,128)S(1)} %shard_map.114.own_a, f32[1,256,1024]{2,1,0:T(8,128)S(1)} %shard_map.118.own_b, ...), custom_call_target="tpu_custom_call" | custom-call | flops 1 | bytes 1 | tf_op jit(solution)/shard_map/pallas_call | solution.py:259
  105.1 13.0 %collective-permute-start.33 = (bf16[128,1024]{1,0:T(8,128)(2,1)S(1)}, bf16[128,1024]{1,0:T(8,128)(2,1)S(1)}, u32[]{:S(2)}, u32[]{:S(2)}) collective-permute-start(bf16[128,1024]{1,0:T(8,128)(2,1)S(1)} %shard_map.125), channel_id=1, source_target_pairs={{0,32},{32,0},{64,96},{96,64},{128,160},{160,128},{192,224},{224,1... | collective-permute-start | bytes 786440 | tf_op jit(solution)/shard_map/ppermute | solution.py:309
  118.2 2.3 %shard_map.124.ours = bf16[128,1024]{1,0:T(8,128)(2,1)S(1)} custom-call(s32[5]{0:T(128)S(1)} %stack.23.spot, f32[256,1024]{1,0:T(8,128)S(1)} %copy-done, f32[1,256,1024]{2,1,0:T(8,128)S(1)} %copy-done.3, f32[1,256,1024]{2,1,0:T(8,128)S(1)} %copy-done.4, f32[1,256,1024]{2,1,0:T(8,128)S(1)} %shard_map.114.own_a, f32[1,256,1024]{2,1,0:T(8,128)S(1)} %shard_map.118.own_b, ...), custom_call_target="tpu_custom_call" | custom-call | flops 1 | bytes 1 | tf_op jit(solution)/shard_map/pallas_call | solution.py:259
  121.8 4.5 %collective-permute-done.34.refs_1_ = bf16[64,1024]{1,0:T(8,128)(2,1)S(1)} collective-permute-done((bf16[64,1024]{1,0:T(8,128)(2,1)S(1)}, bf16[64,1024]{1,0:T(8,128)(2,1)S(1)}, u32[]{:S(2)}, u32[]{:S(2)}) %collective-permute-start.34) | collective-permute-done | bytes 131104 | tf_op jit(solution)/shard_map/ppermute | solution.py:309
  126.6 3.3 %shard_map.128 = (f32[1,256,1024]{2,1,0:T(8,128)}, f32[1,256,1024]{2,1,0:T(8,128)}) custom-call(f32[256,1024]{1,0:T(8,128)S(1)} %copy-done, f32[1,256,1024]{2,1,0:T(8,128)S(1)} %copy-done.3, f32[1,256,1024]{2,1,0:T(8,128)S(1)} %copy-done.4, f32[1,256,1024]{2,1,0:T(8,128)S(1)} %shard_map.114.own_a, f32[1,256,1024]{2,1,0:T(8,128)S(1)} %shard_map.118.own_b, ...), custom_call_target="tpu_custom_call" | custom-call | flops 1 | bytes 1 | tf_op jit(solution)/shard_map/pallas_call | solution.py:282
  129.9 5.3 %collective-permute-done.35.refs_1_ = bf16[64,1024]{1,0:T(8,128)(2,1)S(1)} collective-permute-done((bf16[64,1024]{1,0:T(8,128)(2,1)S(1)}, bf16[64,1024]{1,0:T(8,128)(2,1)S(1)}, u32[]{:S(2)}, u32[]{:S(2)}) %collective-permute-start.35) | collective-permute-done | bytes 131104 | tf_op jit(solution)/shard_map/ppermute | solution.py:309
  136.3 1.4 shard_map.130
  137.7 1.7 %collective-permute-done.36.refs_0_ = bf16[64,1024]{1,0:T(8,128)(2,1)S(1)} collective-permute-done((bf16[64,1024]{1,0:T(8,128)(2,1)S(1)}, bf16[64,1024]{1,0:T(8,128)(2,1)S(1)}, u32[]{:S(2)}, u32[]{:S(2)}) %collective-permute-start.36) | collective-permute-done | bytes 131104 | tf_op jit(solution)/shard_map/ppermute | solution.py:309
  139.4 1.8 %collective-permute-start.37 = (bf16[64,1024]{1,0:T(8,128)(2,1)S(1)}, bf16[64,1024]{1,0:T(8,128)(2,1)S(1)}, u32[]{:S(2)}, u32[]{:S(2)}) collective-permute-start(bf16[64,1024]{1,0:T(8,128)(2,1)S(1)} %collective-permute-done.36.refs_0_), channel_id=1, source_target_pairs={{0,32},{32,0},{64,96},{96,64},{128,160},{160,128},{192,224},{224,1... | collective-permute-start | bytes 393224 | tf_op jit(solution)/shard_map/ppermute | solution.py:309
  141.2 1.6 %shard_map.131 = (f32[256,1024]{1,0:T(8,128)}, f32[256,1024]{1,0:T(8,128)}) custom-call(s32[5]{0:T(128)S(1)} %stack.23.spot, f32[256,1024]{1,0:T(8,128)S(1)} %copy-done, f32[256,1024]{1,0:T(8,128)S(1)} %copy-done.2, bf16[64,1024]{1,0:T(8,128)(2,1)S(1)} %collective-permute-done.36.refs_0_, ...), custom_call_target="tpu_custom_call", output_to_operand_aliasing={{0}: (5, {}), {1}: (6, {})} | custom-call | flops 1 | bytes 1 | tf_op jit(solution)/shard_map/pallas_call | solution.py:337
  142.8 1.4 shard_map.132
  (86 shorter events, 13.6 us)
Async XLA Ops:
  0.8 2.2 %copy-start.1 = (bf16[1,2,128,8192]{3,2,1,0:T(8,128)(2,1)S(1)}, bf16[1,2,128,8192]{3,2,1,0:T(8,128)(2,1)}, u32[]{:S(2)}) copy-start(bf16[1,2,128,8192]{3,2,1,0:T(8,128)(2,1)} %features.3) | copy-start | bytes 12582916
  3.0 1.0 copy-start.5
  5.9 16.1 %collective-permute-start = (bf16[10,128,256]{2,1,0:T(8,128)(2,1)S(1)}, bf16[10,128,256]{2,1,0:T(8,128)(2,1)S(1)}, u32[]{:S(2)}, u32[]{:S(2)}) collective-permute-start(bf16[10,128,256]{2,1,0:T(8,128)(2,1)S(1)} %get-tuple-element.48), channel_id=1, source_target_pairs={{0,1},{1,2},{2,3},{3,0},{4,5},{5,6},{6,7},{7,4},{8,9},{9,10},{10,1... | collective-permute-start | bytes 1966088 | tf_op jit(solution)/shard_map/ppermute | solution.py:46
  8.1 15.5 %collective-permute-start.1 = (bf16[10,128,256]{2,1,0:T(8,128)(2,1)S(1)}, bf16[10,128,256]{2,1,0:T(8,128)(2,1)S(1)}, u32[]{:S(2)}, u32[]{:S(2)}) collective-permute-start(bf16[10,128,256]{2,1,0:T(8,128)(2,1)S(1)} %get-tuple-element.49), channel_id=1, source_target_pairs={{0,3},{1,0},{2,1},{3,2},{4,7},{5,4},{6,5},{7,6},{8,11},{9,8},{10,9... | collective-permute-start | bytes 1966088 | tf_op jit(solution)/shard_map/ppermute | solution.py:46
  10.9 14.7 %collective-permute-start.12 = (bf16[10,128,256]{2,1,0:T(8,128)(2,1)S(1)}, bf16[10,128,256]{2,1,0:T(8,128)(2,1)S(1)}, u32[]{:S(2)}, u32[]{:S(2)}) collective-permute-start(bf16[10,128,256]{2,1,0:T(8,128)(2,1)S(1)} %get-tuple-element.58), channel_id=1, source_target_pairs={{0,4},{1,5},{2,6},{3,7},{4,8},{5,9},{6,10},{7,11},{8,12},{9,13},{1... | collective-permute-start | bytes 1966088 | tf_op jit(solution)/shard_map/ppermute | solution.py:46
  12.2 15.8 %collective-permute-start.13 = (bf16[10,128,256]{2,1,0:T(8,128)(2,1)S(1)}, bf16[10,128,256]{2,1,0:T(8,128)(2,1)S(1)}, u32[]{:S(2)}, u32[]{:S(2)}) collective-permute-start(bf16[10,128,256]{2,1,0:T(8,128)(2,1)S(1)} %get-tuple-element.59), channel_id=1, source_target_pairs={{0,12},{1,13},{2,14},{3,15},{4,0},{5,1},{6,2},{7,3},{8,4},{9,5},{1... | collective-permute-start | bytes 1966088 | tf_op jit(solution)/shard_map/ppermute | solution.py:46
  22.0 7.4 %collective-permute-start.2 = (bf16[4,128,256]{2,1,0:T(8,128)(2,1)S(1)}, bf16[4,128,256]{2,1,0:T(8,128)(2,1)S(1)}, u32[]{:S(2)}, u32[]{:S(2)}) collective-permute-start(bf16[4,128,256]{2,1,0:T(8,128)(2,1)S(1)} %slice.32), channel_id=1, source_target_pairs={{0,1},{1,2},{2,3},{3,0},{4,5},{5,6},{6,7},{7,4},{8,9},{9,10},{10,1... | collective-permute-start | bytes 786440 | tf_op jit(solution)/shard_map/ppermute | solution.py:46
  23.7 5.9 %collective-permute-start.3 = (bf16[4,128,256]{2,1,0:T(8,128)(2,1)S(1)}, bf16[4,128,256]{2,1,0:T(8,128)(2,1)S(1)}, u32[]{:S(2)}, u32[]{:S(2)}) collective-permute-start(bf16[4,128,256]{2,1,0:T(8,128)(2,1)S(1)} %slice.33), channel_id=1, source_target_pairs={{0,3},{1,0},{2,1},{3,2},{4,7},{5,4},{6,5},{7,6},{8,11},{9,8},{10,9... | collective-permute-start | bytes 786440 | tf_op jit(solution)/shard_map/ppermute | solution.py:46
  25.6 8.9 %collective-permute-start.14 = (bf16[4,128,256]{2,1,0:T(8,128)(2,1)S(1)}, bf16[4,128,256]{2,1,0:T(8,128)(2,1)S(1)}, u32[]{:S(2)}, u32[]{:S(2)}) collective-permute-start(bf16[4,128,256]{2,1,0:T(8,128)(2,1)S(1)} %slice.36), channel_id=1, source_target_pairs={{0,4},{1,5},{2,6},{3,7},{4,8},{5,9},{6,10},{7,11},{8,12},{9,13},{1... | collective-permute-start | bytes 786440 | tf_op jit(solution)/shard_map/ppermute | solution.py:46
  28.0 6.5 %collective-permute-start.15 = (bf16[4,128,256]{2,1,0:T(8,128)(2,1)S(1)}, bf16[4,128,256]{2,1,0:T(8,128)(2,1)S(1)}, u32[]{:S(2)}, u32[]{:S(2)}) collective-permute-start(bf16[4,128,256]{2,1,0:T(8,128)(2,1)S(1)} %slice.37), channel_id=1, source_target_pairs={{0,12},{1,13},{2,14},{3,15},{4,0},{5,1},{6,2},{7,3},{8,4},{9,5},{1... | collective-permute-start | bytes 786440 | tf_op jit(solution)/shard_map/ppermute | solution.py:46
  30.0 10.5 %collective-permute-start.24 = (bf16[128,1024]{1,0:T(8,128)(2,1)S(1)}, bf16[128,1024]{1,0:T(8,128)(2,1)S(1)}, u32[]{:S(2)}, u32[]{:S(2)}) collective-permute-start(bf16[128,1024]{1,0:T(8,128)(2,1)S(1)} %get-tuple-element.67), channel_id=1, source_target_pairs={{0,4},{1,5},{2,6},{3,7},{4,8},{5,9},{6,10},{7,11},{8,12},{9,13},{1... | collective-permute-start | bytes 786440 | tf_op jit(solution)/shard_map/ppermute | solution.py:46
  33.2 7.4 %collective-permute-start.25 = (bf16[128,1024]{1,0:T(8,128)(2,1)S(1)}, bf16[128,1024]{1,0:T(8,128)(2,1)S(1)}, u32[]{:S(2)}, u32[]{:S(2)}) collective-permute-start(bf16[128,1024]{1,0:T(8,128)(2,1)S(1)} %get-tuple-element.68), channel_id=1, source_target_pairs={{0,12},{1,13},{2,14},{3,15},{4,0},{5,1},{6,2},{7,3},{8,4},{9,5},{1... | collective-permute-start | bytes 786440 | tf_op jit(solution)/shard_map/ppermute | solution.py:46
  35.0 10.0 %collective-permute-start.28 = (bf16[128,1024]{1,0:T(8,128)(2,1)S(1)}, bf16[128,1024]{1,0:T(8,128)(2,1)S(1)}, u32[]{:S(2)}, u32[]{:S(2)}) collective-permute-start(bf16[128,1024]{1,0:T(8,128)(2,1)S(1)} %get-tuple-element.72), channel_id=1, source_target_pairs={{0,1},{1,2},{2,3},{3,0},{4,5},{5,6},{6,7},{7,4},{8,9},{9,10},{10,1... | collective-permute-start | bytes 786440 | tf_op jit(solution)/shard_map/ppermute | solution.py:46
  35.1 9.9 %collective-permute-start.29 = (bf16[128,1024]{1,0:T(8,128)(2,1)S(1)}, bf16[128,1024]{1,0:T(8,128)(2,1)S(1)}, u32[]{:S(2)}, u32[]{:S(2)}) collective-permute-start(bf16[128,1024]{1,0:T(8,128)(2,1)S(1)} %get-tuple-element.73), channel_id=1, source_target_pairs={{0,3},{1,0},{2,1},{3,2},{4,7},{5,4},{6,5},{7,6},{8,11},{9,8},{10,9... | collective-permute-start | bytes 786440 | tf_op jit(solution)/shard_map/ppermute | solution.py:46
  41.6 13.5 %collective-permute-start.26 = (bf16[256,1024]{1,0:T(8,128)(2,1)S(1)}, bf16[256,1024]{1,0:T(8,128)(2,1)S(1)}, u32[]{:S(2)}, u32[]{:S(2)}) collective-permute-start(bf16[256,1024]{1,0:T(8,128)(2,1)S(1)} %get-tuple-element.70), channel_id=1, source_target_pairs={{0,4},{1,5},{2,6},{3,7},{4,8},{5,9},{6,10},{7,11},{8,12},{9,13},{1... | collective-permute-start | bytes 1572872 | tf_op jit(solution)/shard_map/ppermute | solution.py:46
  41.8 13.2 %collective-permute-start.27 = (bf16[256,1024]{1,0:T(8,128)(2,1)S(1)}, bf16[256,1024]{1,0:T(8,128)(2,1)S(1)}, u32[]{:S(2)}, u32[]{:S(2)}) collective-permute-start(bf16[256,1024]{1,0:T(8,128)(2,1)S(1)} %get-tuple-element.71), channel_id=1, source_target_pairs={{0,12},{1,13},{2,14},{3,15},{4,0},{5,1},{6,2},{7,3},{8,4},{9,5},{1... | collective-permute-start | bytes 1572872 | tf_op jit(solution)/shard_map/ppermute | solution.py:46
  46.0 12.3 %collective-permute-start.30 = (bf16[256,1024]{1,0:T(8,128)(2,1)S(1)}, bf16[256,1024]{1,0:T(8,128)(2,1)S(1)}, u32[]{:S(2)}, u32[]{:S(2)}) collective-permute-start(bf16[256,1024]{1,0:T(8,128)(2,1)S(1)} %get-tuple-element.75), channel_id=1, source_target_pairs={{0,1},{1,2},{2,3},{3,0},{4,5},{5,6},{6,7},{7,4},{8,9},{9,10},{10,1... | collective-permute-start | bytes 1572872 | tf_op jit(solution)/shard_map/ppermute | solution.py:46
  46.1 13.0 %collective-permute-start.31 = (bf16[256,1024]{1,0:T(8,128)(2,1)S(1)}, bf16[256,1024]{1,0:T(8,128)(2,1)S(1)}, u32[]{:S(2)}, u32[]{:S(2)}) collective-permute-start(bf16[256,1024]{1,0:T(8,128)(2,1)S(1)} %get-tuple-element.76), channel_id=1, source_target_pairs={{0,3},{1,0},{2,1},{3,2},{4,7},{5,4},{6,5},{7,6},{8,11},{9,8},{10,9... | collective-permute-start | bytes 1572872 | tf_op jit(solution)/shard_map/ppermute | solution.py:46
  48.8 18.0 %collective-permute-start.4 = (bf16[6,128,256]{2,1,0:T(8,128)(2,1)S(1)}, bf16[6,128,256]{2,1,0:T(8,128)(2,1)S(1)}, u32[]{:S(2)}, u32[]{:S(2)}) collective-permute-start(bf16[6,128,256]{2,1,0:T(8,128)(2,1)S(1)} %get-tuple-element.50), channel_id=1, source_target_pairs={{0,1},{1,2},{2,3},{3,0},{4,5},{5,6},{6,7},{7,4},{8,9},{9,10},{10,1... | collective-permute-start | bytes 1179656 | tf_op jit(solution)/shard_map/ppermute | solution.py:46
  55.1 11.9 %collective-permute-start.5 = (bf16[6,128,256]{2,1,0:T(8,128)(2,1)S(1)}, bf16[6,128,256]{2,1,0:T(8,128)(2,1)S(1)}, u32[]{:S(2)}, u32[]{:S(2)}) collective-permute-start(bf16[6,128,256]{2,1,0:T(8,128)(2,1)S(1)} %get-tuple-element.51), channel_id=1, source_target_pairs={{0,3},{1,0},{2,1},{3,2},{4,7},{5,4},{6,5},{7,6},{8,11},{9,8},{10,9... | collective-permute-start | bytes 1179656 | tf_op jit(solution)/shard_map/ppermute | solution.py:46
  55.1 14.6 %collective-permute-start.16 = (bf16[6,128,256]{2,1,0:T(8,128)(2,1)S(1)}, bf16[6,128,256]{2,1,0:T(8,128)(2,1)S(1)}, u32[]{:S(2)}, u32[]{:S(2)}) collective-permute-start(bf16[6,128,256]{2,1,0:T(8,128)(2,1)S(1)} %get-tuple-element.60), channel_id=1, source_target_pairs={{0,4},{1,5},{2,6},{3,7},{4,8},{5,9},{6,10},{7,11},{8,12},{9,13},{1... | collective-permute-start | bytes 1179656 | tf_op jit(solution)/shard_map/ppermute | solution.py:46
  58.4 12.0 %collective-permute-start.17 = (bf16[6,128,256]{2,1,0:T(8,128)(2,1)S(1)}, bf16[6,128,256]{2,1,0:T(8,128)(2,1)S(1)}, u32[]{:S(2)}, u32[]{:S(2)}) collective-permute-start(bf16[6,128,256]{2,1,0:T(8,128)(2,1)S(1)} %get-tuple-element.61), channel_id=1, source_target_pairs={{0,12},{1,13},{2,14},{3,15},{4,0},{5,1},{6,2},{7,3},{8,4},{9,5},{1... | collective-permute-start | bytes 1179656 | tf_op jit(solution)/shard_map/ppermute | solution.py:46
  60.5 42.4 %collective-permute-start.32 = (bf16[2,256,1024]{2,1,0:T(8,128)(2,1)}, bf16[2,256,1024]{2,1,0:T(8,128)(2,1)}, u32[]{:S(2)}, u32[]{:S(2)}) collective-permute-start(bf16[2,256,1024]{2,1,0:T(8,128)(2,1)} %shard_map.123), channel_id=1, source_target_pairs={{0,16},{1,17},{2,18},{3,19},{4,20},{5,21},{6,22},{7,23},{8,24},{9,... | collective-permute-start | bytes 3145736 | tf_op jit(solution)/shard_map/ppermute | solution.py:384
  66.8 5.7 %collective-permute-start.6 = (bf16[2,128,256]{2,1,0:T(8,128)(2,1)S(1)}, bf16[2,128,256]{2,1,0:T(8,128)(2,1)S(1)}, u32[]{:S(2)}, u32[]{:S(2)}) collective-permute-start(bf16[2,128,256]{2,1,0:T(8,128)(2,1)S(1)} %slice.34), channel_id=1, source_target_pairs={{0,1},{1,2},{2,3},{3,0},{4,5},{5,6},{6,7},{7,4},{8,9},{9,10},{10,1... | collective-permute-start | bytes 393224 | tf_op jit(solution)/shard_map/ppermute | solution.py:46
  67.0 5.6 %collective-permute-start.7 = (bf16[2,128,256]{2,1,0:T(8,128)(2,1)S(1)}, bf16[2,128,256]{2,1,0:T(8,128)(2,1)S(1)}, u32[]{:S(2)}, u32[]{:S(2)}) collective-permute-start(bf16[2,128,256]{2,1,0:T(8,128)(2,1)S(1)} %slice.35), channel_id=1, source_target_pairs={{0,3},{1,0},{2,1},{3,2},{4,7},{5,4},{6,5},{7,6},{8,11},{9,8},{10,9... | collective-permute-start | bytes 393224 | tf_op jit(solution)/shard_map/ppermute | solution.py:46
  69.7 6.1 %collective-permute-start.18 = (bf16[2,128,256]{2,1,0:T(8,128)(2,1)S(1)}, bf16[2,128,256]{2,1,0:T(8,128)(2,1)S(1)}, u32[]{:S(2)}, u32[]{:S(2)}) collective-permute-start(bf16[2,128,256]{2,1,0:T(8,128)(2,1)S(1)} %slice.38), channel_id=1, source_target_pairs={{0,4},{1,5},{2,6},{3,7},{4,8},{5,9},{6,10},{7,11},{8,12},{9,13},{1... | collective-permute-start | bytes 393224 | tf_op jit(solution)/shard_map/ppermute | solution.py:46
  70.4 5.4 %collective-permute-start.19 = (bf16[2,128,256]{2,1,0:T(8,128)(2,1)S(1)}, bf16[2,128,256]{2,1,0:T(8,128)(2,1)S(1)}, u32[]{:S(2)}, u32[]{:S(2)}) collective-permute-start(bf16[2,128,256]{2,1,0:T(8,128)(2,1)S(1)} %slice.39), channel_id=1, source_target_pairs={{0,12},{1,13},{2,14},{3,15},{4,0},{5,1},{6,2},{7,3},{8,4},{9,5},{1... | collective-permute-start | bytes 393224 | tf_op jit(solution)/shard_map/ppermute | solution.py:46
  73.0 6.9 %collective-permute-start.8 = (bf16[128,1024]{1,0:T(8,128)(2,1)S(1)}, bf16[128,1024]{1,0:T(8,128)(2,1)S(1)}, u32[]{:S(2)}, u32[]{:S(2)}) collective-permute-start(bf16[128,1024]{1,0:T(8,128)(2,1)S(1)} %get-tuple-element.52), channel_id=1, source_target_pairs={{0,4},{1,5},{2,6},{3,7},{4,8},{5,9},{6,10},{7,11},{8,12},{9,13},{1... | collective-permute-start | bytes 786440 | tf_op jit(solution)/shard_map/ppermute | solution.py:46
  73.1 6.8 %collective-permute-start.9 = (bf16[128,1024]{1,0:T(8,128)(2,1)S(1)}, bf16[128,1024]{1,0:T(8,128)(2,1)S(1)}, u32[]{:S(2)}, u32[]{:S(2)}) collective-permute-start(bf16[128,1024]{1,0:T(8,128)(2,1)S(1)} %get-tuple-element.53), channel_id=1, source_target_pairs={{0,12},{1,13},{2,14},{3,15},{4,0},{5,1},{6,2},{7,3},{8,4},{9,5},{1... | collective-permute-start | bytes 786440 | tf_op jit(solution)/shard_map/ppermute | solution.py:46
  76.2 8.9 %collective-permute-start.20 = (bf16[128,1024]{1,0:T(8,128)(2,1)S(1)}, bf16[128,1024]{1,0:T(8,128)(2,1)S(1)}, u32[]{:S(2)}, u32[]{:S(2)}) collective-permute-start(bf16[128,1024]{1,0:T(8,128)(2,1)S(1)} %get-tuple-element.62), channel_id=1, source_target_pairs={{0,1},{1,2},{2,3},{3,0},{4,5},{5,6},{6,7},{7,4},{8,9},{9,10},{10,1... | collective-permute-start | bytes 786440 | tf_op jit(solution)/shard_map/ppermute | solution.py:46
  76.5 13.9 %copy-start.11 = (s32[1,256,8]{1,2,0:T(8,128)S(1)}, s32[1,256,8]{1,2,0:T(8,128)}, u32[]{:S(2)}) copy-start(s32[1,256,8]{1,2,0:T(8,128)} %param.15) | copy-start | bytes 24580
  76.6 8.6 %collective-permute-start.21 = (bf16[128,1024]{1,0:T(8,128)(2,1)S(1)}, bf16[128,1024]{1,0:T(8,128)(2,1)S(1)}, u32[]{:S(2)}, u32[]{:S(2)}) collective-permute-start(bf16[128,1024]{1,0:T(8,128)(2,1)S(1)} %get-tuple-element.63), channel_id=1, source_target_pairs={{0,3},{1,0},{2,1},{3,2},{4,7},{5,4},{6,5},{7,6},{8,11},{9,8},{10,9... | collective-permute-start | bytes 786440 | tf_op jit(solution)/shard_map/ppermute | solution.py:46
  82.5 12.7 %collective-permute-start.10 = (bf16[256,1024]{1,0:T(8,128)(2,1)}, bf16[256,1024]{1,0:T(8,128)(2,1)}, u32[]{:S(2)}, u32[]{:S(2)}) collective-permute-start(bf16[256,1024]{1,0:T(8,128)(2,1)} %get-tuple-element.55), channel_id=1, source_target_pairs={{0,4},{1,5},{2,6},{3,7},{4,8},{5,9},{6,10},{7,11},{8,12},{9,13},{1... | collective-permute-start | bytes 1572872 | tf_op jit(solution)/shard_map/ppermute | solution.py:46
  82.5 12.7 %collective-permute-start.11 = (bf16[256,1024]{1,0:T(8,128)(2,1)}, bf16[256,1024]{1,0:T(8,128)(2,1)}, u32[]{:S(2)}, u32[]{:S(2)}) collective-permute-start(bf16[256,1024]{1,0:T(8,128)(2,1)} %get-tuple-element.56), channel_id=1, source_target_pairs={{0,12},{1,13},{2,14},{3,15},{4,0},{5,1},{6,2},{7,3},{8,4},{9,5},{1... | collective-permute-start | bytes 1572872 | tf_op jit(solution)/shard_map/ppermute | solution.py:46
  87.8 15.0 %copy-start = (f32[256,1024]{1,0:T(8,128)S(1)}, f32[256,1024]{1,0:T(8,128)}, u32[]{:S(2)}) copy-start(f32[256,1024]{1,0:T(8,128)} %anchor.11) | copy-start | bytes 3145732
  87.8 15.0 %copy-start.3 = (f32[1,256,1024]{2,1,0:T(8,128)S(1)}, f32[1,256,1024]{2,1,0:T(8,128)}, u32[]{:S(2)}) copy-start(f32[1,256,1024]{2,1,0:T(8,128)} %first.5) | copy-start | bytes 3145732
  87.8 15.1 %copy-start.4 = (f32[1,256,1024]{2,1,0:T(8,128)S(1)}, f32[1,256,1024]{2,1,0:T(8,128)}, u32[]{:S(2)}) copy-start(f32[1,256,1024]{2,1,0:T(8,128)} %second.5) | copy-start | bytes 3145732
  87.8 12.4 %collective-permute-start.22 = (bf16[256,1024]{1,0:T(8,128)(2,1)}, bf16[256,1024]{1,0:T(8,128)(2,1)}, u32[]{:S(2)}, u32[]{:S(2)}) collective-permute-start(bf16[256,1024]{1,0:T(8,128)(2,1)} %get-tuple-element.65), channel_id=1, source_target_pairs={{0,1},{1,2},{2,3},{3,0},{4,5},{5,6},{6,7},{7,4},{8,9},{9,10},{10,1... | collective-permute-start | bytes 1572872 | tf_op jit(solution)/shard_map/ppermute | solution.py:46
  87.8 12.4 %collective-permute-start.23 = (bf16[256,1024]{1,0:T(8,128)(2,1)}, bf16[256,1024]{1,0:T(8,128)(2,1)}, u32[]{:S(2)}, u32[]{:S(2)}) collective-permute-start(bf16[256,1024]{1,0:T(8,128)(2,1)} %get-tuple-element.66), channel_id=1, source_target_pairs={{0,3},{1,0},{2,1},{3,2},{4,7},{5,4},{6,5},{7,6},{8,11},{9,8},{10,9... | collective-permute-start | bytes 1572872 | tf_op jit(solution)/shard_map/ppermute | solution.py:46
  95.2 1.2 copy-start.7
  100.2 1.2 copy-start.9
  105.1 15.4 %collective-permute-start.33 = (bf16[128,1024]{1,0:T(8,128)(2,1)S(1)}, bf16[128,1024]{1,0:T(8,128)(2,1)S(1)}, u32[]{:S(2)}, u32[]{:S(2)}) collective-permute-start(bf16[128,1024]{1,0:T(8,128)(2,1)S(1)} %shard_map.125), channel_id=1, source_target_pairs={{0,32},{32,0},{64,96},{96,64},{128,160},{160,128},{192,224},{224,1... | collective-permute-start | bytes 786440 | tf_op jit(solution)/shard_map/ppermute | solution.py:309
  120.5 15.8 %copy-start.2 = (f32[256,1024]{1,0:T(8,128)S(1)}, f32[256,1024]{1,0:T(8,128)}, u32[]{:S(2)}) copy-start(f32[256,1024]{1,0:T(8,128)} %momentum.5) | copy-start | bytes 3145732
  121.1 5.2 %collective-permute-start.34 = (bf16[64,1024]{1,0:T(8,128)(2,1)S(1)}, bf16[64,1024]{1,0:T(8,128)(2,1)S(1)}, u32[]{:S(2)}, u32[]{:S(2)}) collective-permute-start(bf16[64,1024]{1,0:T(8,128)(2,1)S(1)} %get-tuple-element.78), channel_id=1, source_target_pairs={{0,64},{32,96},{64,0},{96,32},{128,192},{160,224},{192,128},{224,1... | collective-permute-start | bytes 393224 | tf_op jit(solution)/shard_map/ppermute | solution.py:309
  126.4 8.8 %collective-permute-start.35 = (bf16[64,1024]{1,0:T(8,128)(2,1)S(1)}, bf16[64,1024]{1,0:T(8,128)(2,1)S(1)}, u32[]{:S(2)}, u32[]{:S(2)}) collective-permute-start(bf16[64,1024]{1,0:T(8,128)(2,1)S(1)} %shard_map.127.refs_0_), channel_id=1, source_target_pairs={{0,128},{32,160},{64,192},{96,224},{128,0},{160,32},{192,64},{224,... | collective-permute-start | bytes 393224 | tf_op jit(solution)/shard_map/ppermute | solution.py:309
  135.2 4.2 %collective-permute-start.36 = (bf16[64,1024]{1,0:T(8,128)(2,1)S(1)}, bf16[64,1024]{1,0:T(8,128)(2,1)S(1)}, u32[]{:S(2)}, u32[]{:S(2)}) collective-permute-start(bf16[64,1024]{1,0:T(8,128)(2,1)S(1)} %shard_map.129.refs_0_), channel_id=1, source_target_pairs={{0,64},{32,96},{64,0},{96,32},{128,192},{160,224},{192,128},{224,1... | collective-permute-start | bytes 393224 | tf_op jit(solution)/shard_map/ppermute | solution.py:309
  135.3 5.9 %collective-permute-start.38 = (bf16[64,1024]{1,0:T(8,128)(2,1)S(1)}, bf16[64,1024]{1,0:T(8,128)(2,1)S(1)}, u32[]{:S(2)}, u32[]{:S(2)}) collective-permute-start(bf16[64,1024]{1,0:T(8,128)(2,1)S(1)} %shard_map.129.refs_0_), channel_id=1, source_target_pairs={{0,32},{32,0},{64,96},{96,64},{128,160},{160,128},{192,224},{224,1... | collective-permute-start | bytes 393224 | tf_op jit(solution)/shard_map/ppermute | solution.py:309
  139.4 3.4 %collective-permute-start.37 = (bf16[64,1024]{1,0:T(8,128)(2,1)S(1)}, bf16[64,1024]{1,0:T(8,128)(2,1)S(1)}, u32[]{:S(2)}, u32[]{:S(2)}) collective-permute-start(bf16[64,1024]{1,0:T(8,128)(2,1)S(1)} %collective-permute-done.36.refs_0_), channel_id=1, source_target_pairs={{0,32},{32,0},{64,96},{96,64},{128,160},{160,128},{192,224},{224,1... | collective-permute-start | bytes 393224 | tf_op jit(solution)/shard_map/ppermute | solution.py:309
  (3 other events, 2.6 us)

commit v5 on v4

--- a/solution.py
+++ b/solution.py
@@ -54,24 +54,19 @@
     return jax.ShapeDtypeStruct(shape, dtype)
 
 
-def pack_kernel(dim, step, spot, ids, cotangents, features, own, ahead, back, ahead_late, back_late, *scratch):
-    held, words, grads, sems = scratch
+def pack_kernel(dim, step, spot, cotangents, features, own, ahead, back, ahead_late, back_late, *scratch):
+    held, grads, sems = scratch
     tokens, shard = own.shape[1:]
     part = tokens // 4
-    small = [
-        pltpu.make_async_copy(ids, words, sems.at[4]),
-        pltpu.make_async_copy(cotangents.at[0, step], grads, sems.at[5]),
-    ]
+    small = pltpu.make_async_copy(cotangents.at[0, step], grads, sems.at[4])
     loads = []
     for q in range(4):
         rows = pl.ds(q * part, part)
         loads.append(pltpu.make_async_copy(features.at[0, step, rows], held.at[rows], sems.at[q]))
-    for load in small + loads:
+    for load in [small] + loads:
         load.start()
-    for load in small:
-        load.wait()
-    live = jnp.sum((words[0, step : step + 1, :] != 0).astype(jnp.int32))
-    alive = lax.broadcasted_iota(jnp.int32, (tokens, shard), 0) < live
+    small.wait()
+    alive = lax.broadcasted_iota(jnp.int32, (tokens, shard), 0) < spot[5 + step]
     for n in range(4):
         block = grads[:, n * shard : (n + 1) * shard]
         block = jnp.where(alive, block, jnp.zeros_like(block))
@@ -98,23 +93,22 @@
             out[slot, rows, :] = held[rows, at]
 
 
-def pack(dim, step, spot, ids, cotangents, features):
+def pack(dim, step, spot, cotangents, features):
     tokens, rows = features.shape[2:]
     shard = rows // (NZ * NX * NY)
     return pl.pallas_call(
         functools.partial(pack_kernel, dim, step),
-        in_specs=[SMEM, HBM, HBM, HBM],
+        in_specs=[SMEM, HBM, HBM],
         out_specs=[VMEM] * 5,
         out_shape=[shape_of((blocks, tokens, shard), features.dtype) for blocks in (12, 10, 10, 6, 6)],
         scratch_shapes=[
             pltpu.VMEM((tokens, rows), features.dtype),
-            pltpu.VMEM(ids.shape, ids.dtype),
             pltpu.VMEM(cotangents.shape[2:], cotangents.dtype),
-            pltpu.SemaphoreType.DMA((6,)),
+            pltpu.SemaphoreType.DMA((5,)),
         ],
         cost_estimate=SHORT,
         compiler_params=PARAMS,
-    )(spot, ids, cotangents, features)
+    )(spot, cotangents, features)
 
 
 def products(turn, pieces):
@@ -154,7 +148,7 @@
 
 
 def nearest_kernel(*refs):
-    pieces, (low, high, own, ahead, back) = refs[:-5], refs[-5:]
+    pieces, (low, high, ahead, back) = refs[:-4], refs[-4:]
     shard, half = pieces[0].shape[2], low.shape[0]
     for n, value in products(1, pieces):
         at = slice(n * shard, (n + 1) * shard)
@@ -164,19 +158,31 @@
         at = slice(n * shard, (n + 1) * shard)
         back[:half, at] = value[:half].astype(back.dtype)
         back[half:, at] = (value[half:] + high[:, at].astype(jnp.float32)).astype(back.dtype)
-    for n, value in products(0, pieces):
-        own[:, n * shard : (n + 1) * shard] = value
 
 
 def nearest(pieces, low, high):
     _, _, shard = pieces[0].shape
-    shape = (shard, 4 * shard)
-    sent = shape_of(shape, pieces[0].dtype)
-    return pl.pallas_call(
-        nearest_kernel, in_specs=[VMEM] * (len(pieces) + 2), out_specs=[VMEM] * 3,
-        out_shape=[shape_of(shape, jnp.float32), sent, sent],
+    out = shape_of((shard, 4 * shard), pieces[0].dtype)
+    return pl.pallas_call(
+        nearest_kernel, in_specs=[VMEM] * (len(pieces) + 2), out_specs=[VMEM] * 2, out_shape=[out] * 2,
         cost_estimate=SHORT, compiler_params=PARAMS,
     )(*pieces, low, high)
+
+
+def itself_kernel(*refs):
+    pieces, out = refs[:-1], refs[-1]
+    shard = pieces[0].shape[2]
+    for n, value in products(0, pieces):
+        out[:, n * shard : (n + 1) * shard] = value
+
+
+def itself(pieces):
+    _, _, shard = pieces[0].shape
+    return pl.pallas_call(
+        itself_kernel, in_specs=[VMEM] * len(pieces), out_specs=VMEM,
+        out_shape=shape_of((shard, 4 * shard), jnp.float32),
+        cost_estimate=SHORT, compiler_params=PARAMS,
+    )(*pieces)
 
 
 def total_kernel(*refs):
@@ -235,7 +241,7 @@
     half = out.shape[0]
     base = lax.rem(spot[2] + turn, CORES) * half
 
-    @pl.loop(0, half, step=16)
+    @pl.loop(0, half, step=16, unroll=2)
     def _(r):
         rows = pl.ds(pl.multiple_of(base + r, 16), 16)
         for c in range(0, anchor.shape[1], 256):
@@ -356,12 +362,13 @@
     place = lax.axis_index("fsdp").astype(jnp.int32)
     z, x, y = place // PLANE, (place // NY) % NX, place % NY
     copy = lax.axis_index("replica").astype(jnp.int32)
-    spot = jnp.stack([x, y, copy % CORES, copy // CORES, z])
+    live = jnp.sum((token_ids[0] != 0).astype(jnp.int32), axis=1)
+    spot = jnp.stack([x, y, copy % CORES, copy // CORES, z, live[0], live[1]])
 
     rings = ("y", "x")
 
-    sent = [pack("y", 0, spot, token_ids, cotangents, activations)]
-    sent.append(pack("x", 1, spot, token_ids, cotangents, activations))
+    sent = [pack("y", 0, spot, cotangents, activations)]
+    sent.append(pack("x", 1, spot, cotangents, activations))
 
     def gather(ahead, back, handed):
         ahead = [along(ring, block, 1) for ring, block in zip(rings, ahead)]
@@ -374,7 +381,9 @@
         parts = []
         for ring, piece in zip(("x", "y"), pieces):
             low, high = opposite(piece)
-            own, ahead, back = nearest(piece, along(ring, low, 1), along(ring, high, -1))
+            low, high = along(ring, low, 1), along(ring, high, -1)
+            own = itself(piece)
+            ahead, back = nearest(piece, low, after(high, own))
             parts.append([own, along(ring, ahead, 1), along(ring, back, -1)])
         return parts
 

time: 145 us -> 143 us (0.986)
  waiting for transfers between devices: 39.7 us -> 33.2 us
  starting transfers between devices: 68.2 us -> 72.3 us
    ppermute x32, waiting for transfers between devices: 28.2 us -> 24.7 us  [along(): return lax.ppermute(block, 'fsdp', fsdp_shift(*shift))]
    ppermute x6, starting transfers between devices: 16.9 us -> 19.9 us  [swap(): return lax.ppermute(block, 'replica', pairs)]
    ppermute x6, waiting for transfers between devices: 11.5 us -> 8.58 us  [swap(): return lax.ppermute(block, 'replica', pairs)]
    pallas_call x0 -> x4, Pallas kernels: none -> 1.81 us  [itself(): pl.pallas_call(itself_kernel, in_specs=[VMEM] * len(pieces), out_specs=VM...]
    unnamed x25 -> x23, local copies, waits for them, and re-layouts: 8.44 us -> 7.75 us
  transfers between devices with their start and end apart: 39 -> 39, of which waited for: 12 -> 15; matrix products, arithmetic and copies ran while one was open for 0% -> 0% of each run, Pallas kernels for 15% -> 15%
where the time goes in v5:
time: 143 us
  starting transfers between devices  72.3 us (51%)
  waiting for transfers between devices  33.2 us (23%)
  Pallas kernels  27.3 us (19%)
  local copies, waits for them, and re-layouts  7.95 us (6%)
    ppermute x32, starting transfers between devices, along(): return lax.ppermute(block, 'fsdp', fsdp_shift(*shift))  45.5 us
    ppermute x32, waiting for transfers between devices, along(): return lax.ppermute(block, 'fsdp', fsdp_shift(*shift))  24.7 us
    ppermute x6, starting transfers between devices, swap(): return lax.ppermute(block, 'replica', pairs)  19.9 us
    ppermute x6, waiting for transfers between devices, swap(): return lax.ppermute(block, 'replica', pairs)  8.58 us
    unnamed x23, local copies, waits for them, and re-layouts  7.75 us
    ppermute x1, starting transfers between devices, on_device(): got = lax.ppermute(theirs, 'fsdp', fsdp_shift(1, 0, 0))  6.91 us
    pallas_call x4, Pallas kernels, nearest(): pl.pallas_call(nearest_kernel, in_specs=[VMEM] * (len(pieces) + 2), out_s...  4.56 us
    pallas_call x3, Pallas kernels, outer_step(): pl.pallas_call(functools.partial(outer_kernel, turns), in_specs=[SMEM] +...  4.38 us
  transfers between devices with their start and end apart: 39, of which 15 were waited for; matrix products, arithmetic and copies ran while one was open for 0% of the time, Pallas kernels for 15%

profile of v5, /device:TPU:1, one launch (start us, length us, event | category | flops | bytes accessed | tf_op | source)
XLA Modules:
  0.0 142.9 jit_solution(71746791397085419)
XLA Ops:
  1.6 2.2 %copy-done.1 = bf16[1,2,128,8192]{3,2,1,0:T(8,128)(2,1)S(1)} copy-done((bf16[1,2,128,8192]{3,2,1,0:T(8,128)(2,1)S(1)}, bf16[1,2,128,8192]{3,2,1,0:T(8,128)(2,1)}, u32[]{:S(2)}) %copy-start.1) | copy-done | bytes 4194328
  4.8 1.1 shard_map.111
  5.9 2.2 %collective-permute-start = (bf16[10,128,256]{2,1,0:T(8,128)(2,1)S(1)}, bf16[10,128,256]{2,1,0:T(8,128)(2,1)S(1)}, u32[]{:S(2)}, u32[]{:S(2)}) collective-permute-start(bf16[10,128,256]{2,1,0:T(8,128)(2,1)S(1)} %get-tuple-element.48), channel_id=1, source_target_pairs={{0,1},{1,2},{2,3},{3,0},{4,5},{5,6},{6,7},{7,4},{8,9},{9,10},{10,1... | collective-permute-start | bytes 1966088 | tf_op jit(solution)/shard_map/ppermute | solution.py:46
  8.1 1.5 %collective-permute-start.1 = (bf16[10,128,256]{2,1,0:T(8,128)(2,1)S(1)}, bf16[10,128,256]{2,1,0:T(8,128)(2,1)S(1)}, u32[]{:S(2)}, u32[]{:S(2)}) collective-permute-start(bf16[10,128,256]{2,1,0:T(8,128)(2,1)S(1)} %get-tuple-element.49), channel_id=1, source_target_pairs={{0,3},{1,0},{2,1},{3,2},{4,7},{5,4},{6,5},{7,6},{8,11},{9,8},{10,9... | collective-permute-start | bytes 1966088 | tf_op jit(solution)/shard_map/ppermute | solution.py:46
  9.7 1.1 shard_map.116
  10.8 1.3 collective-permute-start.12
  12.1 1.5 %collective-permute-start.13 = (bf16[10,128,256]{2,1,0:T(8,128)(2,1)S(1)}, bf16[10,128,256]{2,1,0:T(8,128)(2,1)S(1)}, u32[]{:S(2)}, u32[]{:S(2)}) collective-permute-start(bf16[10,128,256]{2,1,0:T(8,128)(2,1)S(1)} %get-tuple-element.59), channel_id=1, source_target_pairs={{0,12},{1,13},{2,14},{3,15},{4,0},{5,1},{6,2},{7,3},{8,4},{9,5},{1... | collective-permute-start | bytes 1966088 | tf_op jit(solution)/shard_map/ppermute | solution.py:46
  13.5 8.5 %collective-permute-done.refs_1_ = bf16[10,128,256]{2,1,0:T(8,128)(2,1)S(1)} collective-permute-done((bf16[10,128,256]{2,1,0:T(8,128)(2,1)S(1)}, bf16[10,128,256]{2,1,0:T(8,128)(2,1)S(1)}, u32[]{:S(2)}, u32[]{:S(2)}) %collective-permute-start) | collective-permute-done | bytes 655392 | tf_op jit(solution)/shard_map/ppermute | solution.py:46
  22.0 1.6 %collective-permute-start.2 = (bf16[4,128,256]{2,1,0:T(8,128)(2,1)S(1)}, bf16[4,128,256]{2,1,0:T(8,128)(2,1)S(1)}, u32[]{:S(2)}, u32[]{:S(2)}) collective-permute-start(bf16[4,128,256]{2,1,0:T(8,128)(2,1)S(1)} %slice.35), channel_id=1, source_target_pairs={{0,1},{1,2},{2,3},{3,0},{4,5},{5,6},{6,7},{7,4},{8,9},{9,10},{10,1... | collective-permute-start | bytes 786440 | tf_op jit(solution)/shard_map/ppermute | solution.py:46
  23.7 1.7 %collective-permute-start.3 = (bf16[4,128,256]{2,1,0:T(8,128)(2,1)S(1)}, bf16[4,128,256]{2,1,0:T(8,128)(2,1)S(1)}, u32[]{:S(2)}, u32[]{:S(2)}) collective-permute-start(bf16[4,128,256]{2,1,0:T(8,128)(2,1)S(1)} %slice.36), channel_id=1, source_target_pairs={{0,3},{1,0},{2,1},{3,2},{4,7},{5,4},{6,5},{7,6},{8,11},{9,8},{10,9... | collective-permute-start | bytes 786440 | tf_op jit(solution)/shard_map/ppermute | solution.py:46
  25.5 2.5 %collective-permute-start.14 = (bf16[4,128,256]{2,1,0:T(8,128)(2,1)S(1)}, bf16[4,128,256]{2,1,0:T(8,128)(2,1)S(1)}, u32[]{:S(2)}, u32[]{:S(2)}) collective-permute-start(bf16[4,128,256]{2,1,0:T(8,128)(2,1)S(1)} %slice.39), channel_id=1, source_target_pairs={{0,4},{1,5},{2,6},{3,7},{4,8},{5,9},{6,10},{7,11},{8,12},{9,13},{1... | collective-permute-start | bytes 786440 | tf_op jit(solution)/shard_map/ppermute | solution.py:46
  28.0 1.4 collective-permute-start.15
  30.0 4.4 %collective-permute-start.25 = (bf16[128,1024]{1,0:T(8,128)(2,1)S(1)}, bf16[128,1024]{1,0:T(8,128)(2,1)S(1)}, u32[]{:S(2)}, u32[]{:S(2)}) collective-permute-start(bf16[128,1024]{1,0:T(8,128)(2,1)S(1)} %get-tuple-element.68), channel_id=1, source_target_pairs={{0,12},{1,13},{2,14},{3,15},{4,0},{5,1},{6,2},{7,3},{8,4},{9,5},{1... | collective-permute-start | bytes 786440 | tf_op jit(solution)/shard_map/ppermute | solution.py:46
  34.9 2.6 %collective-permute-start.29 = (bf16[128,1024]{1,0:T(8,128)(2,1)S(1)}, bf16[128,1024]{1,0:T(8,128)(2,1)S(1)}, u32[]{:S(2)}, u32[]{:S(2)}) collective-permute-start(bf16[128,1024]{1,0:T(8,128)(2,1)S(1)} %get-tuple-element.73), channel_id=1, source_target_pairs={{0,3},{1,0},{2,1},{3,2},{4,7},{5,4},{6,5},{7,6},{8,11},{9,8},{10,9... | collective-permute-start | bytes 786440 | tf_op jit(solution)/shard_map/ppermute | solution.py:46
  38.4 1.6 %collective-permute-done.25.refs_6_ = bf16[128,1024]{1,0:T(8,128)(2,1)S(1)} collective-permute-done((bf16[128,1024]{1,0:T(8,128)(2,1)S(1)}, bf16[128,1024]{1,0:T(8,128)(2,1)S(1)}, u32[]{:S(2)}, u32[]{:S(2)}) %collective-permute-start.25) | collective-permute-done | bytes 262176 | tf_op jit(solution)/shard_map/ppermute | solution.py:46
  42.5 2.0 %collective-permute-start.27 = (bf16[256,1024]{1,0:T(8,128)(2,1)S(1)}, bf16[256,1024]{1,0:T(8,128)(2,1)S(1)}, u32[]{:S(2)}, u32[]{:S(2)}) collective-permute-start(bf16[256,1024]{1,0:T(8,128)(2,1)S(1)} %get-tuple-element.71), channel_id=1, source_target_pairs={{0,12},{1,13},{2,14},{3,15},{4,0},{5,1},{6,2},{7,3},{8,4},{9,5},{1... | collective-permute-start | bytes 1572872 | tf_op jit(solution)/shard_map/ppermute | solution.py:46
  45.4 2.7 %collective-permute-start.31 = (bf16[256,1024]{1,0:T(8,128)(2,1)S(1)}, bf16[256,1024]{1,0:T(8,128)(2,1)S(1)}, u32[]{:S(2)}, u32[]{:S(2)}) collective-permute-start(bf16[256,1024]{1,0:T(8,128)(2,1)S(1)} %get-tuple-element.76), channel_id=1, source_target_pairs={{0,3},{1,0},{2,1},{3,2},{4,7},{5,4},{6,5},{7,6},{8,11},{9,8},{10,9... | collective-permute-start | bytes 1572872 | tf_op jit(solution)/shard_map/ppermute | solution.py:46
  48.1 4.6 %collective-permute-done.26.refs_1_ = bf16[256,1024]{1,0:T(8,128)(2,1)S(1)} collective-permute-done((bf16[256,1024]{1,0:T(8,128)(2,1)S(1)}, bf16[256,1024]{1,0:T(8,128)(2,1)S(1)}, u32[]{:S(2)}, u32[]{:S(2)}) %collective-permute-start.26) | collective-permute-done | bytes 524320 | tf_op jit(solution)/shard_map/ppermute | solution.py:46
  52.7 2.2 %collective-permute-start.5 = (bf16[6,128,256]{2,1,0:T(8,128)(2,1)S(1)}, bf16[6,128,256]{2,1,0:T(8,128)(2,1)S(1)}, u32[]{:S(2)}, u32[]{:S(2)}) collective-permute-start(bf16[6,128,256]{2,1,0:T(8,128)(2,1)S(1)} %get-tuple-element.51), channel_id=1, source_target_pairs={{0,3},{1,0},{2,1},{3,2},{4,7},{5,4},{6,5},{7,6},{8,11},{9,8},{10,9... | collective-permute-start | bytes 1179656 | tf_op jit(solution)/shard_map/ppermute | solution.py:46
  55.6 2.0 %collective-permute-start.17 = (bf16[6,128,256]{2,1,0:T(8,128)(2,1)S(1)}, bf16[6,128,256]{2,1,0:T(8,128)(2,1)S(1)}, u32[]{:S(2)}, u32[]{:S(2)}) collective-permute-start(bf16[6,128,256]{2,1,0:T(8,128)(2,1)S(1)} %get-tuple-element.61), channel_id=1, source_target_pairs={{0,12},{1,13},{2,14},{3,15},{4,0},{5,1},{6,2},{7,3},{8,4},{9,5},{1... | collective-permute-start | bytes 1179656 | tf_op jit(solution)/shard_map/ppermute | solution.py:46
  57.6 1.4 shard_map.127
  59.0 6.9 %collective-permute-start.32 = (bf16[2,256,1024]{2,1,0:T(8,128)(2,1)}, bf16[2,256,1024]{2,1,0:T(8,128)(2,1)}, u32[]{:S(2)}, u32[]{:S(2)}) collective-permute-start(bf16[2,256,1024]{2,1,0:T(8,128)(2,1)} %shard_map.127), channel_id=1, source_target_pairs={{0,16},{1,17},{2,18},{3,19},{4,20},{5,21},{6,22},{7,23},{8,24},{9,... | collective-permute-start | bytes 3145736 | tf_op jit(solution)/shard_map/ppermute | solution.py:393
  66.0 2.7 %collective-permute-start.7 = (bf16[2,128,256]{2,1,0:T(8,128)(2,1)S(1)}, bf16[2,128,256]{2,1,0:T(8,128)(2,1)S(1)}, u32[]{:S(2)}, u32[]{:S(2)}) collective-permute-start(bf16[2,128,256]{2,1,0:T(8,128)(2,1)S(1)} %slice.38), channel_id=1, source_target_pairs={{0,3},{1,0},{2,1},{3,2},{4,7},{5,4},{6,5},{7,6},{8,11},{9,8},{10,9... | collective-permute-start | bytes 393224 | tf_op jit(solution)/shard_map/ppermute | solution.py:46
  68.9 2.7 %collective-permute-start.19 = (bf16[2,128,256]{2,1,0:T(8,128)(2,1)S(1)}, bf16[2,128,256]{2,1,0:T(8,128)(2,1)S(1)}, u32[]{:S(2)}, u32[]{:S(2)}) collective-permute-start(bf16[2,128,256]{2,1,0:T(8,128)(2,1)S(1)} %slice.42), channel_id=1, source_target_pairs={{0,12},{1,13},{2,14},{3,15},{4,0},{5,1},{6,2},{7,3},{8,4},{9,5},{1... | collective-permute-start | bytes 393224 | tf_op jit(solution)/shard_map/ppermute | solution.py:46
  74.3 2.2 %collective-permute-start.21 = (bf16[128,1024]{1,0:T(8,128)(2,1)S(1)}, bf16[128,1024]{1,0:T(8,128)(2,1)S(1)}, u32[]{:S(2)}, u32[]{:S(2)}) collective-permute-start(bf16[128,1024]{1,0:T(8,128)(2,1)S(1)} %get-tuple-element.63), channel_id=1, source_target_pairs={{0,3},{1,0},{2,1},{3,2},{4,7},{5,4},{6,5},{7,6},{8,11},{9,8},{10,9... | collective-permute-start | bytes 786440 | tf_op jit(solution)/shard_map/ppermute | solution.py:46
  79.8 1.5 %shard_map.114 = (bf16[256,1024]{1,0:T(8,128)(2,1)}, bf16[256,1024]{1,0:T(8,128)(2,1)}) custom-call(bf16[12,128,256]{2,1,0:T(8,128)(2,1)S(1)} %get-tuple-element.47.refs_0_, bf16[10,128,256]{2,1,0:T(8,128)(2,1)S(1)} %collective-permute-done.refs_1_, bf16[10,128,256]{2,1,0:T(8,128)(2,1)S(1)} %collective-permute-done.1.refs_2_, ...), custom_call_target="tpu_custom_call" | custom-call | flops 1 | bytes 1 | tf_op jit(solution)/shard_map/pallas_call | solution.py:166
  81.3 2.7 %collective-permute-start.11 = (bf16[256,1024]{1,0:T(8,128)(2,1)}, bf16[256,1024]{1,0:T(8,128)(2,1)}, u32[]{:S(2)}, u32[]{:S(2)}) collective-permute-start(bf16[256,1024]{1,0:T(8,128)(2,1)} %get-tuple-element.56), channel_id=1, source_target_pairs={{0,12},{1,13},{2,14},{3,15},{4,0},{5,1},{6,2},{7,3},{8,4},{9,5},{1... | collective-permute-start | bytes 1572872 | tf_op jit(solution)/shard_map/ppermute | solution.py:46
  84.8 1.6 %shard_map.119 = (bf16[256,1024]{1,0:T(8,128)(2,1)}, bf16[256,1024]{1,0:T(8,128)(2,1)}) custom-call(bf16[12,128,256]{2,1,0:T(8,128)(2,1)S(1)} %get-tuple-element.57.refs_0_, bf16[10,128,256]{2,1,0:T(8,128)(2,1)S(1)} %collective-permute-done.12.refs_1_, bf16[10,128,256]{2,1,0:T(8,128)(2,1)S(1)} %collective-permute-done.13.refs_2_, ...), custom_call_target="tpu_custom_call" | custom-call | flops 1 | bytes 1 | tf_op jit(solution)/shard_map/pallas_call | solution.py:166
  86.3 2.7 %collective-permute-start.23 = (bf16[256,1024]{1,0:T(8,128)(2,1)}, bf16[256,1024]{1,0:T(8,128)(2,1)}, u32[]{:S(2)}, u32[]{:S(2)}) collective-permute-start(bf16[256,1024]{1,0:T(8,128)(2,1)} %get-tuple-element.66), channel_id=1, source_target_pairs={{0,3},{1,0},{2,1},{3,2},{4,7},{5,4},{6,5},{7,6},{8,11},{9,8},{10,9... | collective-permute-start | bytes 1572872 | tf_op jit(solution)/shard_map/ppermute | solution.py:46
  89.1 4.3 %collective-permute-done.10.refs_1_ = bf16[256,1024]{1,0:T(8,128)(2,1)} collective-permute-done((bf16[256,1024]{1,0:T(8,128)(2,1)}, bf16[256,1024]{1,0:T(8,128)(2,1)}, u32[]{:S(2)}, u32[]{:S(2)}) %collective-permute-start.10) | collective-permute-done | bytes 524320 | tf_op jit(solution)/shard_map/ppermute | solution.py:46
  93.5 1.2 copy-done.8
  94.7 1.4 shard_map.115.own_a
  96.1 2.6 %collective-permute-done.22.refs_1_ = bf16[256,1024]{1,0:T(8,128)(2,1)} collective-permute-done((bf16[256,1024]{1,0:T(8,128)(2,1)}, bf16[256,1024]{1,0:T(8,128)(2,1)}, u32[]{:S(2)}, u32[]{:S(2)}) %collective-permute-start.22) | collective-permute-done | bytes 524320 | tf_op jit(solution)/shard_map/ppermute | solution.py:46
  98.7 1.2 copy-done.6
  100.0 1.4 shard_map.120.own_b
  101.4 2.2 %shard_map.129 = bf16[128,1024]{1,0:T(8,128)(2,1)S(1)} custom-call(s32[7]{0:T(128)S(1)} %stack.23.spot, f32[256,1024]{1,0:T(8,128)S(1)} %copy-done, f32[1,256,1024]{2,1,0:T(8,128)S(1)} %copy-done.3, f32[1,256,1024]{2,1,0:T(8,128)S(1)} %copy-done.4, f32[1,256,1024]{2,1,0:T(8,128)S(1)} %shard_map.115.own_a, f32[1,256,1024]{2,1,0:T(8,128)S(1)} %shard_map.120.own_b, ...), custom_call_target="tpu_custom_call" | custom-call | flops 1 | bytes 1 | tf_op jit(solution)/shard_map/pallas_call | solution.py:265
  103.6 12.9 %collective-permute-start.33 = (bf16[128,1024]{1,0:T(8,128)(2,1)S(1)}, bf16[128,1024]{1,0:T(8,128)(2,1)S(1)}, u32[]{:S(2)}, u32[]{:S(2)}) collective-permute-start(bf16[128,1024]{1,0:T(8,128)(2,1)S(1)} %shard_map.129), channel_id=1, source_target_pairs={{0,32},{32,0},{64,96},{96,64},{128,160},{160,128},{192,224},{224,1... | collective-permute-start | bytes 786440 | tf_op jit(solution)/shard_map/ppermute | solution.py:315
  116.5 2.2 %shard_map.128.ours = bf16[128,1024]{1,0:T(8,128)(2,1)S(1)} custom-call(s32[7]{0:T(128)S(1)} %stack.23.spot, f32[256,1024]{1,0:T(8,128)S(1)} %copy-done, f32[1,256,1024]{2,1,0:T(8,128)S(1)} %copy-done.3, f32[1,256,1024]{2,1,0:T(8,128)S(1)} %copy-done.4, f32[1,256,1024]{2,1,0:T(8,128)S(1)} %shard_map.115.own_a, f32[1,256,1024]{2,1,0:T(8,128)S(1)} %shard_map.120.own_b, ...), custom_call_target="tpu_custom_call" | custom-call | flops 1 | bytes 1 | tf_op jit(solution)/shard_map/pallas_call | solution.py:265
  120.3 4.2 %collective-permute-done.34.refs_1_ = bf16[64,1024]{1,0:T(8,128)(2,1)S(1)} collective-permute-done((bf16[64,1024]{1,0:T(8,128)(2,1)S(1)}, bf16[64,1024]{1,0:T(8,128)(2,1)S(1)}, u32[]{:S(2)}, u32[]{:S(2)}) %collective-permute-start.34) | collective-permute-done | bytes 131104 | tf_op jit(solution)/shard_map/ppermute | solution.py:315
  124.5 2.7 %collective-permute-start.35 = (bf16[64,1024]{1,0:T(8,128)(2,1)S(1)}, bf16[64,1024]{1,0:T(8,128)(2,1)S(1)}, u32[]{:S(2)}, u32[]{:S(2)}) collective-permute-start(bf16[64,1024]{1,0:T(8,128)(2,1)S(1)} %shard_map.131.refs_0_), channel_id=1, source_target_pairs={{0,128},{32,160},{64,192},{96,224},{128,0},{160,32},{192,64},{224,... | collective-permute-start | bytes 393224 | tf_op jit(solution)/shard_map/ppermute | solution.py:315
  127.3 3.3 %shard_map.132 = (f32[1,256,1024]{2,1,0:T(8,128)}, f32[1,256,1024]{2,1,0:T(8,128)}) custom-call(f32[256,1024]{1,0:T(8,128)S(1)} %copy-done, f32[1,256,1024]{2,1,0:T(8,128)S(1)} %copy-done.3, f32[1,256,1024]{2,1,0:T(8,128)S(1)} %copy-done.4, f32[1,256,1024]{2,1,0:T(8,128)S(1)} %shard_map.115.own_a, f32[1,256,1024]{2,1,0:T(8,128)S(1)} %shard_map.120.own_b, ...), custom_call_target="tpu_custom_call" | custom-call | flops 1 | bytes 1 | tf_op jit(solution)/shard_map/pallas_call | solution.py:288
  130.6 3.1 %collective-permute-done.35.refs_1_ = bf16[64,1024]{1,0:T(8,128)(2,1)S(1)} collective-permute-done((bf16[64,1024]{1,0:T(8,128)(2,1)S(1)}, bf16[64,1024]{1,0:T(8,128)(2,1)S(1)}, u32[]{:S(2)}, u32[]{:S(2)}) %collective-permute-start.35) | collective-permute-done | bytes 131104 | tf_op jit(solution)/shard_map/ppermute | solution.py:315
  133.8 1.1 collective-permute-start.38
  134.9 1.4 shard_map.134
  136.3 1.3 collective-permute-done.36.refs_0_
  137.6 2.1 %collective-permute-start.37 = (bf16[64,1024]{1,0:T(8,128)(2,1)S(1)}, bf16[64,1024]{1,0:T(8,128)(2,1)S(1)}, u32[]{:S(2)}, u32[]{:S(2)}) collective-permute-start(bf16[64,1024]{1,0:T(8,128)(2,1)S(1)} %collective-permute-done.36.refs_0_), channel_id=1, source_target_pairs={{0,32},{32,0},{64,96},{96,64},{128,160},{160,128},{192,224},{224,1... | collective-permute-start | bytes 393224 | tf_op jit(solution)/shard_map/ppermute | solution.py:315
  139.7 1.6 %shard_map.135 = (f32[256,1024]{1,0:T(8,128)}, f32[256,1024]{1,0:T(8,128)}) custom-call(s32[7]{0:T(128)S(1)} %stack.23.spot, f32[256,1024]{1,0:T(8,128)S(1)} %copy-done, f32[256,1024]{1,0:T(8,128)S(1)} %copy-done.2, bf16[64,1024]{1,0:T(8,128)(2,1)S(1)} %collective-permute-done.36.refs_0_, ...), custom_call_target="tpu_custom_call", output_to_operand_aliasing={{0}: (5, {}), {1}: (6, {})} | custom-call | flops 1 | bytes 1 | tf_op jit(solution)/shard_map/pallas_call | solution.py:343
  141.3 1.4 shard_map.136
  (89 shorter events, 17.0 us)
Async XLA Ops:
  1.6 2.2 %copy-start.1 = (bf16[1,2,128,8192]{3,2,1,0:T(8,128)(2,1)S(1)}, bf16[1,2,128,8192]{3,2,1,0:T(8,128)(2,1)}, u32[]{:S(2)}) copy-start(bf16[1,2,128,8192]{3,2,1,0:T(8,128)(2,1)} %features.3) | copy-start | bytes 12582916
  3.8 1.0 copy-start.9
  5.9 16.1 %collective-permute-start = (bf16[10,128,256]{2,1,0:T(8,128)(2,1)S(1)}, bf16[10,128,256]{2,1,0:T(8,128)(2,1)S(1)}, u32[]{:S(2)}, u32[]{:S(2)}) collective-permute-start(bf16[10,128,256]{2,1,0:T(8,128)(2,1)S(1)} %get-tuple-element.48), channel_id=1, source_target_pairs={{0,1},{1,2},{2,3},{3,0},{4,5},{5,6},{6,7},{7,4},{8,9},{9,10},{10,1... | collective-permute-start | bytes 1966088 | tf_op jit(solution)/shard_map/ppermute | solution.py:46
  8.1 15.5 %collective-permute-start.1 = (bf16[10,128,256]{2,1,0:T(8,128)(2,1)S(1)}, bf16[10,128,256]{2,1,0:T(8,128)(2,1)S(1)}, u32[]{:S(2)}, u32[]{:S(2)}) collective-permute-start(bf16[10,128,256]{2,1,0:T(8,128)(2,1)S(1)} %get-tuple-element.49), channel_id=1, source_target_pairs={{0,3},{1,0},{2,1},{3,2},{4,7},{5,4},{6,5},{7,6},{8,11},{9,8},{10,9... | collective-permute-start | bytes 1966088 | tf_op jit(solution)/shard_map/ppermute | solution.py:46
  10.8 14.7 %collective-permute-start.12 = (bf16[10,128,256]{2,1,0:T(8,128)(2,1)S(1)}, bf16[10,128,256]{2,1,0:T(8,128)(2,1)S(1)}, u32[]{:S(2)}, u32[]{:S(2)}) collective-permute-start(bf16[10,128,256]{2,1,0:T(8,128)(2,1)S(1)} %get-tuple-element.58), channel_id=1, source_target_pairs={{0,4},{1,5},{2,6},{3,7},{4,8},{5,9},{6,10},{7,11},{8,12},{9,13},{1... | collective-permute-start | bytes 1966088 | tf_op jit(solution)/shard_map/ppermute | solution.py:46
  12.1 15.9 %collective-permute-start.13 = (bf16[10,128,256]{2,1,0:T(8,128)(2,1)S(1)}, bf16[10,128,256]{2,1,0:T(8,128)(2,1)S(1)}, u32[]{:S(2)}, u32[]{:S(2)}) collective-permute-start(bf16[10,128,256]{2,1,0:T(8,128)(2,1)S(1)} %get-tuple-element.59), channel_id=1, source_target_pairs={{0,12},{1,13},{2,14},{3,15},{4,0},{5,1},{6,2},{7,3},{8,4},{9,5},{1... | collective-permute-start | bytes 1966088 | tf_op jit(solution)/shard_map/ppermute | solution.py:46
  22.0 7.4 %collective-permute-start.2 = (bf16[4,128,256]{2,1,0:T(8,128)(2,1)S(1)}, bf16[4,128,256]{2,1,0:T(8,128)(2,1)S(1)}, u32[]{:S(2)}, u32[]{:S(2)}) collective-permute-start(bf16[4,128,256]{2,1,0:T(8,128)(2,1)S(1)} %slice.35), channel_id=1, source_target_pairs={{0,1},{1,2},{2,3},{3,0},{4,5},{5,6},{6,7},{7,4},{8,9},{9,10},{10,1... | collective-permute-start | bytes 786440 | tf_op jit(solution)/shard_map/ppermute | solution.py:46
  23.7 5.9 %collective-permute-start.3 = (bf16[4,128,256]{2,1,0:T(8,128)(2,1)S(1)}, bf16[4,128,256]{2,1,0:T(8,128)(2,1)S(1)}, u32[]{:S(2)}, u32[]{:S(2)}) collective-permute-start(bf16[4,128,256]{2,1,0:T(8,128)(2,1)S(1)} %slice.36), channel_id=1, source_target_pairs={{0,3},{1,0},{2,1},{3,2},{4,7},{5,4},{6,5},{7,6},{8,11},{9,8},{10,9... | collective-permute-start | bytes 786440 | tf_op jit(solution)/shard_map/ppermute | solution.py:46
  25.5 9.0 %collective-permute-start.14 = (bf16[4,128,256]{2,1,0:T(8,128)(2,1)S(1)}, bf16[4,128,256]{2,1,0:T(8,128)(2,1)S(1)}, u32[]{:S(2)}, u32[]{:S(2)}) collective-permute-start(bf16[4,128,256]{2,1,0:T(8,128)(2,1)S(1)} %slice.39), channel_id=1, source_target_pairs={{0,4},{1,5},{2,6},{3,7},{4,8},{5,9},{6,10},{7,11},{8,12},{9,13},{1... | collective-permute-start | bytes 786440 | tf_op jit(solution)/shard_map/ppermute | solution.py:46
  28.0 6.4 %collective-permute-start.15 = (bf16[4,128,256]{2,1,0:T(8,128)(2,1)S(1)}, bf16[4,128,256]{2,1,0:T(8,128)(2,1)S(1)}, u32[]{:S(2)}, u32[]{:S(2)}) collective-permute-start(bf16[4,128,256]{2,1,0:T(8,128)(2,1)S(1)} %slice.40), channel_id=1, source_target_pairs={{0,12},{1,13},{2,14},{3,15},{4,0},{5,1},{6,2},{7,3},{8,4},{9,5},{1... | collective-permute-start | bytes 786440 | tf_op jit(solution)/shard_map/ppermute | solution.py:46
  30.0 10.0 %collective-permute-start.25 = (bf16[128,1024]{1,0:T(8,128)(2,1)S(1)}, bf16[128,1024]{1,0:T(8,128)(2,1)S(1)}, u32[]{:S(2)}, u32[]{:S(2)}) collective-permute-start(bf16[128,1024]{1,0:T(8,128)(2,1)S(1)} %get-tuple-element.68), channel_id=1, source_target_pairs={{0,12},{1,13},{2,14},{3,15},{4,0},{5,1},{6,2},{7,3},{8,4},{9,5},{1... | collective-permute-start | bytes 786440 | tf_op jit(solution)/shard_map/ppermute | solution.py:46
  34.4 6.4 %collective-permute-start.24 = (bf16[128,1024]{1,0:T(8,128)(2,1)S(1)}, bf16[128,1024]{1,0:T(8,128)(2,1)S(1)}, u32[]{:S(2)}, u32[]{:S(2)}) collective-permute-start(bf16[128,1024]{1,0:T(8,128)(2,1)S(1)} %get-tuple-element.67), channel_id=1, source_target_pairs={{0,4},{1,5},{2,6},{3,7},{4,8},{5,9},{6,10},{7,11},{8,12},{9,13},{1... | collective-permute-start | bytes 786440 | tf_op jit(solution)/shard_map/ppermute | solution.py:46
  34.9 9.6 %collective-permute-start.29 = (bf16[128,1024]{1,0:T(8,128)(2,1)S(1)}, bf16[128,1024]{1,0:T(8,128)(2,1)S(1)}, u32[]{:S(2)}, u32[]{:S(2)}) collective-permute-start(bf16[128,1024]{1,0:T(8,128)(2,1)S(1)} %get-tuple-element.73), channel_id=1, source_target_pairs={{0,3},{1,0},{2,1},{3,2},{4,7},{5,4},{6,5},{7,6},{8,11},{9,8},{10,9... | collective-permute-start | bytes 786440 | tf_op jit(solution)/shard_map/ppermute | solution.py:46
  37.5 7.1 %collective-permute-start.28 = (bf16[128,1024]{1,0:T(8,128)(2,1)S(1)}, bf16[128,1024]{1,0:T(8,128)(2,1)S(1)}, u32[]{:S(2)}, u32[]{:S(2)}) collective-permute-start(bf16[128,1024]{1,0:T(8,128)(2,1)S(1)} %get-tuple-element.72), channel_id=1, source_target_pairs={{0,1},{1,2},{2,3},{3,0},{4,5},{5,6},{6,7},{7,4},{8,9},{9,10},{10,1... | collective-permute-start | bytes 786440 | tf_op jit(solution)/shard_map/ppermute | solution.py:46
  41.6 11.1 %collective-permute-start.26 = (bf16[256,1024]{1,0:T(8,128)(2,1)S(1)}, bf16[256,1024]{1,0:T(8,128)(2,1)S(1)}, u32[]{:S(2)}, u32[]{:S(2)}) collective-permute-start(bf16[256,1024]{1,0:T(8,128)(2,1)S(1)} %get-tuple-element.70), channel_id=1, source_target_pairs={{0,4},{1,5},{2,6},{3,7},{4,8},{5,9},{6,10},{7,11},{8,12},{9,13},{1... | collective-permute-start | bytes 1572872 | tf_op jit(solution)/shard_map/ppermute | solution.py:46
  42.5 12.4 %collective-permute-start.27 = (bf16[256,1024]{1,0:T(8,128)(2,1)S(1)}, bf16[256,1024]{1,0:T(8,128)(2,1)S(1)}, u32[]{:S(2)}, u32[]{:S(2)}) collective-permute-start(bf16[256,1024]{1,0:T(8,128)(2,1)S(1)} %get-tuple-element.71), channel_id=1, source_target_pairs={{0,12},{1,13},{2,14},{3,15},{4,0},{5,1},{6,2},{7,3},{8,4},{9,5},{1... | collective-permute-start | bytes 1572872 | tf_op jit(solution)/shard_map/ppermute | solution.py:46
  45.3 10.3 %collective-permute-start.30 = (bf16[256,1024]{1,0:T(8,128)(2,1)S(1)}, bf16[256,1024]{1,0:T(8,128)(2,1)S(1)}, u32[]{:S(2)}, u32[]{:S(2)}) collective-permute-start(bf16[256,1024]{1,0:T(8,128)(2,1)S(1)} %get-tuple-element.75), channel_id=1, source_target_pairs={{0,1},{1,2},{2,3},{3,0},{4,5},{5,6},{6,7},{7,4},{8,9},{9,10},{10,1... | collective-permute-start | bytes 1572872 | tf_op jit(solution)/shard_map/ppermute | solution.py:46
  45.4 12.2 %collective-permute-start.31 = (bf16[256,1024]{1,0:T(8,128)(2,1)S(1)}, bf16[256,1024]{1,0:T(8,128)(2,1)S(1)}, u32[]{:S(2)}, u32[]{:S(2)}) collective-permute-start(bf16[256,1024]{1,0:T(8,128)(2,1)S(1)} %get-tuple-element.76), channel_id=1, source_target_pairs={{0,3},{1,0},{2,1},{3,2},{4,7},{5,4},{6,5},{7,6},{8,11},{9,8},{10,9... | collective-permute-start | bytes 1572872 | tf_op jit(solution)/shard_map/ppermute | solution.py:46
  48.1 17.8 %collective-permute-start.4 = (bf16[6,128,256]{2,1,0:T(8,128)(2,1)S(1)}, bf16[6,128,256]{2,1,0:T(8,128)(2,1)S(1)}, u32[]{:S(2)}, u32[]{:S(2)}) collective-permute-start(bf16[6,128,256]{2,1,0:T(8,128)(2,1)S(1)} %get-tuple-element.50), channel_id=1, source_target_pairs={{0,1},{1,2},{2,3},{3,0},{4,5},{5,6},{6,7},{7,4},{8,9},{9,10},{10,1... | collective-permute-start | bytes 1179656 | tf_op jit(solution)/shard_map/ppermute | solution.py:46
  52.7 13.3 %collective-permute-start.5 = (bf16[6,128,256]{2,1,0:T(8,128)(2,1)S(1)}, bf16[6,128,256]{2,1,0:T(8,128)(2,1)S(1)}, u32[]{:S(2)}, u32[]{:S(2)}) collective-permute-start(bf16[6,128,256]{2,1,0:T(8,128)(2,1)S(1)} %get-tuple-element.51), channel_id=1, source_target_pairs={{0,3},{1,0},{2,1},{3,2},{4,7},{5,4},{6,5},{7,6},{8,11},{9,8},{10,9... | collective-permute-start | bytes 1179656 | tf_op jit(solution)/shard_map/ppermute | solution.py:46
  54.9 13.8 %collective-permute-start.16 = (bf16[6,128,256]{2,1,0:T(8,128)(2,1)S(1)}, bf16[6,128,256]{2,1,0:T(8,128)(2,1)S(1)}, u32[]{:S(2)}, u32[]{:S(2)}) collective-permute-start(bf16[6,128,256]{2,1,0:T(8,128)(2,1)S(1)} %get-tuple-element.60), channel_id=1, source_target_pairs={{0,4},{1,5},{2,6},{3,7},{4,8},{5,9},{6,10},{7,11},{8,12},{9,13},{1... | collective-permute-start | bytes 1179656 | tf_op jit(solution)/shard_map/ppermute | solution.py:46
  55.6 13.2 %collective-permute-start.17 = (bf16[6,128,256]{2,1,0:T(8,128)(2,1)S(1)}, bf16[6,128,256]{2,1,0:T(8,128)(2,1)S(1)}, u32[]{:S(2)}, u32[]{:S(2)}) collective-permute-start(bf16[6,128,256]{2,1,0:T(8,128)(2,1)S(1)} %get-tuple-element.61), channel_id=1, source_target_pairs={{0,12},{1,13},{2,14},{3,15},{4,0},{5,1},{6,2},{7,3},{8,4},{9,5},{1... | collective-permute-start | bytes 1179656 | tf_op jit(solution)/shard_map/ppermute | solution.py:46
  59.0 42.4 %collective-permute-start.32 = (bf16[2,256,1024]{2,1,0:T(8,128)(2,1)}, bf16[2,256,1024]{2,1,0:T(8,128)(2,1)}, u32[]{:S(2)}, u32[]{:S(2)}) collective-permute-start(bf16[2,256,1024]{2,1,0:T(8,128)(2,1)} %shard_map.127), channel_id=1, source_target_pairs={{0,16},{1,17},{2,18},{3,19},{4,20},{5,21},{6,22},{7,23},{8,24},{9,... | collective-permute-start | bytes 3145736 | tf_op jit(solution)/shard_map/ppermute | solution.py:393
  65.9 5.7 %collective-permute-start.6 = (bf16[2,128,256]{2,1,0:T(8,128)(2,1)S(1)}, bf16[2,128,256]{2,1,0:T(8,128)(2,1)S(1)}, u32[]{:S(2)}, u32[]{:S(2)}) collective-permute-start(bf16[2,128,256]{2,1,0:T(8,128)(2,1)S(1)} %slice.37), channel_id=1, source_target_pairs={{0,1},{1,2},{2,3},{3,0},{4,5},{5,6},{6,7},{7,4},{8,9},{9,10},{10,1... | collective-permute-start | bytes 393224 | tf_op jit(solution)/shard_map/ppermute | solution.py:46
  66.0 5.6 %collective-permute-start.7 = (bf16[2,128,256]{2,1,0:T(8,128)(2,1)S(1)}, bf16[2,128,256]{2,1,0:T(8,128)(2,1)S(1)}, u32[]{:S(2)}, u32[]{:S(2)}) collective-permute-start(bf16[2,128,256]{2,1,0:T(8,128)(2,1)S(1)} %slice.38), channel_id=1, source_target_pairs={{0,3},{1,0},{2,1},{3,2},{4,7},{5,4},{6,5},{7,6},{8,11},{9,8},{10,9... | collective-permute-start | bytes 393224 | tf_op jit(solution)/shard_map/ppermute | solution.py:46
  68.7 5.1 %collective-permute-start.18 = (bf16[2,128,256]{2,1,0:T(8,128)(2,1)S(1)}, bf16[2,128,256]{2,1,0:T(8,128)(2,1)S(1)}, u32[]{:S(2)}, u32[]{:S(2)}) collective-permute-start(bf16[2,128,256]{2,1,0:T(8,128)(2,1)S(1)} %slice.41), channel_id=1, source_target_pairs={{0,4},{1,5},{2,6},{3,7},{4,8},{5,9},{6,10},{7,11},{8,12},{9,13},{1... | collective-permute-start | bytes 393224 | tf_op jit(solution)/shard_map/ppermute | solution.py:46
  68.9 5.0 %collective-permute-start.19 = (bf16[2,128,256]{2,1,0:T(8,128)(2,1)S(1)}, bf16[2,128,256]{2,1,0:T(8,128)(2,1)S(1)}, u32[]{:S(2)}, u32[]{:S(2)}) collective-permute-start(bf16[2,128,256]{2,1,0:T(8,128)(2,1)S(1)} %slice.42), channel_id=1, source_target_pairs={{0,12},{1,13},{2,14},{3,15},{4,0},{5,1},{6,2},{7,3},{8,4},{9,5},{1... | collective-permute-start | bytes 393224 | tf_op jit(solution)/shard_map/ppermute | solution.py:46
  72.1 7.3 %collective-permute-start.9 = (bf16[128,1024]{1,0:T(8,128)(2,1)S(1)}, bf16[128,1024]{1,0:T(8,128)(2,1)S(1)}, u32[]{:S(2)}, u32[]{:S(2)}) collective-permute-start(bf16[128,1024]{1,0:T(8,128)(2,1)S(1)} %get-tuple-element.53), channel_id=1, source_target_pairs={{0,12},{1,13},{2,14},{3,15},{4,0},{5,1},{6,2},{7,3},{8,4},{9,5},{1... | collective-permute-start | bytes 786440 | tf_op jit(solution)/shard_map/ppermute | solution.py:46
  72.9 6.8 %collective-permute-start.8 = (bf16[128,1024]{1,0:T(8,128)(2,1)S(1)}, bf16[128,1024]{1,0:T(8,128)(2,1)S(1)}, u32[]{:S(2)}, u32[]{:S(2)}) collective-permute-start(bf16[128,1024]{1,0:T(8,128)(2,1)S(1)} %get-tuple-element.52), channel_id=1, source_target_pairs={{0,4},{1,5},{2,6},{3,7},{4,8},{5,9},{6,10},{7,11},{8,12},{9,13},{1... | collective-permute-start | bytes 786440 | tf_op jit(solution)/shard_map/ppermute | solution.py:46
  74.3 9.7 %collective-permute-start.21 = (bf16[128,1024]{1,0:T(8,128)(2,1)S(1)}, bf16[128,1024]{1,0:T(8,128)(2,1)S(1)}, u32[]{:S(2)}, u32[]{:S(2)}) collective-permute-start(bf16[128,1024]{1,0:T(8,128)(2,1)S(1)} %get-tuple-element.63), channel_id=1, source_target_pairs={{0,3},{1,0},{2,1},{3,2},{4,7},{5,4},{6,5},{7,6},{8,11},{9,8},{10,9... | collective-permute-start | bytes 786440 | tf_op jit(solution)/shard_map/ppermute | solution.py:46
  76.5 8.2 %collective-permute-start.20 = (bf16[128,1024]{1,0:T(8,128)(2,1)S(1)}, bf16[128,1024]{1,0:T(8,128)(2,1)S(1)}, u32[]{:S(2)}, u32[]{:S(2)}) collective-permute-start(bf16[128,1024]{1,0:T(8,128)(2,1)S(1)} %get-tuple-element.62), channel_id=1, source_target_pairs={{0,1},{1,2},{2,3},{3,0},{4,5},{5,6},{6,7},{7,4},{8,9},{9,10},{10,1... | collective-permute-start | bytes 786440 | tf_op jit(solution)/shard_map/ppermute | solution.py:46
  79.4 9.6 %copy-start.10 = (s32[1,256,8]{1,2,0:T(8,128)S(1)}, s32[1,256,8]{1,2,0:T(8,128)}, u32[]{:S(2)}) copy-start(s32[1,256,8]{1,2,0:T(8,128)} %param.15) | copy-start | bytes 24580
  81.3 12.1 %collective-permute-start.10 = (bf16[256,1024]{1,0:T(8,128)(2,1)}, bf16[256,1024]{1,0:T(8,128)(2,1)}, u32[]{:S(2)}, u32[]{:S(2)}) collective-permute-start(bf16[256,1024]{1,0:T(8,128)(2,1)} %get-tuple-element.55), channel_id=1, source_target_pairs={{0,4},{1,5},{2,6},{3,7},{4,8},{5,9},{6,10},{7,11},{8,12},{9,13},{1... | collective-permute-start | bytes 1572872 | tf_op jit(solution)/shard_map/ppermute | solution.py:46
  81.3 12.2 %collective-permute-start.11 = (bf16[256,1024]{1,0:T(8,128)(2,1)}, bf16[256,1024]{1,0:T(8,128)(2,1)}, u32[]{:S(2)}, u32[]{:S(2)}) collective-permute-start(bf16[256,1024]{1,0:T(8,128)(2,1)} %get-tuple-element.56), channel_id=1, source_target_pairs={{0,12},{1,13},{2,14},{3,15},{4,0},{5,1},{6,2},{7,3},{8,4},{9,5},{1... | collective-permute-start | bytes 1572872 | tf_op jit(solution)/shard_map/ppermute | solution.py:46
  86.3 15.1 %copy-start = (f32[256,1024]{1,0:T(8,128)S(1)}, f32[256,1024]{1,0:T(8,128)}, u32[]{:S(2)}) copy-start(f32[256,1024]{1,0:T(8,128)} %anchor.11) | copy-start | bytes 3145732
  86.3 15.1 %copy-start.3 = (f32[1,256,1024]{2,1,0:T(8,128)S(1)}, f32[1,256,1024]{2,1,0:T(8,128)}, u32[]{:S(2)}) copy-start(f32[1,256,1024]{2,1,0:T(8,128)} %first.5) | copy-start | bytes 3145732
  86.3 15.1 %copy-start.4 = (f32[1,256,1024]{2,1,0:T(8,128)S(1)}, f32[1,256,1024]{2,1,0:T(8,128)}, u32[]{:S(2)}) copy-start(f32[1,256,1024]{2,1,0:T(8,128)} %second.5) | copy-start | bytes 3145732
  86.3 12.4 %collective-permute-start.22 = (bf16[256,1024]{1,0:T(8,128)(2,1)}, bf16[256,1024]{1,0:T(8,128)(2,1)}, u32[]{:S(2)}, u32[]{:S(2)}) collective-permute-start(bf16[256,1024]{1,0:T(8,128)(2,1)} %get-tuple-element.65), channel_id=1, source_target_pairs={{0,1},{1,2},{2,3},{3,0},{4,5},{5,6},{6,7},{7,4},{8,9},{9,10},{10,1... | collective-permute-start | bytes 1572872 | tf_op jit(solution)/shard_map/ppermute | solution.py:46
  86.3 12.4 %collective-permute-start.23 = (bf16[256,1024]{1,0:T(8,128)(2,1)}, bf16[256,1024]{1,0:T(8,128)(2,1)}, u32[]{:S(2)}, u32[]{:S(2)}) collective-permute-start(bf16[256,1024]{1,0:T(8,128)(2,1)} %get-tuple-element.66), channel_id=1, source_target_pairs={{0,3},{1,0},{2,1},{3,2},{4,7},{5,4},{6,5},{7,6},{8,11},{9,8},{10,9... | collective-permute-start | bytes 1572872 | tf_op jit(solution)/shard_map/ppermute | solution.py:46
  93.5 1.2 copy-start.8
  98.7 1.2 copy-start.6
  103.6 15.1 %collective-permute-start.33 = (bf16[128,1024]{1,0:T(8,128)(2,1)S(1)}, bf16[128,1024]{1,0:T(8,128)(2,1)S(1)}, u32[]{:S(2)}, u32[]{:S(2)}) collective-permute-start(bf16[128,1024]{1,0:T(8,128)(2,1)S(1)} %shard_map.129), channel_id=1, source_target_pairs={{0,32},{32,0},{64,96},{96,64},{128,160},{160,128},{192,224},{224,1... | collective-permute-start | bytes 786440 | tf_op jit(solution)/shard_map/ppermute | solution.py:315
  118.7 16.2 %copy-start.2 = (f32[256,1024]{1,0:T(8,128)S(1)}, f32[256,1024]{1,0:T(8,128)}, u32[]{:S(2)}) copy-start(f32[256,1024]{1,0:T(8,128)} %momentum.5) | copy-start | bytes 3145732
  119.3 5.2 %collective-permute-start.34 = (bf16[64,1024]{1,0:T(8,128)(2,1)S(1)}, bf16[64,1024]{1,0:T(8,128)(2,1)S(1)}, u32[]{:S(2)}, u32[]{:S(2)}) collective-permute-start(bf16[64,1024]{1,0:T(8,128)(2,1)S(1)} %get-tuple-element.78), channel_id=1, source_target_pairs={{0,64},{32,96},{64,0},{96,32},{128,192},{160,224},{192,128},{224,1... | collective-permute-start | bytes 393224 | tf_op jit(solution)/shard_map/ppermute | solution.py:315
  124.5 9.1 %collective-permute-start.35 = (bf16[64,1024]{1,0:T(8,128)(2,1)S(1)}, bf16[64,1024]{1,0:T(8,128)(2,1)S(1)}, u32[]{:S(2)}, u32[]{:S(2)}) collective-permute-start(bf16[64,1024]{1,0:T(8,128)(2,1)S(1)} %shard_map.131.refs_0_), channel_id=1, source_target_pairs={{0,128},{32,160},{64,192},{96,224},{128,0},{160,32},{192,64},{224,... | collective-permute-start | bytes 393224 | tf_op jit(solution)/shard_map/ppermute | solution.py:315
  133.7 3.9 %collective-permute-start.36 = (bf16[64,1024]{1,0:T(8,128)(2,1)S(1)}, bf16[64,1024]{1,0:T(8,128)(2,1)S(1)}, u32[]{:S(2)}, u32[]{:S(2)}) collective-permute-start(bf16[64,1024]{1,0:T(8,128)(2,1)S(1)} %shard_map.133.refs_0_), channel_id=1, source_target_pairs={{0,64},{32,96},{64,0},{96,32},{128,192},{160,224},{192,128},{224,1... | collective-permute-start | bytes 393224 | tf_op jit(solution)/shard_map/ppermute | solution.py:315
  133.8 5.9 %collective-permute-start.38 = (bf16[64,1024]{1,0:T(8,128)(2,1)S(1)}, bf16[64,1024]{1,0:T(8,128)(2,1)S(1)}, u32[]{:S(2)}, u32[]{:S(2)}) collective-permute-start(bf16[64,1024]{1,0:T(8,128)(2,1)S(1)} %shard_map.133.refs_0_), channel_id=1, source_target_pairs={{0,32},{32,0},{64,96},{96,64},{128,160},{160,128},{192,224},{224,1... | collective-permute-start | bytes 393224 | tf_op jit(solution)/shard_map/ppermute | solution.py:315
  137.6 3.7 %collective-permute-start.37 = (bf16[64,1024]{1,0:T(8,128)(2,1)S(1)}, bf16[64,1024]{1,0:T(8,128)(2,1)S(1)}, u32[]{:S(2)}, u32[]{:S(2)}) collective-permute-start(bf16[64,1024]{1,0:T(8,128)(2,1)S(1)} %collective-permute-done.36.refs_0_), channel_id=1, source_target_pairs={{0,32},{32,0},{64,96},{96,64},{128,160},{160,128},{192,224},{224,1... | collective-permute-start | bytes 393224 | tf_op jit(solution)/shard_map/ppermute | solution.py:315
  (2 other events, 1.9 us)

commit v6 on v5

--- a/solution.py
+++ b/solution.py
@@ -230,14 +230,16 @@
 
 def inner_steps(anchor, first, second, own, got, here):
     weights, one, two = anchor[here], first[(0,) + here], second[(0,) + here]
-    for step, ref in enumerate(own):
-        gradient = ref[(0,) + here] + got[(step,) + here].astype(jnp.float32)
+    total, itself, ahead, back = own
+    last = itself[here] + ahead[here].astype(jnp.float32) + back[here].astype(jnp.float32)
+    for step, value in enumerate((total[(0,) + here], last)):
+        gradient = value + got[(step,) + here].astype(jnp.float32)
         weights, one, two = adam_update(weights, one, two, gradient)
     return weights, one, two
 
 
-def code_kernel(turn, spot, anchor, first, second, own_a, own_b, got, scale, out):
-    own = own_a, own_b
+def code_kernel(turn, spot, anchor, first, second, *refs):
+    own, (got, scale, out) = refs[:4], refs[4:]
     half = out.shape[0]
     base = lax.rem(spot[2] + turn, CORES) * half
 
@@ -264,14 +266,14 @@
     rows, width = anchor.shape
     return pl.pallas_call(
         functools.partial(code_kernel, turn),
-        in_specs=[SMEM] + [VMEM] * 7, out_specs=VMEM,
+        in_specs=[SMEM] + [VMEM] * 9, out_specs=VMEM,
         out_shape=shape_of((rows // CORES, width), jnp.bfloat16),
         cost_estimate=SHORT, compiler_params=PARAMS,
     )(spot, anchor, first, second, *own, got, exponents)
 
 
-def moment_kernel(anchor, first, second, own_a, own_b, got, new_first, new_second):
-    own = own_a, own_b
+def moment_kernel(anchor, first, second, *refs):
+    own, (got, new_first, new_second) = refs[:4], refs[4:]
 
     @pl.loop(0, anchor.shape[0], step=16)
     def _(r):
@@ -286,7 +288,7 @@
 def moments(anchor, first, second, own, got):
     out = shape_of(first.shape, first.dtype)
     return pl.pallas_call(
-        moment_kernel, in_specs=[VMEM] * 6, out_specs=[VMEM] * 2, out_shape=[out] * 2,
+        moment_kernel, in_specs=[VMEM] * 8, out_specs=[VMEM] * 2, out_shape=[out] * 2,
         cost_estimate=SHORT, compiler_params=PARAMS,
     )(anchor, first, second, *own, got)
 
@@ -392,7 +394,8 @@
     theirs = totals(sum(reduce(soon), []), jnp.bfloat16)
     got = lax.ppermute(theirs, "fsdp", fsdp_shift(1, 0, 0))
     late = gather([block[3] for block in sent], [block[4] for block in sent], 2)
-    own = [totals(part, jnp.float32) for part in reduce([soon[step] + late[step] for step in range(2)])]
+    parts = reduce([soon[step] + late[step] for step in range(2)])
+    own = [totals(parts[0], jnp.float32)] + parts[1]
 
     state = anchor, first_moment, second_moment, own, got
     other = swap(code(1, spot, *state, exponents), 0, 1)

time: 143 us -> 143 us (level)
  starting transfers between devices: 72.3 us -> 74 us
    ppermute x6, starting transfers between devices: 19.9 us -> 21.6 us  [swap(): return lax.ppermute(block, 'replica', pairs)]
    ppermute x6, waiting for transfers between devices: 8.58 us -> 6.99 us  [swap(): return lax.ppermute(block, 'replica', pairs)]
    pallas_call x3 -> x2, Pallas kernels: 4.19 us -> 2.78 us  [totals(): pl.pallas_call(total_kernel, in_specs=[VMEM] * len(parts), out_specs=VMEM...]
    unnamed x23 -> x21, local copies, waits for them, and re-layouts: 7.75 us -> 6.79 us
where the time goes in v6:
time: 143 us
  starting transfers between devices  74 us (52%)
  waiting for transfers between devices  32.6 us (23%)
  Pallas kernels  27.1 us (19%)
  local copies, waits for them, and re-layouts  6.98 us (5%)
    ppermute x32, starting transfers between devices, along(): return lax.ppermute(block, 'fsdp', fsdp_shift(*shift))  45.5 us
    ppermute x32, waiting for transfers between devices, along(): return lax.ppermute(block, 'fsdp', fsdp_shift(*shift))  25.6 us
    ppermute x6, starting transfers between devices, swap(): return lax.ppermute(block, 'replica', pairs)  21.6 us
    ppermute x6, waiting for transfers between devices, swap(): return lax.ppermute(block, 'replica', pairs)  6.99 us
    ppermute x1, starting transfers between devices, on_device(): got = lax.ppermute(theirs, 'fsdp', fsdp_shift(1, 0, 0))  6.91 us
    unnamed x21, local copies, waits for them, and re-layouts  6.79 us
    pallas_call x2, Pallas kernels, code(): pl.pallas_call(functools.partial(code_kernel, turn), in_specs=[SMEM] + [V...  5.12 us
    pallas_call x4, Pallas kernels, nearest(): pl.pallas_call(nearest_kernel, in_specs=[VMEM] * (len(pieces) + 2), out_s...  4.56 us
  transfers between devices with their start and end apart: 39, of which 15 were waited for; matrix products, arithmetic and copies ran while one was open for 0% of the time, Pallas kernels for 15%

profile of v6, /device:TPU:1, one launch (start us, length us, event | category | flops | bytes accessed | tf_op | source)
XLA Modules:
  0.0 142.7 jit_solution(15764480998597642373)
XLA Ops:
  1.6 2.2 %copy-done.1 = bf16[1,2,128,8192]{3,2,1,0:T(8,128)(2,1)S(1)} copy-done((bf16[1,2,128,8192]{3,2,1,0:T(8,128)(2,1)S(1)}, bf16[1,2,128,8192]{3,2,1,0:T(8,128)(2,1)}, u32[]{:S(2)}) %copy-start.1) | copy-done | bytes 4194328
  4.8 1.1 shard_map.111
  5.9 2.2 %collective-permute-start = (bf16[10,128,256]{2,1,0:T(8,128)(2,1)S(1)}, bf16[10,128,256]{2,1,0:T(8,128)(2,1)S(1)}, u32[]{:S(2)}, u32[]{:S(2)}) collective-permute-start(bf16[10,128,256]{2,1,0:T(8,128)(2,1)S(1)} %get-tuple-element.48), channel_id=1, source_target_pairs={{0,1},{1,2},{2,3},{3,0},{4,5},{5,6},{6,7},{7,4},{8,9},{9,10},{10,1... | collective-permute-start | bytes 1966088 | tf_op jit(solution)/shard_map/ppermute | solution.py:46
  8.1 1.5 %collective-permute-start.1 = (bf16[10,128,256]{2,1,0:T(8,128)(2,1)S(1)}, bf16[10,128,256]{2,1,0:T(8,128)(2,1)S(1)}, u32[]{:S(2)}, u32[]{:S(2)}) collective-permute-start(bf16[10,128,256]{2,1,0:T(8,128)(2,1)S(1)} %get-tuple-element.49), channel_id=1, source_target_pairs={{0,3},{1,0},{2,1},{3,2},{4,7},{5,4},{6,5},{7,6},{8,11},{9,8},{10,9... | collective-permute-start | bytes 1966088 | tf_op jit(solution)/shard_map/ppermute | solution.py:46
  9.7 1.1 shard_map.116
  10.8 1.3 collective-permute-start.12
  12.1 1.5 %collective-permute-start.13 = (bf16[10,128,256]{2,1,0:T(8,128)(2,1)S(1)}, bf16[10,128,256]{2,1,0:T(8,128)(2,1)S(1)}, u32[]{:S(2)}, u32[]{:S(2)}) collective-permute-start(bf16[10,128,256]{2,1,0:T(8,128)(2,1)S(1)} %get-tuple-element.59), channel_id=1, source_target_pairs={{0,12},{1,13},{2,14},{3,15},{4,0},{5,1},{6,2},{7,3},{8,4},{9,5},{1... | collective-permute-start | bytes 1966088 | tf_op jit(solution)/shard_map/ppermute | solution.py:46
  13.5 8.5 %collective-permute-done.refs_1_ = bf16[10,128,256]{2,1,0:T(8,128)(2,1)S(1)} collective-permute-done((bf16[10,128,256]{2,1,0:T(8,128)(2,1)S(1)}, bf16[10,128,256]{2,1,0:T(8,128)(2,1)S(1)}, u32[]{:S(2)}, u32[]{:S(2)}) %collective-permute-start) | collective-permute-done | bytes 655392 | tf_op jit(solution)/shard_map/ppermute | solution.py:46
  22.0 1.6 %collective-permute-start.2 = (bf16[4,128,256]{2,1,0:T(8,128)(2,1)S(1)}, bf16[4,128,256]{2,1,0:T(8,128)(2,1)S(1)}, u32[]{:S(2)}, u32[]{:S(2)}) collective-permute-start(bf16[4,128,256]{2,1,0:T(8,128)(2,1)S(1)} %slice.35), channel_id=1, source_target_pairs={{0,1},{1,2},{2,3},{3,0},{4,5},{5,6},{6,7},{7,4},{8,9},{9,10},{10,1... | collective-permute-start | bytes 786440 | tf_op jit(solution)/shard_map/ppermute | solution.py:46
  23.7 1.7 %collective-permute-start.3 = (bf16[4,128,256]{2,1,0:T(8,128)(2,1)S(1)}, bf16[4,128,256]{2,1,0:T(8,128)(2,1)S(1)}, u32[]{:S(2)}, u32[]{:S(2)}) collective-permute-start(bf16[4,128,256]{2,1,0:T(8,128)(2,1)S(1)} %slice.36), channel_id=1, source_target_pairs={{0,3},{1,0},{2,1},{3,2},{4,7},{5,4},{6,5},{7,6},{8,11},{9,8},{10,9... | collective-permute-start | bytes 786440 | tf_op jit(solution)/shard_map/ppermute | solution.py:46
  25.5 2.5 %collective-permute-start.14 = (bf16[4,128,256]{2,1,0:T(8,128)(2,1)S(1)}, bf16[4,128,256]{2,1,0:T(8,128)(2,1)S(1)}, u32[]{:S(2)}, u32[]{:S(2)}) collective-permute-start(bf16[4,128,256]{2,1,0:T(8,128)(2,1)S(1)} %slice.39), channel_id=1, source_target_pairs={{0,4},{1,5},{2,6},{3,7},{4,8},{5,9},{6,10},{7,11},{8,12},{9,13},{1... | collective-permute-start | bytes 786440 | tf_op jit(solution)/shard_map/ppermute | solution.py:46
  28.0 1.4 collective-permute-start.15
  30.0 4.4 %collective-permute-start.25 = (bf16[128,1024]{1,0:T(8,128)(2,1)S(1)}, bf16[128,1024]{1,0:T(8,128)(2,1)S(1)}, u32[]{:S(2)}, u32[]{:S(2)}) collective-permute-start(bf16[128,1024]{1,0:T(8,128)(2,1)S(1)} %get-tuple-element.68), channel_id=1, source_target_pairs={{0,12},{1,13},{2,14},{3,15},{4,0},{5,1},{6,2},{7,3},{8,4},{9,5},{1... | collective-permute-start | bytes 786440 | tf_op jit(solution)/shard_map/ppermute | solution.py:46
  34.9 2.6 %collective-permute-start.29 = (bf16[128,1024]{1,0:T(8,128)(2,1)S(1)}, bf16[128,1024]{1,0:T(8,128)(2,1)S(1)}, u32[]{:S(2)}, u32[]{:S(2)}) collective-permute-start(bf16[128,1024]{1,0:T(8,128)(2,1)S(1)} %get-tuple-element.73), channel_id=1, source_target_pairs={{0,3},{1,0},{2,1},{3,2},{4,7},{5,4},{6,5},{7,6},{8,11},{9,8},{10,9... | collective-permute-start | bytes 786440 | tf_op jit(solution)/shard_map/ppermute | solution.py:46
  38.4 1.6 %collective-permute-done.25.refs_6_ = bf16[128,1024]{1,0:T(8,128)(2,1)S(1)} collective-permute-done((bf16[128,1024]{1,0:T(8,128)(2,1)S(1)}, bf16[128,1024]{1,0:T(8,128)(2,1)S(1)}, u32[]{:S(2)}, u32[]{:S(2)}) %collective-permute-start.25) | collective-permute-done | bytes 262176 | tf_op jit(solution)/shard_map/ppermute | solution.py:46
  42.5 2.0 %collective-permute-start.27 = (bf16[256,1024]{1,0:T(8,128)(2,1)S(1)}, bf16[256,1024]{1,0:T(8,128)(2,1)S(1)}, u32[]{:S(2)}, u32[]{:S(2)}) collective-permute-start(bf16[256,1024]{1,0:T(8,128)(2,1)S(1)} %get-tuple-element.71), channel_id=1, source_target_pairs={{0,12},{1,13},{2,14},{3,15},{4,0},{5,1},{6,2},{7,3},{8,4},{9,5},{1... | collective-permute-start | bytes 1572872 | tf_op jit(solution)/shard_map/ppermute | solution.py:46
  45.4 2.7 %collective-permute-start.31 = (bf16[256,1024]{1,0:T(8,128)(2,1)S(1)}, bf16[256,1024]{1,0:T(8,128)(2,1)S(1)}, u32[]{:S(2)}, u32[]{:S(2)}) collective-permute-start(bf16[256,1024]{1,0:T(8,128)(2,1)S(1)} %get-tuple-element.76), channel_id=1, source_target_pairs={{0,3},{1,0},{2,1},{3,2},{4,7},{5,4},{6,5},{7,6},{8,11},{9,8},{10,9... | collective-permute-start | bytes 1572872 | tf_op jit(solution)/shard_map/ppermute | solution.py:46
  48.1 4.6 %collective-permute-done.26.refs_1_ = bf16[256,1024]{1,0:T(8,128)(2,1)S(1)} collective-permute-done((bf16[256,1024]{1,0:T(8,128)(2,1)S(1)}, bf16[256,1024]{1,0:T(8,128)(2,1)S(1)}, u32[]{:S(2)}, u32[]{:S(2)}) %collective-permute-start.26) | collective-permute-done | bytes 524320 | tf_op jit(solution)/shard_map/ppermute | solution.py:46
  52.7 2.2 %collective-permute-start.5 = (bf16[6,128,256]{2,1,0:T(8,128)(2,1)S(1)}, bf16[6,128,256]{2,1,0:T(8,128)(2,1)S(1)}, u32[]{:S(2)}, u32[]{:S(2)}) collective-permute-start(bf16[6,128,256]{2,1,0:T(8,128)(2,1)S(1)} %get-tuple-element.51), channel_id=1, source_target_pairs={{0,3},{1,0},{2,1},{3,2},{4,7},{5,4},{6,5},{7,6},{8,11},{9,8},{10,9... | collective-permute-start | bytes 1179656 | tf_op jit(solution)/shard_map/ppermute | solution.py:46
  55.6 2.0 %collective-permute-start.17 = (bf16[6,128,256]{2,1,0:T(8,128)(2,1)S(1)}, bf16[6,128,256]{2,1,0:T(8,128)(2,1)S(1)}, u32[]{:S(2)}, u32[]{:S(2)}) collective-permute-start(bf16[6,128,256]{2,1,0:T(8,128)(2,1)S(1)} %get-tuple-element.61), channel_id=1, source_target_pairs={{0,12},{1,13},{2,14},{3,15},{4,0},{5,1},{6,2},{7,3},{8,4},{9,5},{1... | collective-permute-start | bytes 1179656 | tf_op jit(solution)/shard_map/ppermute | solution.py:46
  57.6 1.4 shard_map.126
  59.0 6.9 %collective-permute-start.32 = (bf16[2,256,1024]{2,1,0:T(8,128)(2,1)}, bf16[2,256,1024]{2,1,0:T(8,128)(2,1)}, u32[]{:S(2)}, u32[]{:S(2)}) collective-permute-start(bf16[2,256,1024]{2,1,0:T(8,128)(2,1)} %shard_map.126), channel_id=1, source_target_pairs={{0,16},{1,17},{2,18},{3,19},{4,20},{5,21},{6,22},{7,23},{8,24},{9,... | collective-permute-start | bytes 3145736 | tf_op jit(solution)/shard_map/ppermute | solution.py:395
  66.0 2.7 %collective-permute-start.7 = (bf16[2,128,256]{2,1,0:T(8,128)(2,1)S(1)}, bf16[2,128,256]{2,1,0:T(8,128)(2,1)S(1)}, u32[]{:S(2)}, u32[]{:S(2)}) collective-permute-start(bf16[2,128,256]{2,1,0:T(8,128)(2,1)S(1)} %slice.38), channel_id=1, source_target_pairs={{0,3},{1,0},{2,1},{3,2},{4,7},{5,4},{6,5},{7,6},{8,11},{9,8},{10,9... | collective-permute-start | bytes 393224 | tf_op jit(solution)/shard_map/ppermute | solution.py:46
  68.9 2.7 %collective-permute-start.19 = (bf16[2,128,256]{2,1,0:T(8,128)(2,1)S(1)}, bf16[2,128,256]{2,1,0:T(8,128)(2,1)S(1)}, u32[]{:S(2)}, u32[]{:S(2)}) collective-permute-start(bf16[2,128,256]{2,1,0:T(8,128)(2,1)S(1)} %slice.42), channel_id=1, source_target_pairs={{0,12},{1,13},{2,14},{3,15},{4,0},{5,1},{6,2},{7,3},{8,4},{9,5},{1... | collective-permute-start | bytes 393224 | tf_op jit(solution)/shard_map/ppermute | solution.py:46
  74.3 2.2 %collective-permute-start.21 = (bf16[128,1024]{1,0:T(8,128)(2,1)S(1)}, bf16[128,1024]{1,0:T(8,128)(2,1)S(1)}, u32[]{:S(2)}, u32[]{:S(2)}) collective-permute-start(bf16[128,1024]{1,0:T(8,128)(2,1)S(1)} %get-tuple-element.63), channel_id=1, source_target_pairs={{0,3},{1,0},{2,1},{3,2},{4,7},{5,4},{6,5},{7,6},{8,11},{9,8},{10,9... | collective-permute-start | bytes 786440 | tf_op jit(solution)/shard_map/ppermute | solution.py:46
  78.5 1.3 collective-permute-done.8.refs_9_
  79.8 1.5 %shard_map.114 = (bf16[256,1024]{1,0:T(8,128)(2,1)}, bf16[256,1024]{1,0:T(8,128)(2,1)}) custom-call(bf16[12,128,256]{2,1,0:T(8,128)(2,1)S(1)} %get-tuple-element.47.refs_0_, bf16[10,128,256]{2,1,0:T(8,128)(2,1)S(1)} %collective-permute-done.refs_1_, bf16[10,128,256]{2,1,0:T(8,128)(2,1)S(1)} %collective-permute-done.1.refs_2_, ...), custom_call_target="tpu_custom_call" | custom-call | flops 1 | bytes 1 | tf_op jit(solution)/shard_map/pallas_call | solution.py:166
  81.3 2.7 %collective-permute-start.11 = (bf16[256,1024]{1,0:T(8,128)(2,1)}, bf16[256,1024]{1,0:T(8,128)(2,1)}, u32[]{:S(2)}, u32[]{:S(2)}) collective-permute-start(bf16[256,1024]{1,0:T(8,128)(2,1)} %get-tuple-element.56), channel_id=1, source_target_pairs={{0,12},{1,13},{2,14},{3,15},{4,0},{5,1},{6,2},{7,3},{8,4},{9,5},{1... | collective-permute-start | bytes 1572872 | tf_op jit(solution)/shard_map/ppermute | solution.py:46
  84.8 1.6 %shard_map.119 = (bf16[256,1024]{1,0:T(8,128)(2,1)}, bf16[256,1024]{1,0:T(8,128)(2,1)}) custom-call(bf16[12,128,256]{2,1,0:T(8,128)(2,1)S(1)} %get-tuple-element.57.refs_0_, bf16[10,128,256]{2,1,0:T(8,128)(2,1)S(1)} %collective-permute-done.12.refs_1_, bf16[10,128,256]{2,1,0:T(8,128)(2,1)S(1)} %collective-permute-done.13.refs_2_, ...), custom_call_target="tpu_custom_call" | custom-call | flops 1 | bytes 1 | tf_op jit(solution)/shard_map/pallas_call | solution.py:166
  86.3 2.7 %collective-permute-start.23 = (bf16[256,1024]{1,0:T(8,128)(2,1)}, bf16[256,1024]{1,0:T(8,128)(2,1)}, u32[]{:S(2)}, u32[]{:S(2)}) collective-permute-start(bf16[256,1024]{1,0:T(8,128)(2,1)} %get-tuple-element.66), channel_id=1, source_target_pairs={{0,3},{1,0},{2,1},{3,2},{4,7},{5,4},{6,5},{7,6},{8,11},{9,8},{10,9... | collective-permute-start | bytes 1572872 | tf_op jit(solution)/shard_map/ppermute | solution.py:46
  89.1 4.3 %collective-permute-done.10.refs_1_ = bf16[256,1024]{1,0:T(8,128)(2,1)} collective-permute-done((bf16[256,1024]{1,0:T(8,128)(2,1)}, bf16[256,1024]{1,0:T(8,128)(2,1)}, u32[]{:S(2)}, u32[]{:S(2)}) %collective-permute-start.10) | collective-permute-done | bytes 524320 | tf_op jit(solution)/shard_map/ppermute | solution.py:46
  93.5 1.2 copy-done.7
  94.7 1.4 shard_map.115.refs_0_
  96.1 2.6 %collective-permute-done.22.refs_2_ = bf16[256,1024]{1,0:T(8,128)(2,1)} collective-permute-done((bf16[256,1024]{1,0:T(8,128)(2,1)}, bf16[256,1024]{1,0:T(8,128)(2,1)}, u32[]{:S(2)}, u32[]{:S(2)}) %collective-permute-start.22) | collective-permute-done | bytes 524320 | tf_op jit(solution)/shard_map/ppermute | solution.py:46
  98.8 1.2 copy-done.4
  100.0 2.6 %shard_map.128 = bf16[128,1024]{1,0:T(8,128)(2,1)S(1)} custom-call(s32[7]{0:T(128)S(1)} %stack.23.spot, f32[256,1024]{1,0:T(8,128)S(1)} %copy-done, f32[1,256,1024]{2,1,0:T(8,128)S(1)} %copy-done.3, f32[1,256,1024]{2,1,0:T(8,128)S(1)} %copy-done.4, f32[1,256,1024]{2,1,0:T(8,128)S(1)} %shard_map.115.refs_0_, f32[256,1024]{1,0:T(8,128)S(1)} %shard_map.117.refs_1_, ...), custom_call_target="tpu_custom_call" | custom-call | flops 1 | bytes 1 | tf_op jit(solution)/shard_map/pallas_call | solution.py:267
  102.6 12.9 %collective-permute-start.33 = (bf16[128,1024]{1,0:T(8,128)(2,1)S(1)}, bf16[128,1024]{1,0:T(8,128)(2,1)S(1)}, u32[]{:S(2)}, u32[]{:S(2)}) collective-permute-start(bf16[128,1024]{1,0:T(8,128)(2,1)S(1)} %shard_map.128), channel_id=1, source_target_pairs={{0,32},{32,0},{64,96},{96,64},{128,160},{160,128},{192,224},{224,1... | collective-permute-start | bytes 786440 | tf_op jit(solution)/shard_map/ppermute | solution.py:317
  115.5 2.6 %shard_map.127.ours = bf16[128,1024]{1,0:T(8,128)(2,1)S(1)} custom-call(s32[7]{0:T(128)S(1)} %stack.23.spot, f32[256,1024]{1,0:T(8,128)S(1)} %copy-done, f32[1,256,1024]{2,1,0:T(8,128)S(1)} %copy-done.3, f32[1,256,1024]{2,1,0:T(8,128)S(1)} %copy-done.4, f32[1,256,1024]{2,1,0:T(8,128)S(1)} %shard_map.115.refs_0_, f32[256,1024]{1,0:T(8,128)S(1)} %shard_map.117.refs_1_, ...), custom_call_target="tpu_custom_call" | custom-call | flops 1 | bytes 1 | tf_op jit(solution)/shard_map/pallas_call | solution.py:267
  118.7 2.3 %collective-permute-start.34 = (bf16[64,1024]{1,0:T(8,128)(2,1)S(1)}, bf16[64,1024]{1,0:T(8,128)(2,1)S(1)}, u32[]{:S(2)}, u32[]{:S(2)}) collective-permute-start(bf16[64,1024]{1,0:T(8,128)(2,1)S(1)} %get-tuple-element.78), channel_id=1, source_target_pairs={{0,64},{32,96},{64,0},{96,32},{128,192},{160,224},{192,128},{224,1... | collective-permute-start | bytes 393224 | tf_op jit(solution)/shard_map/ppermute | solution.py:317
  120.9 3.8 %collective-permute-done.34.refs_1_ = bf16[64,1024]{1,0:T(8,128)(2,1)S(1)} collective-permute-done((bf16[64,1024]{1,0:T(8,128)(2,1)S(1)}, bf16[64,1024]{1,0:T(8,128)(2,1)S(1)}, u32[]{:S(2)}, u32[]{:S(2)}) %collective-permute-start.34) | collective-permute-done | bytes 131104 | tf_op jit(solution)/shard_map/ppermute | solution.py:317
  124.8 2.0 %collective-permute-start.35 = (bf16[64,1024]{1,0:T(8,128)(2,1)S(1)}, bf16[64,1024]{1,0:T(8,128)(2,1)S(1)}, u32[]{:S(2)}, u32[]{:S(2)}) collective-permute-start(bf16[64,1024]{1,0:T(8,128)(2,1)S(1)} %shard_map.130.refs_0_), channel_id=1, source_target_pairs={{0,128},{32,160},{64,192},{96,224},{128,0},{160,32},{192,64},{224,... | collective-permute-start | bytes 393224 | tf_op jit(solution)/shard_map/ppermute | solution.py:317
  126.8 3.8 %shard_map.131 = (f32[1,256,1024]{2,1,0:T(8,128)}, f32[1,256,1024]{2,1,0:T(8,128)}) custom-call(f32[256,1024]{1,0:T(8,128)S(1)} %copy-done, f32[1,256,1024]{2,1,0:T(8,128)S(1)} %copy-done.3, f32[1,256,1024]{2,1,0:T(8,128)S(1)} %copy-done.5, f32[1,256,1024]{2,1,0:T(8,128)S(1)} %shard_map.115.refs_0_, f32[256,1024]{1,0:T(8,128)S(1)} %shard_map.117.refs_1_, ...), custom_call_target="tpu_custom_call" | custom-call | flops 1 | bytes 1 | tf_op jit(solution)/shard_map/pallas_call | solution.py:290
  130.6 2.4 %collective-permute-done.35.refs_1_ = bf16[64,1024]{1,0:T(8,128)(2,1)S(1)} collective-permute-done((bf16[64,1024]{1,0:T(8,128)(2,1)S(1)}, bf16[64,1024]{1,0:T(8,128)(2,1)S(1)}, u32[]{:S(2)}, u32[]{:S(2)}) %collective-permute-start.35) | collective-permute-done | bytes 131104 | tf_op jit(solution)/shard_map/ppermute | solution.py:317
  133.1 1.6 %collective-permute-start.38 = (bf16[64,1024]{1,0:T(8,128)(2,1)S(1)}, bf16[64,1024]{1,0:T(8,128)(2,1)S(1)}, u32[]{:S(2)}, u32[]{:S(2)}) collective-permute-start(bf16[64,1024]{1,0:T(8,128)(2,1)S(1)} %shard_map.132.refs_0_), channel_id=1, source_target_pairs={{0,32},{32,0},{64,96},{96,64},{128,160},{160,128},{192,224},{224,1... | collective-permute-start | bytes 393224 | tf_op jit(solution)/shard_map/ppermute | solution.py:317
  134.7 1.4 shard_map.133
  136.9 2.7 %collective-permute-start.37 = (bf16[64,1024]{1,0:T(8,128)(2,1)S(1)}, bf16[64,1024]{1,0:T(8,128)(2,1)S(1)}, u32[]{:S(2)}, u32[]{:S(2)}) collective-permute-start(bf16[64,1024]{1,0:T(8,128)(2,1)S(1)} %collective-permute-done.36.refs_0_), channel_id=1, source_target_pairs={{0,32},{32,0},{64,96},{96,64},{128,160},{160,128},{192,224},{224,1... | collective-permute-start | bytes 393224 | tf_op jit(solution)/shard_map/ppermute | solution.py:317
  139.6 1.6 %shard_map.134 = (f32[256,1024]{1,0:T(8,128)}, f32[256,1024]{1,0:T(8,128)}) custom-call(s32[7]{0:T(128)S(1)} %stack.23.spot, f32[256,1024]{1,0:T(8,128)S(1)} %copy-done, f32[256,1024]{1,0:T(8,128)S(1)} %copy-done.2, bf16[64,1024]{1,0:T(8,128)(2,1)S(1)} %collective-permute-done.36.refs_0_, ...), custom_call_target="tpu_custom_call", output_to_operand_aliasing={{0}: (5, {}), {1}: (6, {})} | custom-call | flops 1 | bytes 1 | tf_op jit(solution)/shard_map/pallas_call | solution.py:345
  141.2 1.4 shard_map.135
  (86 shorter events, 15.5 us)
Async XLA Ops:
  1.6 2.2 %copy-start.1 = (bf16[1,2,128,8192]{3,2,1,0:T(8,128)(2,1)S(1)}, bf16[1,2,128,8192]{3,2,1,0:T(8,128)(2,1)}, u32[]{:S(2)}) copy-start(bf16[1,2,128,8192]{3,2,1,0:T(8,128)(2,1)} %features.3) | copy-start | bytes 12582916
  3.8 1.0 copy-start.8
  5.9 16.1 %collective-permute-start = (bf16[10,128,256]{2,1,0:T(8,128)(2,1)S(1)}, bf16[10,128,256]{2,1,0:T(8,128)(2,1)S(1)}, u32[]{:S(2)}, u32[]{:S(2)}) collective-permute-start(bf16[10,128,256]{2,1,0:T(8,128)(2,1)S(1)} %get-tuple-element.48), channel_id=1, source_target_pairs={{0,1},{1,2},{2,3},{3,0},{4,5},{5,6},{6,7},{7,4},{8,9},{9,10},{10,1... | collective-permute-start | bytes 1966088 | tf_op jit(solution)/shard_map/ppermute | solution.py:46
  8.1 15.5 %collective-permute-start.1 = (bf16[10,128,256]{2,1,0:T(8,128)(2,1)S(1)}, bf16[10,128,256]{2,1,0:T(8,128)(2,1)S(1)}, u32[]{:S(2)}, u32[]{:S(2)}) collective-permute-start(bf16[10,128,256]{2,1,0:T(8,128)(2,1)S(1)} %get-tuple-element.49), channel_id=1, source_target_pairs={{0,3},{1,0},{2,1},{3,2},{4,7},{5,4},{6,5},{7,6},{8,11},{9,8},{10,9... | collective-permute-start | bytes 1966088 | tf_op jit(solution)/shard_map/ppermute | solution.py:46
  10.8 14.7 %collective-permute-start.12 = (bf16[10,128,256]{2,1,0:T(8,128)(2,1)S(1)}, bf16[10,128,256]{2,1,0:T(8,128)(2,1)S(1)}, u32[]{:S(2)}, u32[]{:S(2)}) collective-permute-start(bf16[10,128,256]{2,1,0:T(8,128)(2,1)S(1)} %get-tuple-element.58), channel_id=1, source_target_pairs={{0,4},{1,5},{2,6},{3,7},{4,8},{5,9},{6,10},{7,11},{8,12},{9,13},{1... | collective-permute-start | bytes 1966088 | tf_op jit(solution)/shard_map/ppermute | solution.py:46
  12.1 15.9 %collective-permute-start.13 = (bf16[10,128,256]{2,1,0:T(8,128)(2,1)S(1)}, bf16[10,128,256]{2,1,0:T(8,128)(2,1)S(1)}, u32[]{:S(2)}, u32[]{:S(2)}) collective-permute-start(bf16[10,128,256]{2,1,0:T(8,128)(2,1)S(1)} %get-tuple-element.59), channel_id=1, source_target_pairs={{0,12},{1,13},{2,14},{3,15},{4,0},{5,1},{6,2},{7,3},{8,4},{9,5},{1... | collective-permute-start | bytes 1966088 | tf_op jit(solution)/shard_map/ppermute | solution.py:46
  22.0 7.4 %collective-permute-start.2 = (bf16[4,128,256]{2,1,0:T(8,128)(2,1)S(1)}, bf16[4,128,256]{2,1,0:T(8,128)(2,1)S(1)}, u32[]{:S(2)}, u32[]{:S(2)}) collective-permute-start(bf16[4,128,256]{2,1,0:T(8,128)(2,1)S(1)} %slice.35), channel_id=1, source_target_pairs={{0,1},{1,2},{2,3},{3,0},{4,5},{5,6},{6,7},{7,4},{8,9},{9,10},{10,1... | collective-permute-start | bytes 786440 | tf_op jit(solution)/shard_map/ppermute | solution.py:46
  23.7 5.9 %collective-permute-start.3 = (bf16[4,128,256]{2,1,0:T(8,128)(2,1)S(1)}, bf16[4,128,256]{2,1,0:T(8,128)(2,1)S(1)}, u32[]{:S(2)}, u32[]{:S(2)}) collective-permute-start(bf16[4,128,256]{2,1,0:T(8,128)(2,1)S(1)} %slice.36), channel_id=1, source_target_pairs={{0,3},{1,0},{2,1},{3,2},{4,7},{5,4},{6,5},{7,6},{8,11},{9,8},{10,9... | collective-permute-start | bytes 786440 | tf_op jit(solution)/shard_map/ppermute | solution.py:46
  25.5 9.0 %collective-permute-start.14 = (bf16[4,128,256]{2,1,0:T(8,128)(2,1)S(1)}, bf16[4,128,256]{2,1,0:T(8,128)(2,1)S(1)}, u32[]{:S(2)}, u32[]{:S(2)}) collective-permute-start(bf16[4,128,256]{2,1,0:T(8,128)(2,1)S(1)} %slice.39), channel_id=1, source_target_pairs={{0,4},{1,5},{2,6},{3,7},{4,8},{5,9},{6,10},{7,11},{8,12},{9,13},{1... | collective-permute-start | bytes 786440 | tf_op jit(solution)/shard_map/ppermute | solution.py:46
  28.0 6.4 %collective-permute-start.15 = (bf16[4,128,256]{2,1,0:T(8,128)(2,1)S(1)}, bf16[4,128,256]{2,1,0:T(8,128)(2,1)S(1)}, u32[]{:S(2)}, u32[]{:S(2)}) collective-permute-start(bf16[4,128,256]{2,1,0:T(8,128)(2,1)S(1)} %slice.40), channel_id=1, source_target_pairs={{0,12},{1,13},{2,14},{3,15},{4,0},{5,1},{6,2},{7,3},{8,4},{9,5},{1... | collective-permute-start | bytes 786440 | tf_op jit(solution)/shard_map/ppermute | solution.py:46
  30.0 10.0 %collective-permute-start.25 = (bf16[128,1024]{1,0:T(8,128)(2,1)S(1)}, bf16[128,1024]{1,0:T(8,128)(2,1)S(1)}, u32[]{:S(2)}, u32[]{:S(2)}) collective-permute-start(bf16[128,1024]{1,0:T(8,128)(2,1)S(1)} %get-tuple-element.68), channel_id=1, source_target_pairs={{0,12},{1,13},{2,14},{3,15},{4,0},{5,1},{6,2},{7,3},{8,4},{9,5},{1... | collective-permute-start | bytes 786440 | tf_op jit(solution)/shard_map/ppermute | solution.py:46
  34.4 6.4 %collective-permute-start.24 = (bf16[128,1024]{1,0:T(8,128)(2,1)S(1)}, bf16[128,1024]{1,0:T(8,128)(2,1)S(1)}, u32[]{:S(2)}, u32[]{:S(2)}) collective-permute-start(bf16[128,1024]{1,0:T(8,128)(2,1)S(1)} %get-tuple-element.67), channel_id=1, source_target_pairs={{0,4},{1,5},{2,6},{3,7},{4,8},{5,9},{6,10},{7,11},{8,12},{9,13},{1... | collective-permute-start | bytes 786440 | tf_op jit(solution)/shard_map/ppermute | solution.py:46
  34.9 9.6 %collective-permute-start.29 = (bf16[128,1024]{1,0:T(8,128)(2,1)S(1)}, bf16[128,1024]{1,0:T(8,128)(2,1)S(1)}, u32[]{:S(2)}, u32[]{:S(2)}) collective-permute-start(bf16[128,1024]{1,0:T(8,128)(2,1)S(1)} %get-tuple-element.73), channel_id=1, source_target_pairs={{0,3},{1,0},{2,1},{3,2},{4,7},{5,4},{6,5},{7,6},{8,11},{9,8},{10,9... | collective-permute-start | bytes 786440 | tf_op jit(solution)/shard_map/ppermute | solution.py:46
  37.5 7.1 %collective-permute-start.28 = (bf16[128,1024]{1,0:T(8,128)(2,1)S(1)}, bf16[128,1024]{1,0:T(8,128)(2,1)S(1)}, u32[]{:S(2)}, u32[]{:S(2)}) collective-permute-start(bf16[128,1024]{1,0:T(8,128)(2,1)S(1)} %get-tuple-element.72), channel_id=1, source_target_pairs={{0,1},{1,2},{2,3},{3,0},{4,5},{5,6},{6,7},{7,4},{8,9},{9,10},{10,1... | collective-permute-start | bytes 786440 | tf_op jit(solution)/shard_map/ppermute | solution.py:46
  41.6 11.1 %collective-permute-start.26 = (bf16[256,1024]{1,0:T(8,128)(2,1)S(1)}, bf16[256,1024]{1,0:T(8,128)(2,1)S(1)}, u32[]{:S(2)}, u32[]{:S(2)}) collective-permute-start(bf16[256,1024]{1,0:T(8,128)(2,1)S(1)} %get-tuple-element.70), channel_id=1, source_target_pairs={{0,4},{1,5},{2,6},{3,7},{4,8},{5,9},{6,10},{7,11},{8,12},{9,13},{1... | collective-permute-start | bytes 1572872 | tf_op jit(solution)/shard_map/ppermute | solution.py:46
  42.5 12.4 %collective-permute-start.27 = (bf16[256,1024]{1,0:T(8,128)(2,1)S(1)}, bf16[256,1024]{1,0:T(8,128)(2,1)S(1)}, u32[]{:S(2)}, u32[]{:S(2)}) collective-permute-start(bf16[256,1024]{1,0:T(8,128)(2,1)S(1)} %get-tuple-element.71), channel_id=1, source_target_pairs={{0,12},{1,13},{2,14},{3,15},{4,0},{5,1},{6,2},{7,3},{8,4},{9,5},{1... | collective-permute-start | bytes 1572872 | tf_op jit(solution)/shard_map/ppermute | solution.py:46
  45.3 10.3 %collective-permute-start.30 = (bf16[256,1024]{1,0:T(8,128)(2,1)S(1)}, bf16[256,1024]{1,0:T(8,128)(2,1)S(1)}, u32[]{:S(2)}, u32[]{:S(2)}) collective-permute-start(bf16[256,1024]{1,0:T(8,128)(2,1)S(1)} %get-tuple-element.75), channel_id=1, source_target_pairs={{0,1},{1,2},{2,3},{3,0},{4,5},{5,6},{6,7},{7,4},{8,9},{9,10},{10,1... | collective-permute-start | bytes 1572872 | tf_op jit(solution)/shard_map/ppermute | solution.py:46
  45.4 12.2 %collective-permute-start.31 = (bf16[256,1024]{1,0:T(8,128)(2,1)S(1)}, bf16[256,1024]{1,0:T(8,128)(2,1)S(1)}, u32[]{:S(2)}, u32[]{:S(2)}) collective-permute-start(bf16[256,1024]{1,0:T(8,128)(2,1)S(1)} %get-tuple-element.76), channel_id=1, source_target_pairs={{0,3},{1,0},{2,1},{3,2},{4,7},{5,4},{6,5},{7,6},{8,11},{9,8},{10,9... | collective-permute-start | bytes 1572872 | tf_op jit(solution)/shard_map/ppermute | solution.py:46
  48.1 17.8 %collective-permute-start.4 = (bf16[6,128,256]{2,1,0:T(8,128)(2,1)S(1)}, bf16[6,128,256]{2,1,0:T(8,128)(2,1)S(1)}, u32[]{:S(2)}, u32[]{:S(2)}) collective-permute-start(bf16[6,128,256]{2,1,0:T(8,128)(2,1)S(1)} %get-tuple-element.50), channel_id=1, source_target_pairs={{0,1},{1,2},{2,3},{3,0},{4,5},{5,6},{6,7},{7,4},{8,9},{9,10},{10,1... | collective-permute-start | bytes 1179656 | tf_op jit(solution)/shard_map/ppermute | solution.py:46
  52.7 13.3 %collective-permute-start.5 = (bf16[6,128,256]{2,1,0:T(8,128)(2,1)S(1)}, bf16[6,128,256]{2,1,0:T(8,128)(2,1)S(1)}, u32[]{:S(2)}, u32[]{:S(2)}) collective-permute-start(bf16[6,128,256]{2,1,0:T(8,128)(2,1)S(1)} %get-tuple-element.51), channel_id=1, source_target_pairs={{0,3},{1,0},{2,1},{3,2},{4,7},{5,4},{6,5},{7,6},{8,11},{9,8},{10,9... | collective-permute-start | bytes 1179656 | tf_op jit(solution)/shard_map/ppermute | solution.py:46
  54.9 13.8 %collective-permute-start.16 = (bf16[6,128,256]{2,1,0:T(8,128)(2,1)S(1)}, bf16[6,128,256]{2,1,0:T(8,128)(2,1)S(1)}, u32[]{:S(2)}, u32[]{:S(2)}) collective-permute-start(bf16[6,128,256]{2,1,0:T(8,128)(2,1)S(1)} %get-tuple-element.60), channel_id=1, source_target_pairs={{0,4},{1,5},{2,6},{3,7},{4,8},{5,9},{6,10},{7,11},{8,12},{9,13},{1... | collective-permute-start | bytes 1179656 | tf_op jit(solution)/shard_map/ppermute | solution.py:46
  55.6 13.2 %collective-permute-start.17 = (bf16[6,128,256]{2,1,0:T(8,128)(2,1)S(1)}, bf16[6,128,256]{2,1,0:T(8,128)(2,1)S(1)}, u32[]{:S(2)}, u32[]{:S(2)}) collective-permute-start(bf16[6,128,256]{2,1,0:T(8,128)(2,1)S(1)} %get-tuple-element.61), channel_id=1, source_target_pairs={{0,12},{1,13},{2,14},{3,15},{4,0},{5,1},{6,2},{7,3},{8,4},{9,5},{1... | collective-permute-start | bytes 1179656 | tf_op jit(solution)/shard_map/ppermute | solution.py:46
  59.0 39.8 %collective-permute-start.32 = (bf16[2,256,1024]{2,1,0:T(8,128)(2,1)}, bf16[2,256,1024]{2,1,0:T(8,128)(2,1)}, u32[]{:S(2)}, u32[]{:S(2)}) collective-permute-start(bf16[2,256,1024]{2,1,0:T(8,128)(2,1)} %shard_map.126), channel_id=1, source_target_pairs={{0,16},{1,17},{2,18},{3,19},{4,20},{5,21},{6,22},{7,23},{8,24},{9,... | collective-permute-start | bytes 3145736 | tf_op jit(solution)/shard_map/ppermute | solution.py:395
  65.9 5.7 %collective-permute-start.6 = (bf16[2,128,256]{2,1,0:T(8,128)(2,1)S(1)}, bf16[2,128,256]{2,1,0:T(8,128)(2,1)S(1)}, u32[]{:S(2)}, u32[]{:S(2)}) collective-permute-start(bf16[2,128,256]{2,1,0:T(8,128)(2,1)S(1)} %slice.37), channel_id=1, source_target_pairs={{0,1},{1,2},{2,3},{3,0},{4,5},{5,6},{6,7},{7,4},{8,9},{9,10},{10,1... | collective-permute-start | bytes 393224 | tf_op jit(solution)/shard_map/ppermute | solution.py:46
  66.0 5.6 %collective-permute-start.7 = (bf16[2,128,256]{2,1,0:T(8,128)(2,1)S(1)}, bf16[2,128,256]{2,1,0:T(8,128)(2,1)S(1)}, u32[]{:S(2)}, u32[]{:S(2)}) collective-permute-start(bf16[2,128,256]{2,1,0:T(8,128)(2,1)S(1)} %slice.38), channel_id=1, source_target_pairs={{0,3},{1,0},{2,1},{3,2},{4,7},{5,4},{6,5},{7,6},{8,11},{9,8},{10,9... | collective-permute-start | bytes 393224 | tf_op jit(solution)/shard_map/ppermute | solution.py:46
  68.7 5.1 %collective-permute-start.18 = (bf16[2,128,256]{2,1,0:T(8,128)(2,1)S(1)}, bf16[2,128,256]{2,1,0:T(8,128)(2,1)S(1)}, u32[]{:S(2)}, u32[]{:S(2)}) collective-permute-start(bf16[2,128,256]{2,1,0:T(8,128)(2,1)S(1)} %slice.41), channel_id=1, source_target_pairs={{0,4},{1,5},{2,6},{3,7},{4,8},{5,9},{6,10},{7,11},{8,12},{9,13},{1... | collective-permute-start | bytes 393224 | tf_op jit(solution)/shard_map/ppermute | solution.py:46
  68.9 5.0 %collective-permute-start.19 = (bf16[2,128,256]{2,1,0:T(8,128)(2,1)S(1)}, bf16[2,128,256]{2,1,0:T(8,128)(2,1)S(1)}, u32[]{:S(2)}, u32[]{:S(2)}) collective-permute-start(bf16[2,128,256]{2,1,0:T(8,128)(2,1)S(1)} %slice.42), channel_id=1, source_target_pairs={{0,12},{1,13},{2,14},{3,15},{4,0},{5,1},{6,2},{7,3},{8,4},{9,5},{1... | collective-permute-start | bytes 393224 | tf_op jit(solution)/shard_map/ppermute | solution.py:46
  72.1 6.4 %collective-permute-start.9 = (bf16[128,1024]{1,0:T(8,128)(2,1)S(1)}, bf16[128,1024]{1,0:T(8,128)(2,1)S(1)}, u32[]{:S(2)}, u32[]{:S(2)}) collective-permute-start(bf16[128,1024]{1,0:T(8,128)(2,1)S(1)} %get-tuple-element.53), channel_id=1, source_target_pairs={{0,12},{1,13},{2,14},{3,15},{4,0},{5,1},{6,2},{7,3},{8,4},{9,5},{1... | collective-permute-start | bytes 786440 | tf_op jit(solution)/shard_map/ppermute | solution.py:46
  73.0 6.8 %collective-permute-start.8 = (bf16[128,1024]{1,0:T(8,128)(2,1)S(1)}, bf16[128,1024]{1,0:T(8,128)(2,1)S(1)}, u32[]{:S(2)}, u32[]{:S(2)}) collective-permute-start(bf16[128,1024]{1,0:T(8,128)(2,1)S(1)} %get-tuple-element.52), channel_id=1, source_target_pairs={{0,4},{1,5},{2,6},{3,7},{4,8},{5,9},{6,10},{7,11},{8,12},{9,13},{1... | collective-permute-start | bytes 786440 | tf_op jit(solution)/shard_map/ppermute | solution.py:46
  74.3 9.7 %collective-permute-start.21 = (bf16[128,1024]{1,0:T(8,128)(2,1)S(1)}, bf16[128,1024]{1,0:T(8,128)(2,1)S(1)}, u32[]{:S(2)}, u32[]{:S(2)}) collective-permute-start(bf16[128,1024]{1,0:T(8,128)(2,1)S(1)} %get-tuple-element.63), channel_id=1, source_target_pairs={{0,3},{1,0},{2,1},{3,2},{4,7},{5,4},{6,5},{7,6},{8,11},{9,8},{10,9... | collective-permute-start | bytes 786440 | tf_op jit(solution)/shard_map/ppermute | solution.py:46
  76.5 8.2 %collective-permute-start.20 = (bf16[128,1024]{1,0:T(8,128)(2,1)S(1)}, bf16[128,1024]{1,0:T(8,128)(2,1)S(1)}, u32[]{:S(2)}, u32[]{:S(2)}) collective-permute-start(bf16[128,1024]{1,0:T(8,128)(2,1)S(1)} %get-tuple-element.62), channel_id=1, source_target_pairs={{0,1},{1,2},{2,3},{3,0},{4,5},{5,6},{6,7},{7,4},{8,9},{9,10},{10,1... | collective-permute-start | bytes 786440 | tf_op jit(solution)/shard_map/ppermute | solution.py:46
  78.4 10.6 %copy-start.9 = (s32[1,256,8]{1,2,0:T(8,128)S(1)}, s32[1,256,8]{1,2,0:T(8,128)}, u32[]{:S(2)}) copy-start(s32[1,256,8]{1,2,0:T(8,128)} %param.15) | copy-start | bytes 24580
  81.3 17.4 %copy-start = (f32[256,1024]{1,0:T(8,128)S(1)}, f32[256,1024]{1,0:T(8,128)}, u32[]{:S(2)}) copy-start(f32[256,1024]{1,0:T(8,128)} %anchor.11) | copy-start | bytes 3145732
  81.3 17.4 %copy-start.3 = (f32[1,256,1024]{2,1,0:T(8,128)S(1)}, f32[1,256,1024]{2,1,0:T(8,128)}, u32[]{:S(2)}) copy-start(f32[1,256,1024]{2,1,0:T(8,128)} %first.5) | copy-start | bytes 3145732
  81.3 12.1 %collective-permute-start.10 = (bf16[256,1024]{1,0:T(8,128)(2,1)}, bf16[256,1024]{1,0:T(8,128)(2,1)}, u32[]{:S(2)}, u32[]{:S(2)}) collective-permute-start(bf16[256,1024]{1,0:T(8,128)(2,1)} %get-tuple-element.55), channel_id=1, source_target_pairs={{0,4},{1,5},{2,6},{3,7},{4,8},{5,9},{6,10},{7,11},{8,12},{9,13},{1... | collective-permute-start | bytes 1572872 | tf_op jit(solution)/shard_map/ppermute | solution.py:46
  81.3 12.2 %collective-permute-start.11 = (bf16[256,1024]{1,0:T(8,128)(2,1)}, bf16[256,1024]{1,0:T(8,128)(2,1)}, u32[]{:S(2)}, u32[]{:S(2)}) collective-permute-start(bf16[256,1024]{1,0:T(8,128)(2,1)} %get-tuple-element.56), channel_id=1, source_target_pairs={{0,12},{1,13},{2,14},{3,15},{4,0},{5,1},{6,2},{7,3},{8,4},{9,5},{1... | collective-permute-start | bytes 1572872 | tf_op jit(solution)/shard_map/ppermute | solution.py:46
  86.3 12.4 %collective-permute-start.22 = (bf16[256,1024]{1,0:T(8,128)(2,1)}, bf16[256,1024]{1,0:T(8,128)(2,1)}, u32[]{:S(2)}, u32[]{:S(2)}) collective-permute-start(bf16[256,1024]{1,0:T(8,128)(2,1)} %get-tuple-element.65), channel_id=1, source_target_pairs={{0,1},{1,2},{2,3},{3,0},{4,5},{5,6},{6,7},{7,4},{8,9},{9,10},{10,1... | collective-permute-start | bytes 1572872 | tf_op jit(solution)/shard_map/ppermute | solution.py:46
  86.3 12.4 %collective-permute-start.23 = (bf16[256,1024]{1,0:T(8,128)(2,1)}, bf16[256,1024]{1,0:T(8,128)(2,1)}, u32[]{:S(2)}, u32[]{:S(2)}) collective-permute-start(bf16[256,1024]{1,0:T(8,128)(2,1)} %get-tuple-element.66), channel_id=1, source_target_pairs={{0,3},{1,0},{2,1},{3,2},{4,7},{5,4},{6,5},{7,6},{8,11},{9,8},{10,9... | collective-permute-start | bytes 1572872 | tf_op jit(solution)/shard_map/ppermute | solution.py:46
  93.5 1.2 copy-start.7
  98.8 1.2 copy-start.4
  102.6 24.2 %copy-start.5 = (f32[1,256,1024]{2,1,0:T(8,128)S(1)}, f32[1,256,1024]{2,1,0:T(8,128)}, u32[]{:S(2)}) copy-start(f32[1,256,1024]{2,1,0:T(8,128)} %second.5) | copy-start | bytes 3145732
  102.6 15.5 %collective-permute-start.33 = (bf16[128,1024]{1,0:T(8,128)(2,1)S(1)}, bf16[128,1024]{1,0:T(8,128)(2,1)S(1)}, u32[]{:S(2)}, u32[]{:S(2)}) collective-permute-start(bf16[128,1024]{1,0:T(8,128)(2,1)S(1)} %shard_map.128), channel_id=1, source_target_pairs={{0,32},{32,0},{64,96},{96,64},{128,160},{160,128},{192,224},{224,1... | collective-permute-start | bytes 786440 | tf_op jit(solution)/shard_map/ppermute | solution.py:317
  118.6 16.0 %copy-start.2 = (f32[256,1024]{1,0:T(8,128)S(1)}, f32[256,1024]{1,0:T(8,128)}, u32[]{:S(2)}) copy-start(f32[256,1024]{1,0:T(8,128)} %momentum.5) | copy-start | bytes 3145732
  118.7 6.1 %collective-permute-start.34 = (bf16[64,1024]{1,0:T(8,128)(2,1)S(1)}, bf16[64,1024]{1,0:T(8,128)(2,1)S(1)}, u32[]{:S(2)}, u32[]{:S(2)}) collective-permute-start(bf16[64,1024]{1,0:T(8,128)(2,1)S(1)} %get-tuple-element.78), channel_id=1, source_target_pairs={{0,64},{32,96},{64,0},{96,32},{128,192},{160,224},{192,128},{224,1... | collective-permute-start | bytes 393224 | tf_op jit(solution)/shard_map/ppermute | solution.py:317
  124.8 8.2 %collective-permute-start.35 = (bf16[64,1024]{1,0:T(8,128)(2,1)S(1)}, bf16[64,1024]{1,0:T(8,128)(2,1)S(1)}, u32[]{:S(2)}, u32[]{:S(2)}) collective-permute-start(bf16[64,1024]{1,0:T(8,128)(2,1)S(1)} %shard_map.130.refs_0_), channel_id=1, source_target_pairs={{0,128},{32,160},{64,192},{96,224},{128,0},{160,32},{192,64},{224,... | collective-permute-start | bytes 393224 | tf_op jit(solution)/shard_map/ppermute | solution.py:317
  133.0 3.9 %collective-permute-start.36 = (bf16[64,1024]{1,0:T(8,128)(2,1)S(1)}, bf16[64,1024]{1,0:T(8,128)(2,1)S(1)}, u32[]{:S(2)}, u32[]{:S(2)}) collective-permute-start(bf16[64,1024]{1,0:T(8,128)(2,1)S(1)} %shard_map.132.refs_0_), channel_id=1, source_target_pairs={{0,64},{32,96},{64,0},{96,32},{128,192},{160,224},{192,128},{224,1... | collective-permute-start | bytes 393224 | tf_op jit(solution)/shard_map/ppermute | solution.py:317
  133.1 6.5 %collective-permute-start.38 = (bf16[64,1024]{1,0:T(8,128)(2,1)S(1)}, bf16[64,1024]{1,0:T(8,128)(2,1)S(1)}, u32[]{:S(2)}, u32[]{:S(2)}) collective-permute-start(bf16[64,1024]{1,0:T(8,128)(2,1)S(1)} %shard_map.132.refs_0_), channel_id=1, source_target_pairs={{0,32},{32,0},{64,96},{96,64},{128,160},{160,128},{192,224},{224,1... | collective-permute-start | bytes 393224 | tf_op jit(solution)/shard_map/ppermute | solution.py:317
  136.9 4.3 %collective-permute-start.37 = (bf16[64,1024]{1,0:T(8,128)(2,1)S(1)}, bf16[64,1024]{1,0:T(8,128)(2,1)S(1)}, u32[]{:S(2)}, u32[]{:S(2)}) collective-permute-start(bf16[64,1024]{1,0:T(8,128)(2,1)S(1)} %collective-permute-done.36.refs_0_), channel_id=1, source_target_pairs={{0,32},{32,0},{64,96},{96,64},{128,160},{160,128},{192,224},{224,1... | collective-permute-start | bytes 393224 | tf_op jit(solution)/shard_map/ppermute | solution.py:317
  (1 other events, 1.0 us)
